TPU v7x, 32 devices: a whole 2x2x4 slice. The times are simulated.
32 devices in a mesh: docs: 8 (over z, x), seq: 4 (over y, core).
Axes of the slice: x: 2, y: 2, z: 4, core: 2. Of those that a mesh axis runs over, the one named last changes fastest.
Arguments:
- tokens: bfloat16 [8, 1024, 1024], P('docs', 'seq'), may hold values from -6 to 6
- cotangent: bfloat16 [8, 1024, 1024], P('docs', 'seq'), may hold values from -6 to 6
- cache_keys: bfloat16 [8, 2048, 1024], P(None, ('docs', 'seq')), may hold values from -6 to 6
- cache_values: bfloat16 [8, 2048, 1024], P(None, ('docs', 'seq')), may hold values from -6 to 6
- neighbours: int32 [8, 1024, 64], P('docs', 'seq'), may hold values from 0 to 4095
- partner: int32 [8], replicated, may hold values from 0 to 7, as said below
- has_memory: int32 [8], replicated, may hold values from 0 to 1, as said below
- w_heads: float32 [1024, 3072], P(('docs', 'seq')), may hold values from -0.1875 to 0.1875
- moment_heads: float32 [1024, 3072], P(('docs', 'seq')), may hold values from -0.0004272461 to 0.0004272461
- square_heads: float32 [1024, 3072], P(('docs', 'seq')), may hold values from 8e-11 to 3.2e-10
- w_merge: float32 [1024, 1024], P(('docs', 'seq')), may hold values from -1.5 to 1.5
- moment_merge: float32 [1024, 1024], P(('docs', 'seq')), may hold values from -0.0004272461 to 0.0004272461
- square_merge: float32 [1024, 1024], P(('docs', 'seq')), may hold values from 4.671058e-12 to 1.8684231e-11
- w_gate: float32 [1024, 2816], P(('docs', 'seq')), may hold values from -0.1875 to 0.1875
- moment_gate: float32 [1024, 2816], P(('docs', 'seq')), may hold values from -0.0004272461 to 0.0004272461
- square_gate: float32 [1024, 2816], P(('docs', 'seq')), may hold values from 8e-11 to 3.2e-10
- w_up: float32 [1024, 2816], P(('docs', 'seq')), may hold values from -0.1875 to 0.1875
- moment_up: float32 [1024, 2816], P(('docs', 'seq')), may hold values from -0.0004272461 to 0.0004272461
- square_up: float32 [1024, 2816], P(('docs', 'seq')), may hold values from 8e-11 to 3.2e-10
- w_down: float32 [2816, 1024], P(('docs', 'seq')), may hold values from -0.109375 to 0.109375
- moment_down: float32 [2816, 1024], P(('docs', 'seq')), may hold values from -0.0004272461 to 0.0004272461
- square_down: float32 [2816, 1024], P(('docs', 'seq')), may hold values from 8e-11 to 3.2e-10
- gains: float32 [2, 1024], P(None, ('docs', 'seq')), may hold values from 0.25 to 3
- moment_gains: float32 [2, 1024], P(None, ('docs', 'seq')), may hold values from -0.0008544922 to 0.0008544922
- square_gains: float32 [2, 1024], P(None, ('docs', 'seq')), may hold values from 2e-10 to 8e-10
Outputs:
- activations: bfloat16 [8, 1024, 1024], P('docs', 'seq')
- input_grad: float32 [8, 1024, 1024], P('docs', 'seq')
- heads_moment: float32 [1024, 3072], P(('docs', 'seq'))
- heads_square: float32 [1024, 3072], P(('docs', 'seq'))
- heads_weight: float32 [1024, 3072], P(('docs', 'seq'))
- merge_moment: float32 [1024, 1024], P(('docs', 'seq'))
- merge_square: float32 [1024, 1024], P(('docs', 'seq'))
- merge_weight: float32 [1024, 1024], P(('docs', 'seq'))
- gate_moment: float32 [1024, 2816], P(('docs', 'seq'))
- gate_square: float32 [1024, 2816], P(('docs', 'seq'))
- gate_weight: float32 [1024, 2816], P(('docs', 'seq'))
- up_moment: float32 [1024, 2816], P(('docs', 'seq'))
- up_square: float32 [1024, 2816], P(('docs', 'seq'))
- up_weight: float32 [1024, 2816], P(('docs', 'seq'))
- down_moment: float32 [2816, 1024], P(('docs', 'seq'))
- down_square: float32 [2816, 1024], P(('docs', 'seq'))
- down_weight: float32 [2816, 1024], P(('docs', 'seq'))
- gains_moment: float32 [2, 1024], P(None, ('docs', 'seq'))
- gains_square: float32 [2, 1024], P(None, ('docs', 'seq'))
- gains_weight: float32 [2, 1024], P(None, ('docs', 'seq'))
- clip_norm: float32 [], replicated
- layer_norms: float32 [2, 6], replicated
Inputs may be any that keep to these rules, and one draw needn't show every extreme that they name: Exactly half of the documents have memory; a document with memory has as partner another document with memory and partners are mutual; a document without memory is its own partner. `has_memory`: exactly half of the 8 documents have memory. `neighbours`: indices below 2048 name keys of the document's own cache, the others keys of its partner's cache; they are read only for documents with memory.
All inputs are finite; a program needn't handle non-finite values.
Results may differ from a plain program's by a relative error of at most 0.015.
Values may be sent and summed in bfloat16 or wider, within the bound.
No kernel may reach another device: no remote copies, remote signals or barrier semaphores. Data moves between devices by JAX's collectives and lax.ppermute only.
A program may use at most 256 MiB of HBM per device.

v0:
```python
import jax
import jax.numpy as jnp
from jax import lax
from jax.sharding import PartitionSpec as P

HEADS = 8
HEAD_DIM = 128
MEM = 2048
STEP = 10


NORM_EPS = 1e-06
BETA_ONE = 0.9
BETA_TWO = 0.999
ADAM_EPS = 1e-06
DECAY = 0.01
RATE = 0.5
CLIP = 1.0


def norm_rows(values):
    row_scale = lax.rsqrt(jnp.mean(values * values, axis=-1, keepdims=True) + NORM_EPS)
    return (values * row_scale, row_scale)


def norm_back(grad_normed, unit_rows, row_scale, gain_row):
    weighted = grad_normed * gain_row
    inner = jnp.mean(weighted * unit_rows, axis=-1, keepdims=True)
    return (row_scale * (weighted - unit_rows * inner), jnp.sum(grad_normed * unit_rows, axis=0))


def angles(positions, half_size):
    frequency = jnp.exp(-jnp.log(10000.0) * jnp.arange(half_size, dtype=jnp.float32) / half_size)
    angle_grid = positions.astype(jnp.float32)[:, None] * frequency[None, :]
    return (jnp.cos(angle_grid)[:, None, :], jnp.sin(angle_grid)[:, None, :])


def rotate(values, cosine_table, sine_table):
    half_size = values.shape[-1] // 2
    first_half = values[..., :half_size]
    second_half = values[..., half_size:]
    return jnp.concatenate(
        [
            first_half * cosine_table - second_half * sine_table,
            second_half * cosine_table + first_half * sine_table,
        ],
        axis=-1,
    )


def rotate_back(values, cosine_table, sine_table):
    half_size = values.shape[-1] // 2
    first_half = values[..., :half_size]
    second_half = values[..., half_size:]
    return jnp.concatenate(
        [
            first_half * cosine_table + second_half * sine_table,
            second_half * cosine_table - first_half * sine_table,
        ],
        axis=-1,
    )


def shards(
    tokens,
    cotangent,
    cache_keys,
    cache_values,
    neighbours,
    partner,
    has_memory,
    w_heads,
    moment_heads,
    square_heads,
    w_merge,
    moment_merge,
    square_merge,
    w_gate,
    moment_gate,
    square_gate,
    w_up,
    moment_up,
    square_up,
    w_down,
    moment_down,
    square_down,
    gains,
    moment_gains,
    square_gains,
):
    docs_here, row_count, feature_width = tokens.shape
    seq_count = lax.axis_size("seq")
    seq_index = lax.axis_index("seq")
    doc_index = lax.axis_index("docs")
    length = row_count * seq_count
    token_count = docs_here * row_count
    score_scale = HEAD_DIM ** (-0.5)
    masters = (w_heads, w_merge, w_gate, w_up, w_down, gains)
    moments = (moment_heads, moment_merge, moment_gate, moment_up, moment_down, moment_gains)
    squares = (square_heads, square_merge, square_gate, square_up, square_down, square_gains)
    decays = (DECAY, DECAY, DECAY, DECAY, DECAY, 0.0)
    weight_local = jnp.stack([jnp.sum(member * member) for member in masters])
    low_masters = [member.astype(jnp.bfloat16) for member in masters]
    gathered = (
        lax.all_gather(low_masters[0], ("docs", "seq"), axis=0, tiled=True),
        lax.all_gather(low_masters[1], ("docs", "seq"), axis=0, tiled=True),
        lax.all_gather(low_masters[2], ("docs", "seq"), axis=0, tiled=True),
        lax.all_gather(low_masters[3], ("docs", "seq"), axis=0, tiled=True),
        lax.all_gather(low_masters[4], ("docs", "seq"), axis=0, tiled=True),
        lax.all_gather(low_masters[5], ("docs", "seq"), axis=1, tiled=True),
    )
    heads_full, merge_full, gate_full, up_full, down_full, gains_full = gathered
    gain_one = gains_full[0].astype(jnp.float32)
    gain_two = gains_full[1].astype(jnp.float32)
    inputs = tokens.astype(jnp.float32).reshape(token_count, feature_width)
    unit_one, scale_one = norm_rows(inputs)
    normed_one = (unit_one * gain_one).astype(jnp.bfloat16)
    projected = jnp.dot(normed_one, heads_full, preferred_element_type=jnp.float32)
    head_shape = (docs_here, row_count, HEADS, HEAD_DIM)
    query_raw = projected[:, :feature_width].reshape(head_shape)
    key_raw = projected[:, feature_width : 2 * feature_width].reshape(head_shape)
    value_raw = projected[:, 2 * feature_width :].reshape(head_shape)
    positions = seq_index * row_count + jnp.arange(row_count, dtype=jnp.int32)
    cosine_table, sine_table = angles(positions, HEAD_DIM // 2)
    query_local = rotate(query_raw, cosine_table, sine_table).astype(jnp.bfloat16)
    query_memory = query_raw.astype(jnp.bfloat16)
    key_local = (
        rotate(key_raw, cosine_table, sine_table)
        .astype(jnp.bfloat16)
        .reshape(docs_here, row_count, feature_width)
    )
    value_local = value_raw.astype(jnp.bfloat16).reshape(docs_here, row_count, feature_width)
    key_grid, value_grid = (
        lax.all_gather(key_local, "seq", axis=1, tiled=True),
        lax.all_gather(value_local, "seq", axis=1, tiled=True),
    )
    key_grid = key_grid.reshape(docs_here, length, HEADS, HEAD_DIM)
    value_grid = value_grid.reshape(docs_here, length, HEADS, HEAD_DIM)
    own_rows = jnp.concatenate([cache_keys, cache_values], axis=2)
    mate_rows = jnp.take(own_rows, partner, axis=0)
    outgoing = jnp.concatenate([own_rows, mate_rows], axis=2)
    arrived = lax.all_to_all(outgoing, "docs", split_axis=0, concat_axis=1, tiled=True)
    memory = lax.all_gather(arrived, "seq", axis=1, tiled=True)
    slab_rows = arrived.shape[1]
    per_device = cache_keys.shape[1]
    gathered_index = jnp.arange(MEM, dtype=jnp.int32)
    seq_anchor = gathered_index // slab_rows
    remainder = gathered_index % slab_rows
    anchor = (
        remainder // per_device * seq_count + seq_anchor
    ) * per_device + remainder % per_device
    my_docs = doc_index * docs_here + jnp.arange(docs_here, dtype=jnp.int32)
    memory_flag = jnp.take(has_memory, my_docs) > 0
    any_memory = jnp.any(memory_flag)
    block_rows = min(512, MEM)
    block_ids = jnp.arange(MEM // block_rows, dtype=jnp.int32)

    def memory_block(block_index):
        block_start = block_index * block_rows
        rows_here = lax.dynamic_slice_in_dim(memory, block_start, block_rows, 1)
        anchor_here = lax.dynamic_slice_in_dim(anchor, block_start, block_rows, 0)
        pair_shape = (docs_here, 2 * block_rows, HEADS, HEAD_DIM)
        keys_pair = jnp.concatenate(
            [rows_here[..., :feature_width], rows_here[..., 2 * feature_width : 3 * feature_width]],
            axis=1,
        ).reshape(pair_shape)
        values_pair = jnp.concatenate(
            [
                rows_here[..., feature_width : 2 * feature_width],
                rows_here[..., 3 * feature_width :],
            ],
            axis=1,
        ).reshape(pair_shape)
        targets = jnp.concatenate([anchor_here, anchor_here + MEM])
        chosen = jnp.any(neighbours[:, :, :, None] == targets[None, None, None, :], axis=2)
        chosen = chosen & memory_flag[:, None, None]
        scores = (
            jnp.einsum(
                "dqhe,dkhe->dhqk", query_memory, keys_pair, preferred_element_type=jnp.float32
            )
            * score_scale
        )
        scores = jnp.where(chosen[:, None], scores, -jnp.inf)
        return (scores, keys_pair, values_pair)

    causal = positions[:, None] >= jnp.arange(length, dtype=jnp.int32)[None, :]
    local_scores = (
        jnp.einsum("dqhe,dkhe->dhqk", query_local, key_grid, preferred_element_type=jnp.float32)
        * score_scale
    )
    local_scores = jnp.where(causal[None, None], local_scores, -jnp.inf)
    running_max = jnp.max(local_scores, axis=-1)
    running_sum = jnp.sum(jnp.exp(local_scores - running_max[..., None]), axis=-1)

    def stat_step(state_pair, block_index):
        old_max, old_sum = state_pair
        scores, keys_pair, values_pair = memory_block(block_index)
        new_max = jnp.maximum(old_max, jnp.max(scores, axis=-1))
        new_sum = old_sum * jnp.exp(old_max - new_max) + jnp.sum(
            jnp.exp(scores - new_max[..., None]), axis=-1
        )
        return ((new_max, new_sum), None)

    def memory_stats(state_pair):
        return lax.scan(stat_step, state_pair, block_ids)[0]

    running_max, running_sum = lax.cond(
        any_memory, memory_stats, lambda state_pair: state_pair, (running_max, running_sum)
    )
    log_total = running_max + jnp.log(running_sum)
    prob_local = jnp.exp(local_scores - log_total[..., None])
    prob_local_low = prob_local.astype(jnp.bfloat16)
    attended = jnp.einsum(
        "dhqk,dkhe->dqhe", prob_local_low, value_grid, preferred_element_type=jnp.float32
    )

    def value_step(accumulated, block_index):
        scores, keys_pair, values_pair = memory_block(block_index)
        prob_low = jnp.exp(scores - log_total[..., None]).astype(jnp.bfloat16)
        return (
            accumulated
            + jnp.einsum(
                "dhqk,dkhe->dqhe", prob_low, values_pair, preferred_element_type=jnp.float32
            ),
            None,
        )

    def memory_values(accumulated):
        return lax.scan(value_step, accumulated, block_ids)[0]

    attended = lax.cond(any_memory, memory_values, lambda accumulated: accumulated, attended)
    blended = attended.reshape(token_count, feature_width).astype(jnp.bfloat16)
    middle = inputs + jnp.dot(blended, merge_full, preferred_element_type=jnp.float32)
    unit_two, scale_two = norm_rows(middle)
    normed_two = (unit_two * gain_two).astype(jnp.bfloat16)
    gate_raw = jnp.dot(normed_two, gate_full, preferred_element_type=jnp.float32)
    up_raw = jnp.dot(normed_two, up_full, preferred_element_type=jnp.float32)
    sigmoid_gate = jax.nn.sigmoid(gate_raw)
    silu_gate = gate_raw * sigmoid_gate
    active = (silu_gate * up_raw).astype(jnp.bfloat16)
    result = middle + jnp.dot(active, down_full, preferred_element_type=jnp.float32)
    activations = result.astype(jnp.bfloat16).reshape(docs_here, row_count, feature_width)
    weights_back = (
        lax.all_gather(low_masters[0], ("docs", "seq"), axis=0, tiled=True),
        lax.all_gather(low_masters[1], ("docs", "seq"), axis=0, tiled=True),
        lax.all_gather(low_masters[2], ("docs", "seq"), axis=0, tiled=True),
        lax.all_gather(low_masters[3], ("docs", "seq"), axis=0, tiled=True),
        lax.all_gather(low_masters[4], ("docs", "seq"), axis=0, tiled=True),
        lax.all_gather(low_masters[5], ("docs", "seq"), axis=1, tiled=True),
    )
    heads_back, merge_back, gate_back, up_back, down_back = (
        weights_back[0],
        weights_back[1],
        weights_back[2],
        weights_back[3],
        weights_back[4],
    )
    grad_ffn = cotangent.reshape(token_count, feature_width)
    grad_out = grad_ffn.astype(jnp.float32)
    g_down = jnp.einsum("rf,rd->fd", active, grad_ffn, preferred_element_type=jnp.float32)
    grad_active = jnp.einsum("rd,fd->rf", grad_ffn, down_back, preferred_element_type=jnp.float32)
    grad_gate = (
        grad_active * up_raw * sigmoid_gate * (1.0 + gate_raw * (1.0 - sigmoid_gate))
    ).astype(jnp.bfloat16)
    grad_up = (grad_active * silu_gate).astype(jnp.bfloat16)
    g_gate = jnp.einsum("rd,rf->df", normed_two, grad_gate, preferred_element_type=jnp.float32)
    g_up = jnp.einsum("rd,rf->df", normed_two, grad_up, preferred_element_type=jnp.float32)
    grad_normed_two = jnp.einsum(
        "rf,df->rd", grad_gate, gate_back, preferred_element_type=jnp.float32
    ) + jnp.einsum("rf,df->rd", grad_up, up_back, preferred_element_type=jnp.float32)
    grad_norm_two, grad_gain_two = norm_back(grad_normed_two, unit_two, scale_two, gain_two)
    grad_middle = grad_out + grad_norm_two
    grad_branch = grad_middle.astype(jnp.bfloat16)
    g_merge = jnp.einsum("rd,re->de", blended, grad_branch, preferred_element_type=jnp.float32)
    grad_attended = jnp.einsum(
        "re,de->rd", grad_branch, merge_back, preferred_element_type=jnp.float32
    )
    grad_attended = grad_attended.astype(jnp.bfloat16).reshape(head_shape)
    grad_prob_local = jnp.einsum(
        "dqhe,dkhe->dhqk", grad_attended, value_grid, preferred_element_type=jnp.float32
    )
    row_delta = jnp.sum(prob_local * grad_prob_local, axis=-1)

    def delta_step(accumulated, block_index):
        scores, keys_pair, values_pair = memory_block(block_index)
        prob_full = jnp.exp(scores - log_total[..., None])
        grad_prob = jnp.einsum(
            "dqhe,dkhe->dhqk", grad_attended, values_pair, preferred_element_type=jnp.float32
        )
        return (accumulated + jnp.sum(prob_full * grad_prob, axis=-1), None)

    def memory_delta(accumulated):
        return lax.scan(delta_step, accumulated, block_ids)[0]

    row_delta = lax.cond(any_memory, memory_delta, lambda accumulated: accumulated, row_delta)
    grad_scores_local = (prob_local * (grad_prob_local - row_delta[..., None])).astype(jnp.bfloat16)
    grad_query_local = (
        jnp.einsum(
            "dhqk,dkhe->dqhe", grad_scores_local, key_grid, preferred_element_type=jnp.float32
        )
        * score_scale
    )
    grad_key_grid = (
        jnp.einsum(
            "dhqk,dqhe->dkhe", grad_scores_local, query_local, preferred_element_type=jnp.float32
        )
        * score_scale
    )
    grad_value_grid = jnp.einsum(
        "dhqk,dqhe->dkhe", prob_local_low, grad_attended, preferred_element_type=jnp.float32
    )
    key_share, value_share = (
        lax.psum_scatter(
            grad_key_grid.reshape(docs_here, length, feature_width).astype(jnp.bfloat16),
            "seq",
            scatter_dimension=1,
            tiled=True,
        ).astype(jnp.float32),
        lax.psum_scatter(
            grad_value_grid.reshape(docs_here, length, feature_width).astype(jnp.bfloat16),
            "seq",
            scatter_dimension=1,
            tiled=True,
        ).astype(jnp.float32),
    )

    def query_step(accumulated, block_index):
        scores, keys_pair, values_pair = memory_block(block_index)
        prob_full = jnp.exp(scores - log_total[..., None])
        grad_prob = jnp.einsum(
            "dqhe,dkhe->dhqk", grad_attended, values_pair, preferred_element_type=jnp.float32
        )
        grad_scores = (prob_full * (grad_prob - row_delta[..., None])).astype(jnp.bfloat16)
        return (
            accumulated
            + jnp.einsum(
                "dhqk,dkhe->dqhe", grad_scores, keys_pair, preferred_element_type=jnp.float32
            )
            * score_scale,
            None,
        )

    def memory_query(accumulated):
        return lax.scan(query_step, accumulated, block_ids)[0]

    grad_query_memory = lax.cond(
        any_memory,
        memory_query,
        lambda accumulated: accumulated,
        jnp.zeros(head_shape, jnp.float32),
    )
    grad_query = rotate_back(grad_query_local, cosine_table, sine_table) + grad_query_memory
    grad_key = rotate_back(key_share.reshape(head_shape), cosine_table, sine_table)
    grad_projected = jnp.concatenate(
        [
            grad_query.reshape(token_count, feature_width),
            grad_key.reshape(token_count, feature_width),
            value_share.reshape(token_count, feature_width),
        ],
        axis=1,
    ).astype(jnp.bfloat16)
    g_heads = jnp.einsum(
        "rd,rc->dc", normed_one, grad_projected, preferred_element_type=jnp.float32
    )
    grad_normed_one = jnp.einsum(
        "rc,dc->rd", grad_projected, heads_back, preferred_element_type=jnp.float32
    )
    grad_norm_one, grad_gain_one = norm_back(grad_normed_one, unit_one, scale_one, gain_one)
    input_grad = (grad_middle + grad_norm_one).reshape(docs_here, row_count, feature_width)
    g_gains = jnp.stack([grad_gain_one, grad_gain_two])
    reduced = (
        lax.psum_scatter(g_heads, ("docs", "seq"), scatter_dimension=0, tiled=True),
        lax.psum_scatter(g_merge, ("docs", "seq"), scatter_dimension=0, tiled=True),
        lax.psum_scatter(g_gate, ("docs", "seq"), scatter_dimension=0, tiled=True),
        lax.psum_scatter(g_up, ("docs", "seq"), scatter_dimension=0, tiled=True),
        lax.psum_scatter(g_down, ("docs", "seq"), scatter_dimension=0, tiled=True),
        lax.psum_scatter(g_gains, ("docs", "seq"), scatter_dimension=1, tiled=True),
    )
    grad_local = jnp.stack([jnp.sum(member * member) for member in reduced])
    grad_total, weight_total = lax.psum((grad_local, weight_local), ("docs", "seq"))
    grad_norm = jnp.sqrt(jnp.sum(grad_total))
    factor = CLIP / jnp.maximum(grad_norm, CLIP)
    fix_one = 1.0 - BETA_ONE**STEP
    fix_two = 1.0 - BETA_TWO**STEP
    new_moments = []
    new_squares = []
    directions = []
    for master, moment, square, gradient, decay_rate in zip(
        masters, moments, squares, reduced, decays
    ):
        clipped = factor * gradient
        moment_new = BETA_ONE * moment + (1.0 - BETA_ONE) * clipped
        square_new = BETA_TWO * square + (1.0 - BETA_TWO) * clipped * clipped
        direction = (
            moment_new / fix_one / (jnp.sqrt(square_new / fix_two) + ADAM_EPS) + decay_rate * master
        )
        new_moments.append(moment_new)
        new_squares.append(square_new)
        directions.append(direction)
    update_local = jnp.stack([jnp.sum(member * member) for member in directions])
    update_total = lax.psum(update_local, ("docs", "seq"))
    weight_norm = jnp.sqrt(weight_total)
    update_norm = jnp.sqrt(update_total)
    trust = weight_norm / update_norm
    new_weights = [
        master - RATE * trust[place] * directions[place] for place, master in enumerate(masters)
    ]
    layer_norms = jnp.stack([weight_norm, update_norm])
    return (
        activations,
        input_grad,
        new_moments[0],
        new_squares[0],
        new_weights[0],
        new_moments[1],
        new_squares[1],
        new_weights[1],
        new_moments[2],
        new_squares[2],
        new_weights[2],
        new_moments[3],
        new_squares[3],
        new_weights[3],
        new_moments[4],
        new_squares[4],
        new_weights[4],
        new_moments[5],
        new_squares[5],
        new_weights[5],
        grad_norm,
        layer_norms,
    )


def solution(mesh):
    placed = (
        P("docs", "seq", None),
        P("docs", "seq", None),
        P(None, ("docs", "seq"), None),
        P(None, ("docs", "seq"), None),
        P("docs", "seq", None),
        P(),
        P(),
        P(("docs", "seq"), None),
        P(("docs", "seq"), None),
        P(("docs", "seq"), None),
        P(("docs", "seq"), None),
        P(("docs", "seq"), None),
        P(("docs", "seq"), None),
        P(("docs", "seq"), None),
        P(("docs", "seq"), None),
        P(("docs", "seq"), None),
        P(("docs", "seq"), None),
        P(("docs", "seq"), None),
        P(("docs", "seq"), None),
        P(("docs", "seq"), None),
        P(("docs", "seq"), None),
        P(("docs", "seq"), None),
        P(None, ("docs", "seq")),
        P(None, ("docs", "seq")),
        P(None, ("docs", "seq")),
    )
    return jax.shard_map(
        shards,
        mesh=mesh,
        in_specs=placed,
        out_specs=(
            P("docs", "seq", None),
            P("docs", "seq", None),
            P(("docs", "seq"), None),
            P(("docs", "seq"), None),
            P(("docs", "seq"), None),
            P(("docs", "seq"), None),
            P(("docs", "seq"), None),
            P(("docs", "seq"), None),
            P(("docs", "seq"), None),
            P(("docs", "seq"), None),
            P(("docs", "seq"), None),
            P(("docs", "seq"), None),
            P(("docs", "seq"), None),
            P(("docs", "seq"), None),
            P(("docs", "seq"), None),
            P(("docs", "seq"), None),
            P(("docs", "seq"), None),
            P(None, ("docs", "seq")),
            P(None, ("docs", "seq")),
            P(None, ("docs", "seq")),
            P(),
            P(),
        ),
        check_vma=False,
    )
```

profile of v0, /device:TPU:0, one launch (start us, length us, event | category | flops | bytes accessed | tf_op | source)
XLA Modules:
  0.0 2010.2 jit_solution(1087877597257523331)
XLA Ops:
  18.5 7.4 all-to-all-start
  26.6 113.9 %all-gather.1 = bf16[32,32,2]{1,2,0:T(2,128)(2,1)S(1)} all-gather(bf16[1,32,2]{1,2,0:T(2,128)(2,1)S(1)} %get-tuple-element.744), channel_id=1, replica_groups=mesh['docs'=8,'seq'=4] {'docs','seq'}, dimensions={0}, use_global_device_ids=true | all-gather | bytes 4224 | tf_op jit(solution)/shard_map/all_gather | solution.py:110
  141.9 8.0 all-gather.11.cloned.1.call-done
  170.3 35.0 %all-gather.13.cloned.1.call-done = bf16[1,1024,1024]{1,2,0:T(8,128)(2,1)} async-done(((bf16[1,256,1024]{1,2,0:T(8,128)(2,1)}), bf16[1,1024,1024]{1,2,0:T(8,128)(2,1)}) %all-gather.13.cloned.1.call-update) | async-done | bytes 2097168 | tf_op jit(solution)/shard_map/all_gather | solution.py:134
  212.2 100.7 %all-gather.15.cloned.1.call-done = bf16[1,2048,4096]{2,1,0:T(8,128)(2,1)} async-done(((bf16[1,512,4096]{2,1,0:T(8,128)(2,1)}), bf16[1,2048,4096]{2,1,0:T(8,128)(2,1)}) %all-gather.15.cloned.1.call-update) | async-done | bytes 16777232 | tf_op jit(solution)/shard_map/all_gather | solution.py:143
  314.1 23.3 %all-gather.25.cloned.1.call-done = bf16[1024,1024]{1,0:T(8,128)(2,1)} async-done(((bf16[256,1024]{1,0:T(8,128)(2,1)}), bf16[1024,1024]{1,0:T(8,128)(2,1)}) %all-gather.25.cloned.1.call-update) | async-done | bytes 2097168 | tf_op jit(solution)/shard_map/all_gather | solution.py:135
  343.6 53.6 %all-gather.17.cloned.1.call-done = bf16[1024,1024]{1,0:T(8,128)(2,1)} async-done(((bf16[32,1024]{1,0:T(8,128)(2,1)}), bf16[1024,1024]{1,0:T(8,128)(2,1)}) %all-gather.17.cloned.1.call-update) | async-done | bytes 2097168 | tf_op jit(solution)/shard_map/all_gather | solution.py:106
  399.8 66.8 %all-gather.19.cloned.1.call-done = bf16[1024,2816]{1,0:T(8,128)(2,1)} async-done(((bf16[32,2816]{1,0:T(8,128)(2,1)}), bf16[1024,2816]{1,0:T(8,128)(2,1)}) %all-gather.19.cloned.1.call-update) | async-done | bytes 5767184 | tf_op jit(solution)/shard_map/all_gather | solution.py:107
  472.5 63.9 %all-gather.21.cloned.1.call-done = bf16[1024,2816]{1,0:T(8,128)(2,1)} async-done(((bf16[32,2816]{1,0:T(8,128)(2,1)}), bf16[1024,2816]{1,0:T(8,128)(2,1)}) %all-gather.21.cloned.1.call-update) | async-done | bytes 5767184 | tf_op jit(solution)/shard_map/all_gather | solution.py:108
  542.3 63.9 %all-gather.23.cloned.1.call-done = bf16[2816,1024]{1,0:T(8,128)(2,1)} async-done(((bf16[88,1024]{1,0:T(8,128)(2,1)}), bf16[2816,1024]{1,0:T(8,128)(2,1)}) %all-gather.23.cloned.1.call-update) | async-done | bytes 5767184 | tf_op jit(solution)/shard_map/all_gather | solution.py:109
  606.1 9.0 multiply_convert_fusion.2
  625.4 8.7 multiply_reduce_fusion
  653.6 9.6 conditional.7
  667.4 150.0 %reduce-scatter.11.cloned.1.call-done = bf16[1,256,1024]{1,2,0:T(8,128)(2,1)} async-done(((bf16[1,1024,1024]{1,2,0:T(8,128)(2,1)}), bf16[1,256,1024]{1,2,0:T(8,128)(2,1)}) %reduce-scatter.11.cloned.1.call-update) | async-done | bytes 524304 | tf_op jit(solution)/shard_map/reduce_scatter | solution.py:313
  825.5 25.8 %reduce-scatter.13.cloned.1.call-done = bf16[1,256,1024]{1,2,0:T(8,128)(2,1)} async-done(((bf16[1,1024,1024]{1,2,0:T(8,128)(2,1)}), bf16[1,256,1024]{1,2,0:T(8,128)(2,1)}) %reduce-scatter.13.cloned.1.call-update) | async-done | bytes 524304 | tf_op jit(solution)/shard_map/reduce_scatter | solution.py:319
  885.4 7.3 fusion.85
  899.6 216.0 %reduce-scatter.25.cloned.1.call-done = f32[32,2]{1,0:T(8,128)} async-done(((f32[1024,2]{1,0:T(8,128)}), f32[32,2]{1,0:T(8,128)}) %reduce-scatter.25.cloned.1.call-update) | async-done | bytes 272
  1117.0 137.7 %reduce-scatter.17.cloned.1.call-done = f32[32,1024]{1,0:T(8,128)} async-done(((f32[1024,1024]{1,0:T(8,128)}), f32[32,1024]{1,0:T(8,128)}) %reduce-scatter.17.cloned.1.call-update) | async-done | bytes 131088 | tf_op jit(solution)/shard_map/reduce_scatter | solution.py:373
  1256.3 156.8 %reduce-scatter.15.cloned.1.call-done = f32[32,3072]{1,0:T(8,128)} async-done(((f32[1024,3072]{1,0:T(8,128)}), f32[32,3072]{1,0:T(8,128)}) %reduce-scatter.15.cloned.1.call-update) | async-done | bytes 393232 | tf_op jit(solution)/shard_map/reduce_scatter | solution.py:372
  1414.8 154.5 %reduce-scatter.19.cloned.1.call-done = f32[32,2816]{1,0:T(8,128)} async-done(((f32[1024,2816]{1,0:T(8,128)}), f32[32,2816]{1,0:T(8,128)}) %reduce-scatter.19.cloned.1.call-update) | async-done | bytes 360464 | tf_op jit(solution)/shard_map/reduce_scatter | solution.py:374
  1571.0 153.1 %reduce-scatter.21.cloned.1.call-done = f32[32,2816]{1,0:T(8,128)} async-done(((f32[1024,2816]{1,0:T(8,128)}), f32[32,2816]{1,0:T(8,128)}) %reduce-scatter.21.cloned.1.call-update) | async-done | bytes 360464 | tf_op jit(solution)/shard_map/reduce_scatter | solution.py:375
  1725.7 153.5 %reduce-scatter.23.cloned.1.call-done = f32[88,1024]{1,0:T(8,128)} async-done(((f32[2816,1024]{1,0:T(8,128)}), f32[88,1024]{1,0:T(8,128)}) %reduce-scatter.23.cloned.1.call-update) | async-done | bytes 360464 | tf_op jit(solution)/shard_map/reduce_scatter | solution.py:376
  1884.9 36.8 %psum.21 = f32[6]{0:T(128)S(1)} all-reduce(f32[6]{0:T(128)S(1)} %stack.90), channel_id=1, replica_groups=mesh['docs'=8,'seq'=4] {'docs','seq'}, use_global_device_ids=true, to_apply=%region_46.47 | all-reduce | flops 6 | bytes 48 | tf_op jit(solution)/shard_map/psum | solution.py:380
  1946.7 40.9 %all-reduce = (f32[6]{0:T(128)S(1)}, f32[6]{0:T(128)S(1)}) all-reduce(f32[6]{0:T(128)S(1)} %stack.104, f32[6]{0:T(128)S(1)} %stack.97), channel_id=1, replica_groups=mesh['docs'=8,'seq'=4] {'docs','seq'}, use_global_device_ids=true, to_apply=%region_61.62 | all-reduce | flops 12 | bytes 96 | tf_op jit(solution)/shard_map/psum | solution.py:401
  (271 shorter events, 193.3 us)
Async XLA Ops:
  7.2 142.8 %all-gather.11.cloned.1.call-start = ((), (), s32[]{:S(2)}) async-start(), calls=%async_computation.9 | async-start | bytes 6488064 | tf_op jit(solution)/shard_map/all_gather | solution.py:105
  18.5 142.5 %all-to-all-start = ((bf16[8,64,4096]{2,1,0:T(8,128)(2,1)}), bf16[8,64,4096]{2,1,0:T(8,128)(2,1)}, u32[]{:S(2)}, u32[]{:S(2)}) async-start(bf16[8,64,4096]{2,1,0:T(8,128)(2,1)} %pad_maximum_fusion.7), calls=%async_computation | async-start | bytes 8388608 | tf_op jit(solution)/shard_map/all_to_all | solution.py:142
  25.9 179.4 %all-gather.13.cloned.1.call-start = ((), (), s32[]{:S(2)}) async-start(), calls=%async_computation.10 | async-start | bytes 2621440 | tf_op jit(solution)/shard_map/all_gather | solution.py:134
  161.0 151.9 %all-gather.15.cloned.1.call-start = ((), (), s32[]{:S(2)}) async-start(), calls=%async_computation.11 | async-start | bytes 20971520 | tf_op jit(solution)/shard_map/all_gather | solution.py:143
  161.7 175.7 %all-gather.25.cloned.1.call-start = ((), (), s32[]{:S(2)}) async-start(), calls=%async_computation.23 | async-start | bytes 2621440 | tf_op jit(solution)/shard_map/all_gather | solution.py:135
  163.9 233.3 %all-gather.17.cloned.1.call-start = ((), (), s32[]{:S(2)}) async-start(), calls=%async_computation.12 | async-start | bytes 2162688 | tf_op jit(solution)/shard_map/all_gather | solution.py:106
  164.6 302.1 %all-gather.19.cloned.1.call-start = ((), (), s32[]{:S(2)}) async-start(), calls=%async_computation.13 | async-start | bytes 5947392 | tf_op jit(solution)/shard_map/all_gather | solution.py:107
  165.4 371.0 %all-gather.21.cloned.1.call-start = ((), (), s32[]{:S(2)}) async-start(), calls=%async_computation.14 | async-start | bytes 5947392 | tf_op jit(solution)/shard_map/all_gather | solution.py:108
  167.1 439.0 %all-gather.23.cloned.1.call-start = ((), (), s32[]{:S(2)}) async-start(), calls=%async_computation.15 | async-start | bytes 5947392 | tf_op jit(solution)/shard_map/all_gather | solution.py:109
  167.9 649.5 %reduce-scatter.11.cloned.1.call-start = ((), (), s32[]{:S(2)}) async-start(), calls=%async_computation.16 | async-start | bytes 2621440 | tf_op jit(solution)/shard_map/reduce_scatter | solution.py:313
  646.4 205.0 %reduce-scatter.13.cloned.1.call-start = ((), (), s32[]{:S(2)}) async-start(), calls=%async_computation.17 | async-start | bytes 2621440 | tf_op jit(solution)/shard_map/reduce_scatter | solution.py:319
  653.5 462.1 %reduce-scatter.25.cloned.1.call-start = ((), (), s32[]{:S(2)}) async-start(), calls=%async_computation.24 | async-start | bytes 540672
  858.4 396.3 %reduce-scatter.17.cloned.1.call-start = ((), (), s32[]{:S(2)}) async-start(), calls=%async_computation.19 | async-start | bytes 4325376 | tf_op jit(solution)/shard_map/reduce_scatter | solution.py:373
  861.2 551.9 %reduce-scatter.15.cloned.1.call-start = ((), (), s32[]{:S(2)}) async-start(), calls=%async_computation.18 | async-start | bytes 12976128 | tf_op jit(solution)/shard_map/reduce_scatter | solution.py:372
  868.8 700.5 %reduce-scatter.19.cloned.1.call-start = ((), (), s32[]{:S(2)}) async-start(), calls=%async_computation.20 | async-start | bytes 11894784 | tf_op jit(solution)/shard_map/reduce_scatter | solution.py:374
  877.0 847.0 %reduce-scatter.21.cloned.1.call-start = ((), (), s32[]{:S(2)}) async-start(), calls=%async_computation.21 | async-start | bytes 11894784 | tf_op jit(solution)/shard_map/reduce_scatter | solution.py:375
  884.4 994.8 %reduce-scatter.23.cloned.1.call-start = ((), (), s32[]{:S(2)}) async-start(), calls=%async_computation.22 | async-start | bytes 11894784 | tf_op jit(solution)/shard_map/reduce_scatter | solution.py:376
  894.0 1029.1 %copy-start.64 = (f32[2,32]{1,0:T(2,128)S(1)}, f32[2,32]{1,0:T(2,128)}, u32[]{:S(2)}) copy-start(f32[2,32]{1,0:T(2,128)} %param.64) | copy-start | bytes 772
  894.0 1029.1 %copy-start.65 = (f32[2,32]{1,0:T(2,128)S(1)}, f32[2,32]{1,0:T(2,128)}, u32[]{:S(2)}) copy-start(f32[2,32]{1,0:T(2,128)} %param.65) | copy-start | bytes 772
  894.0 1030.4 %copy-start.24 = (f32[32,3072]{1,0:T(8,128)S(1)}, f32[32,3072]{1,0:T(8,128)}, u32[]{:S(2)}) copy-start(f32[32,3072]{1,0:T(8,128)} %param.48) | copy-start | bytes 1179652
  894.0 1033.4 %copy-start.42 = (f32[32,1024]{1,0:T(8,128)S(1)}, f32[32,1024]{1,0:T(8,128)}, u32[]{:S(2)}) copy-start(f32[32,1024]{1,0:T(8,128)} %param.51) | copy-start | bytes 393220
  899.6 1030.2 %copy-start.26 = (f32[88,1024]{1,0:T(8,128)S(1)}, f32[88,1024]{1,0:T(8,128)}, u32[]{:S(2)}) copy-start(f32[88,1024]{1,0:T(8,128)} %param.60) | copy-start | bytes 1081348
  899.6 1033.3 %copy-start.28 = (f32[32,2816]{1,0:T(8,128)S(1)}, f32[32,2816]{1,0:T(8,128)}, u32[]{:S(2)}) copy-start(f32[32,2816]{1,0:T(8,128)} %param.54) | copy-start | bytes 1081348
  899.6 1033.3 %copy-start.29 = (f32[32,2816]{1,0:T(8,128)S(1)}, f32[32,2816]{1,0:T(8,128)}, u32[]{:S(2)}) copy-start(f32[32,2816]{1,0:T(8,128)} %param.57) | copy-start | bytes 1081348
  (58 other events, 2741.9 us)
Sparse Core Ops, SparseCore 0:
  11.5 138.4 all-gather.10
  161.1 44.1 all-gather.12
  206.9 105.9 all-gather.14
  314.8 22.5 all-gather.24
  340.7 56.4 all-gather.16
  400.5 66.1 all-gather.18
  470.1 66.2 all-gather.20
  539.9 66.2 all-gather.22
  646.5 170.8 reduce-scatter.10
  819.9 31.3 reduce-scatter.12
  858.5 257.0 reduce-scatter.24
  1117.9 136.8 reduce-scatter.16
  1261.8 151.2 reduce-scatter.14
  1415.3 153.9 reduce-scatter.18
  1571.4 152.5 reduce-scatter.20
  1726.2 152.9 reduce-scatter.22
where the time goes:
time: 2020 us; the launch traced here: 2010 us
  waiting for transfers between devices  1560 us (77%)
  blocking collectives  192 us (10%)
  matrix products  111 us (5%)
  other arithmetic  66.7 us (3%)
  local copies, waits for them, and re-layouts  38.1 us (2%)
  between operations  21.7 us (1%)
    unnamed x17, waiting for transfers between devices  217 us
    reduce_scatter x1, waiting for transfers between devices, shards(): lax.psum_scatter(g_heads, ('docs', 'seq'), scatter_dimension=0, tiled=True)  157 us
    reduce_scatter x1, waiting for transfers between devices, shards(): lax.psum_scatter(g_gate, ('docs', 'seq'), scatter_dimension=0, tiled=True)  154 us
    reduce_scatter x1, waiting for transfers between devices, shards(): lax.psum_scatter(g_down, ('docs', 'seq'), scatter_dimension=0, tiled=True)  154 us
    reduce_scatter x1, waiting for transfers between devices, shards(): lax.psum_scatter(g_up, ('docs', 'seq'), scatter_dimension=0, tiled=True)  153 us
    reduce_scatter x1, waiting for transfers between devices, shards(): lax.psum_scatter(grad_key_grid.reshape(docs_here, length, feature_width)....  150 us
    reduce_scatter x1, waiting for transfers between devices, shards(): lax.psum_scatter(g_merge, ('docs', 'seq'), scatter_dimension=0, tiled=True)  138 us
    all_gather x1, blocking collectives, shards(): lax.all_gather(low_masters[5], ('docs', 'seq'), axis=1, tiled=True)  114 us
  transfers between devices with their start and end apart: 17, of which 16 were waited for; matrix products, arithmetic and copies ran while one was open for 6% of the time, Pallas kernels for 0%

commit v1 on v0

v1 whole, which is shorter than its diff:
```python
import functools
import math

import jax
import jax.numpy as jnp
from jax import lax
from jax.experimental import pallas as pl
from jax.experimental.pallas import tpu as pltpu
from jax.sharding import PartitionSpec as P

HEADS = 8
HEAD_DIM = 128
STEP = 10
NORM_EPS = 1e-06
BETA_ONE = 0.9
BETA_TWO = 0.999
ADAM_EPS = 1e-06
DECAY = 0.01
RATE = 0.5
CLIP = 1.0
LANES = 128
LOG2E = math.log2(math.e)
SCALE = HEAD_DIM ** (-0.5)
BF = jnp.bfloat16
F32 = jnp.float32
VMEM_LIMIT = 56 * 1024 * 1024


def seq_shape():
    count = lax.axis_size("seq")
    cores = 2 if count % 2 == 0 else 1
    return count // cores, cores


def docs_shape():
    count = lax.axis_size("docs")
    nx = 1 << ((count.bit_length() - 1) // 2)
    while count % nx:
        nx //= 2
    return count // nx, nx


def send_seq(x, dy, dc):
    ny, nc = seq_shape()
    pairs = [
        (y * nc + c, (y + dy) % ny * nc + (c + dc) % nc) for y in range(ny) for c in range(nc)
    ]
    return lax.ppermute(x, "seq", pairs)


def send_x(x, dx):
    nz, nx = docs_shape()
    pairs = [(z * nx + i, z * nx + (i + dx) % nx) for z in range(nz) for i in range(nx)]
    return lax.ppermute(x, "docs", pairs)


def send_z(x, step, senders):
    nz, nx = docs_shape()
    pairs = [(z * nx + i, (z + step) * nx + i) for z in senders for i in range(nx)]
    return lax.ppermute(x, "docs", pairs)


def put(buffer, block, place):
    starts = list(place) + [0] * (buffer.ndim - len(place))
    block = block.reshape((1,) * (buffer.ndim - block.ndim) + block.shape)
    return lax.dynamic_update_slice(buffer, block, starts)


def seq_gather(block):
    ny, nc = seq_shape()
    index = lax.axis_index("seq")
    y, c = index // nc, index % nc
    column = jnp.zeros((ny,) + block.shape, block.dtype)
    column = put(column, block, [y])
    for dy in range(1, ny):
        column = put(column, send_seq(block, dy, 0), [(y - dy) % ny])
    whole = jnp.zeros((ny, nc) + block.shape, block.dtype)
    whole = lax.dynamic_update_slice(whole, column[:, None], (0, c, 0, 0))
    for dc in range(1, nc):
        other = send_seq(column, 0, dc)
        whole = lax.dynamic_update_slice(whole, other[:, None], (0, (c - dc) % nc, 0, 0))
    return whole.reshape((ny * nc * block.shape[0],) + block.shape[1:])


def seq_reduce(partial):
    ny, nc = seq_shape()
    index = lax.axis_index("seq")
    y, c = index // nc, index % nc
    rows = partial.shape[0] // (ny * nc)
    blocks = partial.reshape(ny, nc, rows, partial.shape[1])
    column = lax.dynamic_index_in_dim(blocks, c, 1, False)
    for dc in range(1, nc):
        away = lax.dynamic_index_in_dim(blocks, (c + dc) % nc, 1, False).astype(BF)
        column = column + send_seq(away, 0, dc).astype(F32)
    total = lax.dynamic_index_in_dim(column, y, 0, False)
    for dy in range(1, ny):
        away = lax.dynamic_index_in_dim(column, (y + dy) % ny, 0, False).astype(BF)
        total = total + send_seq(away, dy, 0).astype(F32)
    return total


def seq_swap(blocks):
    ny, nc = seq_shape()
    index = lax.axis_index("seq")
    y, c = index // nc, index % nc
    out = jnp.zeros_like(blocks)
    out = put(out, lax.dynamic_index_in_dim(blocks, index, 0, False), [index])
    for dy in range(ny):
        for dc in range(nc):
            if dy == 0 and dc == 0:
                continue
            there = (y + dy) % ny * nc + (c + dc) % nc
            here = (y - dy) % ny * nc + (c - dc) % nc
            away = lax.dynamic_index_in_dim(blocks, there, 0, False)
            out = put(out, send_seq(away, dy, dc), [here])
    return out


def docs_gather(block):
    nz, nx = docs_shape()
    index = lax.axis_index("docs")
    z, x = index // nx, index % nx
    ups, downs = [block], [block]
    for step in range(1, nz):
        ups.append(send_z(ups[-1], 1, range(step - 1, nz - 1)))
        downs.append(send_z(downs[-1], -1, range(1, nz - step + 1)))
    column = jnp.zeros((nz,) + block.shape, block.dtype)
    column = put(column, block, [z])
    for step in range(1, nz):
        arrived = jnp.where(z >= step, ups[step], downs[nz - step])
        column = put(column, arrived, [(z - step) % nz])
    whole = jnp.zeros((nz, nx) + block.shape, block.dtype)
    whole = lax.dynamic_update_slice(whole, column[:, None], (0, x, 0, 0))
    for dx in range(1, nx):
        other = send_x(column, dx)
        whole = lax.dynamic_update_slice(whole, other[:, None], (0, (x - dx) % nx, 0, 0))
    return whole.reshape((nz * nx,) + block.shape)


def docs_reduce(blocks):
    nz, nx = docs_shape()
    index = lax.axis_index("docs")
    z, x = index // nx, index % nx
    grid = blocks.reshape((nz, nx) + blocks.shape[1:])
    column = lax.dynamic_index_in_dim(grid, x, 1, False).astype(F32)
    for dx in range(1, nx):
        away = lax.dynamic_index_in_dim(grid, (x + dx) % nx, 1, False).astype(BF)
        column = column + send_x(away, dx).astype(F32)
    total = lax.dynamic_index_in_dim(column, z, 0, False)
    for sign in (1, -1):
        carry = None
        for step in range(nz - 1, 0, -1):
            place = jnp.clip(z + sign * step, 0, nz - 1)
            value = lax.dynamic_index_in_dim(column, place, 0, False)
            if carry is not None:
                value = value + carry.astype(F32)
            senders = range(nz - step) if sign > 0 else range(step, nz)
            carry = send_z(value.astype(BF), sign, senders)
        if carry is not None:
            total = total + carry.astype(F32)
    return total


def sum_everywhere(values):
    for axis in ("seq", "docs"):
        count = lax.axis_size(axis)
        if count & (count - 1):
            values = lax.psum(values, axis)
            continue
        reach = 1
        while reach < count:
            values = values + lax.ppermute(values, axis, [(i, i ^ reach) for i in range(count)])
            reach *= 2
    return values


def dot(a, b):
    return lax.dot_general(a, b, (((1,), (0,)), ((), ())), preferred_element_type=F32)


def dot_nt(a, b):
    return lax.dot_general(a, b, (((1,), (1,)), ((), ())), preferred_element_type=F32)


def dot_tn(a, b):
    return lax.dot_general(a, b, (((0,), (0,)), ((), ())), preferred_element_type=F32)


def params():
    return pltpu.CompilerParams(vmem_limit_bytes=VMEM_LIMIT)


def rows_of(rows, cols):
    return pl.BlockSpec((rows, cols), lambda i: (i, 0))


def all_of(rows, cols):
    return pl.BlockSpec((rows, cols), lambda i: (0, 0))


def project_kernel(heads, x, gain, weight, cosine, sine, normed, ql, qm, kl, vl):
    values = x[...].astype(F32)
    scale = lax.rsqrt(jnp.mean(values * values, axis=-1, keepdims=True) + NORM_EPS)
    low = (values * scale * gain[...]).astype(BF)
    normed[...] = low
    out = dot(low, weight[...])
    width = heads * HEAD_DIM
    cos, sin = cosine[...], sine[...]
    for h in range(heads):
        part = slice(h * HEAD_DIM, (h + 1) * HEAD_DIM)
        q = out[:, h * HEAD_DIM : (h + 1) * HEAD_DIM]
        k = out[:, width + h * HEAD_DIM : width + (h + 1) * HEAD_DIM]
        qm[:, part] = q.astype(BF)
        ql[:, part] = (q * cos + pltpu.roll(q, HEAD_DIM // 2, 1) * sin).astype(BF)
        kl[:, part] = (k * cos + pltpu.roll(k, HEAD_DIM // 2, 1) * sin).astype(BF)
    vl[...] = out[:, 2 * width : 3 * width].astype(BF)


def project(x, gain, weight, cosine, sine, heads):
    length, width = x.shape
    span = min(256, length)
    cols = heads * HEAD_DIM
    low = jax.ShapeDtypeStruct((length, cols), BF)
    return pl.pallas_call(
        functools.partial(project_kernel, heads),
        grid=(length // span,),
        in_specs=[
            rows_of(span, width),
            all_of(1, width),
            all_of(width, 3 * cols),
            rows_of(span, HEAD_DIM),
            rows_of(span, HEAD_DIM),
        ],
        out_specs=[rows_of(span, width)] + [rows_of(span, cols)] * 4,
        out_shape=[jax.ShapeDtypeStruct((length, width), BF)] + [low] * 4,
        compiler_params=params(),
        name="project",
    )(x, gain, weight, cosine, sine)


def causal(span, length):
    row = pl.program_id(0) * span + lax.broadcasted_iota(jnp.int32, (span, length), 0)
    return lax.broadcasted_iota(jnp.int32, (span, length), 1) <= row


def allowed(words, chunk, chunk_keys):
    tiles = chunk_keys // LANES
    parts = []
    for tile in range(tiles):
        bit = chunk * tiles + tile
        mask = (1 << bit) if bit < 31 else -(1 << 31)
        parts.append((words & jnp.int32(mask)) != 0)
    return parts


def select_tiles(parts, values, other):
    cut = [
        jnp.where(part, values[:, t * LANES : (t + 1) * LANES], other)
        for t, part in enumerate(parts)
    ]
    return jnp.concatenate(cut, axis=1)


def attend_kernel(heads, chunk_keys, flag, ql, qm, kl, vl, words, kv, out, low, lse, high, total):
    span = ql.shape[0]
    length = kl.shape[0]
    width = heads * HEAD_DIM
    factor = SCALE * LOG2E
    seen = causal(span, length)
    for h in range(heads):
        part = slice(h * HEAD_DIM, (h + 1) * HEAD_DIM)
        scores = dot_nt(ql[:, part], kl[:, part]) * factor
        scores = jnp.where(seen, scores, -jnp.inf)
        top = jnp.max(scores, axis=1, keepdims=True)
        expo = jnp.exp2(scores - top)
        high[:, h : h + 1] = top
        total[:, h : h + 1] = jnp.sum(expo, axis=1, keepdims=True)
        out[:, part] = dot(expo.astype(BF), vl[:, part])

    @pl.when(flag[0] > 0)
    def _():
        bits = words[...]
        count = kv.shape[0] // chunk_keys
        state = [
            (high[:, h : h + 1], total[:, h : h + 1], out[:, h * HEAD_DIM : (h + 1) * HEAD_DIM])
            for h in range(heads)
        ]
        for chunk in range(count):
            here = slice(chunk * chunk_keys, (chunk + 1) * chunk_keys)
            parts = allowed(bits, chunk, chunk_keys)
            for h in range(heads):
                part = slice(h * HEAD_DIM, (h + 1) * HEAD_DIM)
                top, weight, sums = state[h]
                scores = dot_nt(qm[:, part], kv[here, part]) * factor
                scores = select_tiles(parts, scores, -jnp.inf)
                new_top = jnp.maximum(top, jnp.max(scores, axis=1, keepdims=True))
                shrink = jnp.exp2(top - new_top)
                expo = jnp.exp2(scores - new_top)
                weight = weight * shrink + jnp.sum(expo, axis=1, keepdims=True)
                value = kv[here, width + h * HEAD_DIM : width + (h + 1) * HEAD_DIM]
                sums = sums * shrink + dot(expo.astype(BF), value)
                state[h] = (new_top, weight, sums)
        for h in range(heads):
            high[:, h : h + 1], total[:, h : h + 1] = state[h][0], state[h][1]
            out[:, h * HEAD_DIM : (h + 1) * HEAD_DIM] = state[h][2]

    for h in range(heads):
        part = slice(h * HEAD_DIM, (h + 1) * HEAD_DIM)
        sums = total[:, h : h + 1]
        values = out[:, part] / sums
        out[:, part] = values
        low[:, part] = values.astype(BF)
        lse[:, h : h + 1] = high[:, h : h + 1] + jnp.log2(sums)


def attend(flag, ql, qm, kl, vl, words, kv, heads):
    length, width = ql.shape
    span = min(256, length)
    keys = kv.shape[0]
    return pl.pallas_call(
        functools.partial(attend_kernel, heads, min(1024, keys)),
        grid=(length // span,),
        in_specs=[
            pl.BlockSpec(memory_space=pltpu.SMEM),
            rows_of(span, width),
            rows_of(span, width),
            all_of(length, width),
            all_of(length, width),
            rows_of(span, LANES),
            all_of(keys, 2 * width),
        ],
        out_specs=[rows_of(span, width), rows_of(span, width), rows_of(span, LANES)],
        out_shape=[
            jax.ShapeDtypeStruct((length, width), F32),
            jax.ShapeDtypeStruct((length, width), BF),
            jax.ShapeDtypeStruct((length, LANES), F32),
        ],
        scratch_shapes=[pltpu.VMEM((span, LANES), F32), pltpu.VMEM((span, LANES), F32)],
        compiler_params=params(),
        name="attend",
    )(flag, ql, qm, kl, vl, words, kv)


def attend_back_kernel(
    heads, chunk_keys, flag, ql, qm, kl, vl, words, kv, att, go, lse, cosq, sinq, cosk, sink,
    gq, gk, gv, sum_k, sum_v, sum_q,
):
    span = ql.shape[0]
    length = kl.shape[0]
    width = heads * HEAD_DIM
    factor = SCALE * LOG2E
    step = pl.program_id(0)
    last = pl.num_programs(0) - 1
    seen = causal(span, length)

    @pl.when(step == 0)
    def _():
        sum_k[...] = jnp.zeros_like(sum_k)
        sum_v[...] = jnp.zeros_like(sum_v)

    deltas = []
    for h in range(heads):
        part = slice(h * HEAD_DIM, (h + 1) * HEAD_DIM)
        grad = go[:, part]
        delta = jnp.sum(grad.astype(F32) * att[:, part], axis=1, keepdims=True)
        deltas.append(delta)
        query = ql[:, part]
        scores = dot_nt(query, kl[:, part]) * factor
        prob = jnp.where(seen, jnp.exp2(scores - lse[:, h : h + 1]), 0.0)
        grad_prob = dot_nt(grad, vl[:, part])
        grad_scores = (prob * (grad_prob - delta)).astype(BF)
        sum_v[:, part] += dot_tn(prob.astype(BF), grad)
        sum_k[:, part] += dot_tn(grad_scores, query)
        back = dot(grad_scores, kl[:, part]) * SCALE
        back = back * cosq[...] - pltpu.roll(back, HEAD_DIM // 2, 1) * sinq[...]
        sum_q[:, part] = back

    @pl.when(flag[0] > 0)
    def _():
        bits = words[...]
        count = kv.shape[0] // chunk_keys
        sums = [None] * heads
        for chunk in range(count):
            here = slice(chunk * chunk_keys, (chunk + 1) * chunk_keys)
            parts = allowed(bits, chunk, chunk_keys)
            for h in range(heads):
                part = slice(h * HEAD_DIM, (h + 1) * HEAD_DIM)
                key = kv[here, part]
                scores = dot_nt(qm[:, part], key) * factor
                prob = select_tiles(parts, jnp.exp2(scores - lse[:, h : h + 1]), 0.0)
                value = kv[here, width + h * HEAD_DIM : width + (h + 1) * HEAD_DIM]
                grad_prob = dot_nt(go[:, part], value)
                grad_scores = (prob * (grad_prob - deltas[h])).astype(BF)
                fresh = dot(grad_scores, key)
                sums[h] = fresh if sums[h] is None else sums[h] + fresh
        for h in range(heads):
            sum_q[:, h * HEAD_DIM : (h + 1) * HEAD_DIM] += sums[h] * SCALE

    gq[...] = sum_q[...].astype(BF)

    @pl.when(step == last)
    def _():
        gv[...] = sum_v[...].astype(BF)
        for h in range(heads):
            part = slice(h * HEAD_DIM, (h + 1) * HEAD_DIM)
            back = sum_k[:, part] * SCALE
            back = back * cosk[...] - pltpu.roll(back, HEAD_DIM // 2, 1) * sink[...]
            gk[:, part] = back.astype(BF)


def attend_back(flag, ql, qm, kl, vl, words, kv, att, go, lse, cosine, sine, heads):
    length, width = ql.shape
    span = min(256, length)
    keys = kv.shape[0]
    low = jax.ShapeDtypeStruct((length, width), BF)
    return pl.pallas_call(
        functools.partial(attend_back_kernel, heads, min(1024, keys)),
        grid=(length // span,),
        in_specs=[
            pl.BlockSpec(memory_space=pltpu.SMEM),
            rows_of(span, width),
            rows_of(span, width),
            all_of(length, width),
            all_of(length, width),
            rows_of(span, LANES),
            all_of(keys, 2 * width),
            rows_of(span, width),
            rows_of(span, width),
            rows_of(span, LANES),
            rows_of(span, HEAD_DIM),
            rows_of(span, HEAD_DIM),
            all_of(length, HEAD_DIM),
            all_of(length, HEAD_DIM),
        ],
        out_specs=[rows_of(span, width), all_of(length, width), all_of(length, width)],
        out_shape=[low] * 3,
        scratch_shapes=[
            pltpu.VMEM((length, width), F32),
            pltpu.VMEM((length, width), F32),
            pltpu.VMEM((span, width), F32),
        ],
        compiler_params=params(),
        name="attend_back",
    )(flag, ql, qm, kl, vl, words, kv, att, go, lse, cosine, sine, cosine, sine)


def norm_rows(values):
    row_scale = lax.rsqrt(jnp.mean(values * values, axis=-1, keepdims=True) + NORM_EPS)
    return (values * row_scale, row_scale)


def norm_back(grad_normed, unit_rows, row_scale, gain_row):
    weighted = grad_normed * gain_row
    inner = jnp.mean(weighted * unit_rows, axis=-1, keepdims=True)
    return row_scale * (weighted - unit_rows * inner)


def rotation(length):
    half = HEAD_DIM // 2
    frequency = jnp.exp(-jnp.log(10000.0) * jnp.arange(half, dtype=F32) / half)
    grid = jnp.arange(length, dtype=F32)[:, None] * frequency[None, :]
    cos, sin = jnp.cos(grid), jnp.sin(grid)
    return jnp.concatenate([cos, cos], 1), jnp.concatenate([-sin, sin], 1)


def mask_words(neighbours, per_device):
    memory = per_device * lax.axis_size("docs") * lax.axis_size("seq")
    doc, slot = neighbours // memory, neighbours % memory
    source, row = slot // per_device, slot % per_device
    place = source * (2 * per_device) + doc * per_device + row
    bit = jnp.left_shift(jnp.int32(1), place // LANES)
    lane = jnp.arange(LANES, dtype=jnp.int32)
    hits = jnp.where((place % LANES)[:, :, None] == lane, bit[:, :, None], 0)
    return lax.reduce(hits, jnp.int32(0), lax.bitwise_or, (1,))


def shards(
    tokens, cotangent, cache_keys, cache_values, neighbours, partner, has_memory,
    w_heads, moment_heads, square_heads, w_merge, moment_merge, square_merge,
    w_gate, moment_gate, square_gate, w_up, moment_up, square_up,
    w_down, moment_down, square_down, gains, moment_gains, square_gains,
):
    _, rows, width = tokens.shape
    seq_count = lax.axis_size("seq")
    docs_count = lax.axis_size("docs")
    devices = seq_count * docs_count
    seq_index = lax.axis_index("seq")
    doc_index = lax.axis_index("docs")
    length = rows * seq_count
    heads = HEADS // seq_count
    cols = heads * HEAD_DIM
    weight_rows = w_heads.shape[0]
    down_rows = w_down.shape[0]
    inner = w_gate.shape[1] // seq_count
    inner_pad = -(-inner // LANES) * LANES
    per_device = cache_keys.shape[1]
    masters = (w_heads, w_merge, w_gate, w_up, w_down, gains)
    moments = (moment_heads, moment_merge, moment_gate, moment_up, moment_down, moment_gains)
    squares = (square_heads, square_merge, square_gate, square_up, square_down, square_gains)
    decays = (DECAY, DECAY, DECAY, DECAY, DECAY, 0.0)
    lows = [member.astype(BF) for member in masters]

    pair = jnp.stack([cache_keys, cache_values], axis=2)
    pair = jnp.stack([pair, jnp.take(pair, partner, axis=0)], axis=1)
    pair = pair.reshape(docs_count, 2 * per_device, 2, seq_count, cols)
    pair = pair.transpose(0, 3, 1, 2, 4).reshape(devices, 2 * per_device, 2 * cols)
    memory = lax.all_to_all(pair, ("docs", "seq"), split_axis=0, concat_axis=0, tiled=True)
    memory = memory.reshape(devices * 2 * per_device, 2 * cols)
    flag = jnp.take(has_memory, doc_index[None])

    def columns(member):
        split = member.reshape(weight_rows, docs_count, seq_count, down_rows)
        split = split.transpose(2, 0, 1, 3).reshape(seq_count, weight_rows, inner)
        return jnp.pad(split, ((0, 0), (0, 0), (0, inner_pad - inner)))

    by_head = lows[0].reshape(weight_rows, 3, seq_count, cols).transpose(2, 0, 1, 3)
    by_head = by_head.reshape(seq_count, weight_rows, 3 * cols)
    gain_cols = jnp.pad(lows[5].T, ((0, 0), (0, LANES - 2)))
    gain_cols = jnp.broadcast_to(gain_cols[None], (seq_count, weight_rows, LANES))
    first = seq_swap(jnp.concatenate([by_head, gain_cols], axis=2))
    first = docs_gather(first.reshape(seq_count * weight_rows, 3 * cols + LANES))
    first = first.reshape(width, 3 * cols + LANES)
    heads_here = first[:, : 3 * cols]
    gain_one = first[:, 3 * cols].astype(F32)[None, :]
    gain_two = first[:, 3 * cols + 1].astype(F32)[None, :]

    x_low = seq_gather(tokens[0])
    words = mask_words(seq_gather(neighbours[0]), per_device)
    cosine, sine = rotation(length)
    normed_one, query_local, query_memory, key_local, value_local = project(
        x_low, gain_one, heads_here, cosine, sine, heads
    )

    second = docs_gather(jnp.concatenate([lows[1], lows[4]], axis=0))
    merge_here = second[:, :weight_rows].reshape(docs_count * weight_rows, width)
    merge_full = seq_gather(merge_here).reshape(seq_count, docs_count, weight_rows, width)
    merge_full = merge_full.transpose(1, 0, 2, 3).reshape(width, width)
    down_here = second[:, weight_rows:].reshape(inner, width)
    down_here = jnp.pad(down_here, ((0, inner_pad - inner), (0, 0)))
    third = seq_swap(jnp.concatenate([columns(lows[2]), columns(lows[3])], axis=2))
    third = docs_gather(third.reshape(seq_count * weight_rows, 2 * inner_pad))
    gate_up = third.reshape(width, 2 * inner_pad)
    grad_low = seq_gather(cotangent[0])

    attended, blended_here, lse = attend(
        flag, query_local, query_memory, key_local, value_local, words, memory, heads
    )

    def mine(member):
        return lax.dynamic_slice_in_dim(member, seq_index * rows, rows, 0)

    blended = seq_gather(blended_here)
    blended = blended.reshape(seq_count, length, cols).transpose(1, 0, 2).reshape(length, width)
    middle = x_low.astype(F32) + jnp.dot(blended, merge_full, preferred_element_type=F32)
    unit_two, _ = norm_rows(middle)
    normed_two = (unit_two * gain_two).astype(BF)
    raw = jnp.dot(normed_two, gate_up, preferred_element_type=F32)
    gate_raw, up_raw = raw[:, :inner_pad], raw[:, inner_pad:]
    sigmoid_gate = jax.nn.sigmoid(gate_raw)
    silu_gate = gate_raw * sigmoid_gate
    active = (silu_gate * up_raw).astype(BF)
    grad_active = dot_nt(grad_low, down_here)
    grad_gate = grad_active * up_raw * sigmoid_gate * (1.0 + gate_raw * (1.0 - sigmoid_gate))
    grad_up = grad_active * silu_gate
    grad_raw = jnp.concatenate([grad_gate.astype(BF), grad_up.astype(BF)], axis=1)

    grad_normed_two = seq_reduce(dot_nt(grad_raw, gate_up))
    middle_mine = mine(middle)
    unit_mine, scale_mine = norm_rows(middle_mine)
    grad_middle = cotangent[0].astype(F32) + norm_back(
        grad_normed_two, unit_mine, scale_mine, gain_two
    )
    grad_branch = seq_gather(grad_middle.astype(BF))
    merge_rows = lax.dynamic_slice_in_dim(merge_full, seq_index * cols, cols, 0)
    grad_attended = dot_nt(grad_branch, merge_rows).astype(BF)

    g_raw = dot_tn(normed_two, grad_raw).astype(BF)
    g_raw = lax.psum_scatter(g_raw, "docs", scatter_dimension=0, tiled=True)
    g_down = dot_tn(active, grad_low)[:inner].astype(BF)
    g_down = lax.psum_scatter(g_down, "docs", scatter_dimension=0, tiled=True)
    g_merge = dot_tn(blended, grad_branch).reshape(docs_count, seq_count, weight_rows, width)
    g_merge = lax.dynamic_index_in_dim(g_merge, seq_index, 1, False).astype(BF)
    g_merge = lax.psum_scatter(
        g_merge.reshape(docs_count * weight_rows, width), "docs", scatter_dimension=0, tiled=True
    )

    down_out = jnp.dot(active, down_here, preferred_element_type=F32)
    activations = (middle_mine + seq_reduce(down_out)).astype(BF)[None]

    grad_q, grad_k, grad_v = attend_back(
        flag, query_local, query_memory, key_local, value_local, words, memory,
        attended, grad_attended, lse, cosine, sine, heads,
    )
    grad_projected = jnp.concatenate([grad_q, grad_k, grad_v], axis=1)
    g_heads = dot_tn(normed_one, grad_projected)
    g_heads = docs_reduce(g_heads.reshape(docs_count, width // docs_count, 3 * cols))
    grad_normed_one = seq_reduce(dot_nt(grad_projected, heads_here))
    unit_one, scale_one = norm_rows(tokens[0].astype(F32))
    input_grad = grad_middle + norm_back(grad_normed_one, unit_one, scale_one, gain_one)
    input_grad = input_grad[None]

    def own_rows(member):
        return seq_swap(member.astype(BF).reshape(seq_count, weight_rows, member.shape[1]))

    g_heads = own_rows(g_heads).reshape(seq_count, weight_rows, 3, cols)
    g_heads = g_heads.transpose(1, 2, 0, 3).reshape(weight_rows, 3 * width).astype(F32)
    g_raw = own_rows(g_raw).reshape(seq_count, weight_rows, 2, inner_pad)[..., :inner]
    g_raw = g_raw.reshape(seq_count, weight_rows, 2, docs_count, down_rows)
    g_raw = g_raw.transpose(2, 1, 3, 0, 4).reshape(2, weight_rows, inner * seq_count).astype(F32)
    g_gate, g_up = g_raw[0], g_raw[1]
    gain_rows = [lows[5][0].astype(F32), lows[5][1].astype(F32)]
    g_gain_one = jnp.sum(g_heads * lows[0].astype(F32), axis=1) / gain_rows[0]
    g_gain_two = (
        jnp.sum(g_gate * lows[2].astype(F32) + g_up * lows[3].astype(F32), axis=1) / gain_rows[1]
    )
    reduced = (
        g_heads,
        g_merge.astype(F32),
        g_gate,
        g_up,
        g_down.astype(F32),
        jnp.stack([g_gain_one, g_gain_two]),
    )

    weight_local = jnp.stack([jnp.sum(member * member) for member in masters])
    grad_local = sum(jnp.sum(member * member) for member in reduced)
    totals = sum_everywhere(jnp.concatenate([grad_local[None], weight_local]))
    grad_norm = jnp.sqrt(totals[0])
    factor = CLIP / jnp.maximum(grad_norm, CLIP)
    fix_one = 1.0 - BETA_ONE**STEP
    fix_two = 1.0 - BETA_TWO**STEP
    new_moments = []
    new_squares = []
    directions = []
    for master, moment, square, gradient, decay_rate in zip(
        masters, moments, squares, reduced, decays
    ):
        clipped = factor * gradient
        moment_new = BETA_ONE * moment + (1.0 - BETA_ONE) * clipped
        square_new = BETA_TWO * square + (1.0 - BETA_TWO) * clipped * clipped
        direction = (
            moment_new / fix_one / (jnp.sqrt(square_new / fix_two) + ADAM_EPS) + decay_rate * master
        )
        new_moments.append(moment_new)
        new_squares.append(square_new)
        directions.append(direction)
    update_local = jnp.stack([jnp.sum(member * member) for member in directions])
    weight_norm = jnp.sqrt(totals[1:])
    update_norm = jnp.sqrt(sum_everywhere(update_local))
    trust = weight_norm / update_norm
    results = [activations, input_grad]
    for place, master in enumerate(masters):
        new_weight = master - RATE * trust[place] * directions[place]
        results += [new_moments[place], new_squares[place], new_weight]
    return (*results, grad_norm, jnp.stack([weight_norm, update_norm]))


def solution(mesh):
    by_token = P("docs", "seq", None)
    by_slot = P(None, ("docs", "seq"), None)
    by_row = P(("docs", "seq"), None)
    by_gain = P(None, ("docs", "seq"))
    return jax.shard_map(
        shards,
        mesh=mesh,
        in_specs=(by_token, by_token, by_slot, by_slot, by_token, P(), P())
        + (by_row,) * 15
        + (by_gain,) * 3,
        out_specs=(by_token, by_token) + (by_row,) * 15 + (by_gain,) * 3 + (P(), P()),
        check_vma=False,
    )
```

time: 2020 us -> 657 us (0.33)
  waiting for transfers between devices: 1560 us -> 233 us
  blocking collectives: 192 us -> 0 us
  starting transfers between devices: 8.29 us -> 82.3 us
  matrix products: 111 us -> 38.3 us
  local copies, waits for them, and re-layouts: 38.1 us -> 110 us
  Pallas kernels: 0 us -> 67.1 us
  other arithmetic: 66.7 us -> 90.1 us
    reduce_scatter x7 -> x3, waiting for transfers between devices: 931 us -> 54.1 us  [the longest x1 54.1 us: shards(): g_raw = lax.psum_scatter(g_raw, 'docs', scatter_dimension=0, tiled=True)]
    all_gather x8 -> x0, waiting for transfers between devices: 415 us -> none  [the longest x1 101 us: shards(): memory = lax.all_gather(arrived, 'seq', axis=1, tiled=True)]
    unnamed x17 -> x3, waiting for transfers between devices: 217 us -> 0.05 us
    ppermute x0 -> x68, waiting for transfers between devices: none -> 178 us  [the longest x30 73.3 us: send_seq(): return lax.ppermute(x, 'seq', pairs)]
    all_gather x1 -> x0, blocking collectives: 114 us -> none  [shards(): lax.all_gather(low_masters[5], ('docs', 'seq'), axis=1, tiled=True)]
    ppermute x0 -> x68, starting transfers between devices: none -> 78 us  [the longest x24 45.2 us: send_z(): return lax.ppermute(x, 'docs', pairs)]
    psum x2 -> x0, blocking collectives: 77.7 us -> none  [the longest x1 40.9 us: shards(): update_total = lax.psum(update_local, ('docs', 'seq'))]
    dot_general x21 -> x11, matrix products: 111 us -> 38.3 us  [the longest x4 14.6 us: dot_tn(): lax.dot_general(a, b, (((0,), (0,)), ((), ())), preferred_element_type=F32)]
  transfers between devices with their start and end apart: 17 -> 72, of which waited for: 16 -> 35; matrix products, arithmetic and copies ran while one was open for 6% -> 27% of each run, Pallas kernels for 0% -> 10%
where the time goes in v1:
time: 657 us; the launch traced here: 646 us
  waiting for transfers between devices  233 us (35%)
  local copies, waits for them, and re-layouts  110 us (17%)
  other arithmetic  90.1 us (14%)
  starting transfers between devices  82.3 us (13%)
  Pallas kernels  67.1 us (10%)
  matrix products  38.3 us (6%)
  between operations  25.9 us (4%)
    ppermute x30, waiting for transfers between devices, send_seq(): return lax.ppermute(x, 'seq', pairs)  73.3 us
    reduce_scatter x1, waiting for transfers between devices, shards(): g_raw = lax.psum_scatter(g_raw, 'docs', scatter_dimension=0, tiled=True)  54.1 us
    ppermute x24, waiting for transfers between devices, send_z(): return lax.ppermute(x, 'docs', pairs)  45.8 us
    ppermute x24, starting transfers between devices, send_z(): return lax.ppermute(x, 'docs', pairs)  45.2 us
    ppermute x4, waiting for transfers between devices, send_x(): return lax.ppermute(x, 'docs', pairs)  38.1 us
    pallas_call x1, Pallas kernels, attend(): pl.pallas_call(functools.partial(attend_kernel, heads, min(1024, keys)),...  30.9 us
    pallas_call x1, Pallas kernels, attend_back(): pl.pallas_call(functools.partial(attend_back_kernel, heads, min(1024, key...  30.1 us
    ppermute x10, waiting for transfers between devices, sum_everywhere(): lax.ppermute(values, axis, [(i, i ^ reach) for i in range(count)])  21.2 us
  transfers between devices with their start and end apart: 72, of which 35 were waited for; matrix products, arithmetic and copies ran while one was open for 27% of the time, Pallas kernels for 10%

profile of v1, /device:TPU:0, one launch (start us, length us, event | category | flops | bytes accessed | tf_op | source)
XLA Modules:
  0.0 645.9 jit_solution(7171283186759071874)
XLA Ops:
  12.7 6.3 collective-permute-start.16
  40.7 7.8 %reshape.467 = bf16[8,128,2,4,256]{4,3,1,2,0:T(4,128)(2,1)} reshape(bf16[8,2,64,2,1024]{4,2,1,3,0:T(8,128)(2,1)} %copy.163) | data formatting | bytes 8388608 | tf_op jit(solution)/shard_map/reshape | solution.py:505
  48.5 7.5 %copy.164 = bf16[8,4,128,2,256]{2,4,3,1,0:T(8,128)(2,1)} copy(bf16[8,4,128,2,256]{4,1,2,3,0:T(4,128)(2,1)} %bitcast.369) | data formatting | bytes 8388608 | tf_op jit(solution)/shard_map/transpose | solution.py:506
  74.9 13.4 %collective-permute-done.3 = bf16[32,896]{1,0:T(8,128)(2,1)S(1)} collective-permute-done((bf16[32,896]{1,0:T(8,128)(2,1)S(1)}, bf16[32,896]{1,0:T(8,128)(2,1)S(1)}, u32[]{:S(2)}, u32[]{:S(2)}) %collective-permute-start.3) | collective-permute-done | bytes 57376 | tf_op jit(solution)/shard_map/ppermute | solution.py:48
  119.2 20.6 %select_reduce_fusion.words = s32[1024,128]{1,0:T(8,128)} fusion(s32[1024,64]{1,0:T(8,128)S(1)} %copy.162, s32[1024,64]{1,0:T(8,128)S(1)} %copy.161), kind=kLoop, calls=%fused_computation.1 | loop fusion | flops 25034752 | bytes 1048576 | tf_op jit(solution)/shard_map/reduce | solution.py:474
  144.6 5.2 collective-permute-start.5
  172.2 10.0 %collective-permute-done.19 = bf16[120,1024]{1,0:T(8,128)(2,1)S(1)} collective-permute-done((bf16[120,1024]{1,0:T(8,128)(2,1)S(1)}, bf16[120,1024]{1,0:T(8,128)(2,1)S(1)}, u32[]{:S(2)}, u32[]{:S(2)}) %collective-permute-start.19) | collective-permute-done | bytes 245792 | tf_op jit(solution)/shard_map/ppermute | solution.py:60
  187.7 6.3 collective-permute-done.8
  199.0 9.6 %collective-permute-done.31 = bf16[128,1536]{1,0:T(8,128)(2,1)S(1)} collective-permute-done((bf16[128,1536]{1,0:T(8,128)(2,1)S(1)}, bf16[128,1536]{1,0:T(8,128)(2,1)S(1)}, u32[]{:S(2)}, u32[]{:S(2)}) %collective-permute-start.31) | collective-permute-done | bytes 393248 | tf_op jit(solution)/shard_map/ppermute | solution.py:60
  219.9 18.7 %collective-permute-done.11 = bf16[4,128,896]{2,1,0:T(8,128)(2,1)S(1)} collective-permute-done((bf16[4,128,896]{2,1,0:T(8,128)(2,1)S(1)}, bf16[4,128,896]{2,1,0:T(8,128)(2,1)S(1)}, u32[]{:S(2)}, u32[]{:S(2)}) %collective-permute-start.11) | collective-permute-done | bytes 917536 | tf_op jit(solution)/shard_map/ppermute | solution.py:54
  241.4 6.1 project.1
  249.1 6.5 %copy.165 = bf16[32,128,512]{2,1,0:T(8,128)(2,1)} copy(bf16[32,128,512]{1,2,0:T(8,128)(2,1)} %all-to-all-done) | data formatting | bytes 8388608 | tf_op jit(solution)/shard_map/all_to_all | solution.py:507
  255.6 30.9 %attend.1 = (f32[1024,256]{1,0:T(8,128)}, bf16[1024,256]{1,0:T(8,128)(2,1)}, f32[1024,128]{1,0:T(8,128)}) custom-call(s32[1]{0:T(128)S(6)} %select_n.550.flag, bf16[1024,256]{1,0:T(8,128)(2,1)} %get-tuple-element.33.ql, bf16[1024,256]{1,0:T(8,128)(2,1)} %get-tuple-element.34.qm, bf16[1024,256]{1,0:T(8,128)(2,1)} %get-tuple-element.35.kl, ...), custom_call_target="tpu_custom_call" | custom-call | tf_op jit(solution)/shard_map/attend/pallas_call | solution.py:320
  288.6 12.4 %collective-permute-done.14 = bf16[1024,256]{1,0:T(8,128)(2,1)S(1)} collective-permute-done((bf16[1024,256]{1,0:T(8,128)(2,1)}, bf16[1024,256]{1,0:T(8,128)(2,1)S(1)}, u32[]{:S(2)}, u32[]{:S(2)}) %collective-permute-start.14) | collective-permute-done | bytes 524320 | tf_op jit(solution)/shard_map/ppermute | solution.py:48
  312.7 5.0 multiply_reduce_fusion
  347.9 6.1 collective-permute-done.36
  354.0 10.2 %collective-permute-done.40 = bf16[256,1024]{1,0:T(8,128)(2,1)S(1)} collective-permute-done((bf16[256,1024]{1,0:T(8,128)(2,1)}, bf16[256,1024]{1,0:T(8,128)(2,1)S(1)}, u32[]{:S(2)}, u32[]{:S(2)}) %collective-permute-start.40) | collective-permute-done | bytes 524320 | tf_op jit(solution)/shard_map/ppermute | solution.py:48
  370.7 12.2 %collective-permute-done.41 = bf16[256,1024]{1,0:T(8,128)(2,1)S(1)} collective-permute-done((bf16[256,1024]{1,0:T(8,128)(2,1)S(1)}, bf16[256,1024]{1,0:T(8,128)(2,1)S(1)}, u32[]{:S(2)}, u32[]{:S(2)}) %collective-permute-start.41) | collective-permute-done | bytes 524320 | tf_op jit(solution)/shard_map/ppermute | solution.py:48
  389.0 8.5 %convolution_convert_fusion = bf16[1024,1536]{1,0:T(8,128)(2,1)} fusion(f32[1024,1024]{1,0:T(8,128)} %copy-done.23, f32[1024]{0:T(1024)S(1)} %get-tuple-element.55, f32[1024]{0:T(1024)S(1)} %add_rsqrt_fusion, bf16[1024,768]{1,0:T(8,128)(2,1)} %copy-done.38, bf16[1024,768]{1,0:T(8,128)(2,1)} %copy-done.37), kind=kOutput, calls=%fused_computation.7 | convolution fusion | flops 3232235520 | bytes 10493952 | tf_op jit(solution)/shard_map/dot_general | solution.py:186
  400.2 30.1 %attend_back.1 = (bf16[1024,256]{1,0:T(8,128)(2,1)}, bf16[1024,256]{1,0:T(8,128)(2,1)}, bf16[1024,256]{1,0:T(8,128)(2,1)}) custom-call(s32[1]{0:T(128)S(6)} %select_n.550.flag, bf16[1024,256]{1,0:T(8,128)(2,1)} %get-tuple-element.33.ql, bf16[1024,256]{1,0:T(8,128)(2,1)} %get-tuple-element.34.qm, bf16[1024,256]{1,0:T(8,128)(2,1)} %get-tuple-element.35.kl, ...), custom_call_target="tpu_custom_call" | custom-call | tf_op jit(solution)/shard_map/attend_back/pallas_call | solution.py:416
  442.4 15.2 %collective-permute-done.45 = bf16[4,128,768]{2,1,0:T(8,128)(2,1)} collective-permute-done((bf16[4,128,768]{2,1,0:T(8,128)(2,1)S(1)}, bf16[4,128,768]{2,1,0:T(8,128)(2,1)}, u32[]{:S(2)}, u32[]{:S(2)}) %collective-permute-start.45) | collective-permute-done | bytes 786464 | tf_op jit(solution)/shard_map/ppermute | solution.py:54
  477.7 5.4 collective-permute-start.48
  489.6 7.1 %collective-permute-done.51 = bf16[128,768]{1,0:T(8,128)(2,1)S(1)} collective-permute-done((bf16[128,768]{1,0:T(8,128)(2,1)}, bf16[128,768]{1,0:T(8,128)(2,1)S(1)}, u32[]{:S(2)}, u32[]{:S(2)}) %collective-permute-start.51) | collective-permute-done | bytes 196640 | tf_op jit(solution)/shard_map/ppermute | solution.py:60
  505.4 54.1 %reduce-scatter.6.cloned.1.call-done = bf16[128,1536]{1,0:T(8,128)(2,1)} async-done(((bf16[1024,1536]{1,0:T(8,128)(2,1)}), bf16[128,1536]{1,0:T(8,128)(2,1)}) %reduce-scatter.6.cloned.1.call-update) | async-done | bytes 393232 | tf_op jit(solution)/shard_map/reduce_scatter | solution.py:578
  (483 shorter events, 304.8 us)
Async XLA Ops:
  11.4 133.2 %collective-permute-start.17 = (bf16[120,1024]{1,0:T(8,128)(2,1)}, bf16[120,1024]{1,0:T(8,128)(2,1)}, u32[]{:S(2)}, u32[]{:S(2)}) collective-permute-start(bf16[120,1024]{1,0:T(8,128)(2,1)} %pad_maximum_fusion.5), channel_id=1, source_target_pairs={{8,0},{12,4},{16,8},{20,12},{24,16},{28,20},{9,1},{13,5},{17,9},{2... | collective-permute-start | bytes 737288 | tf_op jit(solution)/shard_map/ppermute | solution.py:60
  12.7 137.1 %collective-permute-start.16 = (bf16[120,1024]{1,0:T(8,128)(2,1)}, bf16[120,1024]{1,0:T(8,128)(2,1)}, u32[]{:S(2)}, u32[]{:S(2)}) collective-permute-start(bf16[120,1024]{1,0:T(8,128)(2,1)} %pad_maximum_fusion.5), channel_id=1, source_target_pairs={{0,8},{4,12},{8,16},{12,20},{16,24},{20,28},{1,9},{5,13},{9,17},{1... | collective-permute-start | bytes 737288 | tf_op jit(solution)/shard_map/ppermute | solution.py:60
  24.9 76.7 %collective-permute-start.25 = (bf16[32,1536]{1,0:T(8,128)(2,1)}, bf16[32,1536]{1,0:T(8,128)(2,1)}, u32[]{:S(2)}, u32[]{:S(2)}) collective-permute-start(bf16[32,1536]{1,0:T(8,128)(2,1)} %get-tuple-element.107), channel_id=1, source_target_pairs={{0,1},{1,0},{2,3},{3,2},{4,5},{5,4},{6,7},{7,6},{8,9},{9,8},{10,11... | collective-permute-start | bytes 294920 | tf_op jit(solution)/shard_map/ppermute | solution.py:48
  24.9 78.6 %collective-permute-start.26 = (bf16[32,1536]{1,0:T(8,128)(2,1)}, bf16[32,1536]{1,0:T(8,128)(2,1)}, u32[]{:S(2)}, u32[]{:S(2)}) collective-permute-start(bf16[32,1536]{1,0:T(8,128)(2,1)} %get-tuple-element.106), channel_id=1, source_target_pairs={{0,2},{1,3},{2,0},{3,1},{4,6},{5,7},{6,4},{7,5},{8,10},{9,11},{10,... | collective-permute-start | bytes 294920 | tf_op jit(solution)/shard_map/ppermute | solution.py:48
  30.2 42.4 %collective-permute-start.2 = (bf16[32,896]{1,0:T(8,128)(2,1)S(1)}, bf16[32,896]{1,0:T(8,128)(2,1)S(1)}, u32[]{:S(2)}, u32[]{:S(2)}) collective-permute-start(bf16[32,896]{1,0:T(8,128)(2,1)S(1)} %get-tuple-element.117), channel_id=1, source_target_pairs={{0,1},{1,0},{2,3},{3,2},{4,5},{5,4},{6,7},{7,6},{8,9},{9,8},{10,11... | collective-permute-start | bytes 172040 | tf_op jit(solution)/shard_map/ppermute | solution.py:48
  56.0 193.1 %all-to-all-start = ((bf16[32,128,512]{1,2,0:T(8,128)(2,1)}), bf16[32,128,512]{1,2,0:T(8,128)(2,1)}, u32[]{:S(2)}, u32[]{:S(2)}) async-start(bf16[32,128,512]{1,2,0:T(8,128)(2,1)} %bitcast.368), calls=%async_computation | async-start | bytes 8388608 | tf_op jit(solution)/shard_map/all_to_all | solution.py:507
  60.1 426.3 %reduce-scatter.8.cloned.1.call-start = ((), (), s32[]{:S(2)}) async-start(), calls=%async_computation.6 | async-start | bytes 1622016 | tf_op jit(solution)/shard_map/reduce_scatter | solution.py:580
  101.6 38.2 %collective-permute-start = (bf16[256,1024]{1,0:T(8,128)(2,1)S(1)}, bf16[256,1024]{1,0:T(8,128)(2,1)}, u32[]{:S(2)}, u32[]{:S(2)}) collective-permute-start(bf16[256,1024]{1,0:T(8,128)(2,1)S(1)} %bitcast.376), channel_id=1, source_target_pairs={{0,2},{1,3},{2,0},{3,1},{4,6},{5,7},{6,4},{7,5},{8,10},{9,11},{10,... | collective-permute-start | bytes 1572872 | tf_op jit(solution)/shard_map/ppermute | solution.py:48
  103.5 50.2 %collective-permute-start.37 = (bf16[256,1024]{1,0:T(8,128)(2,1)}, bf16[256,1024]{1,0:T(8,128)(2,1)}, u32[]{:S(2)}, u32[]{:S(2)}) collective-permute-start(bf16[256,1024]{1,0:T(8,128)(2,1)} %bitcast.84), channel_id=1, source_target_pairs={{0,2},{1,3},{2,0},{3,1},{4,6},{5,7},{6,4},{7,5},{8,10},{9,11},{10,... | collective-permute-start | bytes 1572872 | tf_op jit(solution)/shard_map/ppermute | solution.py:48
  114.5 42.4 %collective-permute-start.6 = (bf16[128,896]{1,0:T(8,128)(2,1)}, bf16[128,896]{1,0:T(8,128)(2,1)}, u32[]{:S(2)}, u32[]{:S(2)}) collective-permute-start(bf16[128,896]{1,0:T(8,128)(2,1)} %bitcast.18), channel_id=1, source_target_pairs={{8,0},{12,4},{16,8},{20,12},{24,16},{28,20},{9,1},{13,5},{17,9},{2... | collective-permute-start | bytes 688136 | tf_op jit(solution)/shard_map/ppermute | solution.py:60
  168.2 27.2 %collective-permute-start.30 = (bf16[128,1536]{1,0:T(8,128)(2,1)S(1)}, bf16[128,1536]{1,0:T(8,128)(2,1)S(1)}, u32[]{:S(2)}, u32[]{:S(2)}) collective-permute-start(bf16[128,1536]{1,0:T(8,128)(2,1)S(1)} %collective-permute-done.29), channel_id=1, source_target_pairs={{8,0},{12,4},{16,8},{20,12},{9,1},{13,5},{17,9},{21,13},{10,2},{14... | collective-permute-start | bytes 1179656 | tf_op jit(solution)/shard_map/ppermute | solution.py:60
  169.5 28.6 %collective-permute-start.32 = (bf16[128,1536]{1,0:T(8,128)(2,1)S(1)}, bf16[128,1536]{1,0:T(8,128)(2,1)S(1)}, u32[]{:S(2)}, u32[]{:S(2)}) collective-permute-start(bf16[128,1536]{1,0:T(8,128)(2,1)S(1)} %collective-permute-done.28), channel_id=1, source_target_pairs={{8,16},{12,20},{16,24},{20,28},{9,17},{13,21},{17,25},{21,29},{10,... | collective-permute-start | bytes 1179656 | tf_op jit(solution)/shard_map/ppermute | solution.py:60
  170.9 23.0 %collective-permute-start.8 = (bf16[128,896]{1,0:T(8,128)(2,1)S(1)}, bf16[128,896]{1,0:T(8,128)(2,1)S(1)}, u32[]{:S(2)}, u32[]{:S(2)}) collective-permute-start(bf16[128,896]{1,0:T(8,128)(2,1)S(1)} %collective-permute-done.7), channel_id=1, source_target_pairs={{8,0},{12,4},{9,1},{13,5},{10,2},{14,6},{11,3},{15,7}} | collective-permute-start | bytes 688136 | tf_op jit(solution)/shard_map/ppermute | solution.py:60
  184.4 30.1 %collective-permute-start.1 = (bf16[2,256,1024]{2,1,0:T(8,128)(2,1)}, bf16[2,256,1024]{2,1,0:T(8,128)(2,1)S(1)}, u32[]{:S(2)}, u32[]{:S(2)}) collective-permute-start(bf16[2,256,1024]{2,1,0:T(8,128)(2,1)} %bitcast_dynamic-update-slice_fusion.23), channel_id=1, source_target_pairs={{0,1},{1,0},{2,3},{3,2},{4,5},{5,4},{6,7},{7,6},{8,9},{9,8},{10,11... | collective-permute-start | bytes 3145736 | tf_op jit(solution)/shard_map/ppermute | solution.py:48
  194.1 24.8 %collective-permute-start.22 = (bf16[4,120,1024]{2,1,0:T(8,128)(2,1)}, bf16[4,120,1024]{2,1,0:T(8,128)(2,1)S(1)}, u32[]{:S(2)}, u32[]{:S(2)}) collective-permute-start(bf16[4,120,1024]{2,1,0:T(8,128)(2,1)} %bitcast_dynamic-update-slice_fusion.28), channel_id=1, source_target_pairs={{0,4},{4,0},{8,12},{12,8},{16,20},{20,16},{24,28},{28,24},{1,5},{5... | collective-permute-start | bytes 2949128 | tf_op jit(solution)/shard_map/ppermute | solution.py:54
  198.2 40.4 %collective-permute-start.11 = (bf16[4,128,896]{2,1,0:T(8,128)(2,1)S(1)}, bf16[4,128,896]{2,1,0:T(8,128)(2,1)S(1)}, u32[]{:S(2)}, u32[]{:S(2)}) collective-permute-start(bf16[4,128,896]{2,1,0:T(8,128)(2,1)S(1)} %bitcast_dynamic-update-slice_fusion.32), channel_id=1, source_target_pairs={{0,4},{4,0},{8,12},{12,8},{16,20},{20,16},{24,28},{28,24},{1,5},{5... | collective-permute-start | bytes 2752520 | tf_op jit(solution)/shard_map/ppermute | solution.py:54
  211.8 89.3 %collective-permute-start.34 = (bf16[4,128,1536]{2,1,0:T(8,128)(2,1)}, bf16[4,128,1536]{2,1,0:T(8,128)(2,1)}, u32[]{:S(2)}, u32[]{:S(2)}) collective-permute-start(bf16[4,128,1536]{2,1,0:T(8,128)(2,1)} %bitcast_dynamic-update-slice_fusion.24), channel_id=1, source_target_pairs={{0,4},{4,0},{8,12},{12,8},{16,20},{20,16},{24,28},{28,24},{1,5},{5... | collective-permute-start | bytes 4718600 | tf_op jit(solution)/shard_map/ppermute | solution.py:54
  219.1 29.9 %collective-permute-start.23 = (bf16[256,1024]{1,0:T(8,128)(2,1)S(1)}, bf16[256,1024]{1,0:T(8,128)(2,1)S(1)}, u32[]{:S(2)}, u32[]{:S(2)}) collective-permute-start(bf16[256,1024]{1,0:T(8,128)(2,1)S(1)} %bitcast.397), channel_id=1, source_target_pairs={{0,2},{1,3},{2,0},{3,1},{4,6},{5,7},{6,4},{7,5},{8,10},{9,11},{10,... | collective-permute-start | bytes 1572872 | tf_op jit(solution)/shard_map/ppermute | solution.py:48
  249.0 53.7 %collective-permute-start.24 = (bf16[2,256,1024]{2,1,0:T(8,128)(2,1)S(1)}, bf16[2,256,1024]{2,1,0:T(8,128)(2,1)}, u32[]{:S(2)}, u32[]{:S(2)}) collective-permute-start(bf16[2,256,1024]{2,1,0:T(8,128)(2,1)S(1)} %bitcast_dynamic-update-slice_fusion.19), channel_id=1, source_target_pairs={{0,1},{1,0},{2,3},{3,2},{4,5},{5,4},{6,7},{7,6},{8,9},{9,8},{10,11... | collective-permute-start | bytes 3145736 | tf_op jit(solution)/shard_map/ppermute | solution.py:48
  342.4 21.8 %collective-permute-start.40 = (bf16[256,1024]{1,0:T(8,128)(2,1)}, bf16[256,1024]{1,0:T(8,128)(2,1)S(1)}, u32[]{:S(2)}, u32[]{:S(2)}) collective-permute-start(bf16[256,1024]{1,0:T(8,128)(2,1)} %fusion.24), channel_id=1, source_target_pairs={{0,2},{1,3},{2,0},{3,1},{4,6},{5,7},{6,4},{7,5},{8,10},{9,11},{10,... | collective-permute-start | bytes 1572872 | tf_op jit(solution)/shard_map/ppermute | solution.py:48
  346.4 141.6 %reduce-scatter.4.cloned.1.call-start = ((), (), s32[]{:S(2)}) async-start(), calls=%async_computation.4 | async-start | bytes 589824 | tf_op jit(solution)/shard_map/reduce_scatter | solution.py:583
  389.0 170.5 %reduce-scatter.6.cloned.1.call-start = ((), (), s32[]{:S(2)}) async-start(), calls=%async_computation.5 | async-start | bytes 3538944 | tf_op jit(solution)/shard_map/reduce_scatter | solution.py:578
  442.4 31.7 %collective-permute-start.43 = (bf16[2,256,1024]{2,1,0:T(8,128)(2,1)}, bf16[2,256,1024]{2,1,0:T(8,128)(2,1)}, u32[]{:S(2)}, u32[]{:S(2)}) collective-permute-start(bf16[2,256,1024]{2,1,0:T(8,128)(2,1)} %fusion.15), channel_id=1, source_target_pairs={{0,1},{1,0},{2,3},{3,2},{4,5},{5,4},{6,7},{7,6},{8,9},{9,8},{10,11... | collective-permute-start | bytes 3145736 | tf_op jit(solution)/shard_map/ppermute | solution.py:48
  477.2 22.6 %collective-permute-start.44 = (bf16[256,1024]{1,0:T(8,128)(2,1)}, bf16[256,1024]{1,0:T(8,128)(2,1)S(1)}, u32[]{:S(2)}, u32[]{:S(2)}) collective-permute-start(bf16[256,1024]{1,0:T(8,128)(2,1)} %fusion.25), channel_id=1, source_target_pairs={{0,2},{1,3},{2,0},{3,1},{4,6},{5,7},{6,4},{7,5},{8,10},{9,11},{10,... | collective-permute-start | bytes 1572872 | tf_op jit(solution)/shard_map/ppermute | solution.py:48
  (118 other events, 1148.5 us)
Sparse Core Ops, SparseCore 0:
  346.6 69.1 reduce-scatter.7
  419.1 61.4 reduce-scatter.3
  484.6 74.9 reduce-scatter.5

commit v2 on v1

v2 whole, which is shorter than its diff:
```python
import functools
import math

import jax
import jax.numpy as jnp
from jax import lax
from jax.experimental import pallas as pl
from jax.experimental.pallas import tpu as pltpu
from jax.sharding import PartitionSpec as P

HEADS = 8
HEAD_DIM = 128
STEP = 10
NORM_EPS = 1e-06
BETA_ONE = 0.9
BETA_TWO = 0.999
ADAM_EPS = 1e-06
DECAY = 0.01
RATE = 0.5
CLIP = 1.0
LANES = 128
LOG2E = math.log2(math.e)
SCALE = HEAD_DIM ** (-0.5)
BF = jnp.bfloat16
F32 = jnp.float32
VMEM_LIMIT = 56 * 1024 * 1024


def send(x, axis, bits):
    return lax.ppermute(x, axis, [(i, i ^ bits) for i in range(lax.axis_size(axis))])


def token(*done):
    total = jnp.zeros((), F32)
    for member in done:
        corner = lax.slice(member, (0,) * member.ndim, (1,) * member.ndim)
        total = total + corner.reshape(()).astype(F32) * 0
    return total


def after(x, *done):
    return x + token(*done).astype(x.dtype)


def pieces_of(block, axis):
    bit = lax.axis_size(axis) // 2
    pieces = {0: block}
    while bit:
        pieces.update({k | bit: send(piece, axis, bit) for k, piece in list(pieces.items())})
        bit //= 2
    return [pieces[k] for k in range(len(pieces))]


def pick(pieces, axis, device):
    away = lax.axis_index(axis) ^ device
    picked = pieces[0]
    for k in range(1, len(pieces)):
        picked = jnp.where(away == k, pieces[k], picked)
    return picked


def stack(pieces, axis, dim=0):
    return jnp.concatenate([pick(pieces, axis, j) for j in range(len(pieces))], axis=dim)


def swap(cut):
    me = lax.axis_index("seq")
    return [cut(me)] + [send(cut(me ^ k), "seq", k) for k in range(1, lax.axis_size("seq"))]


def halve(blocks, axis, stage, late=0.0, low=1):
    mine = (lax.axis_index(axis) >> stage) & 1
    pairs = blocks.reshape((-1, 2, low) + blocks.shape[1:])
    away = lax.dynamic_index_in_dim(pairs, 1 - mine, 1, False).astype(BF)
    kept = lax.dynamic_index_in_dim(pairs, mine, 1, False).astype(F32)
    total = (kept + late) + send(away, axis, 1 << stage).astype(F32)
    return total.reshape((-1,) + blocks.shape[1:])


def reduce_over(blocks, axis, stage=0, late=0.0):
    while blocks.shape[0] > 1:
        blocks = halve(blocks, axis, stage, late if blocks.shape[0] == 2 else 0.0)
        stage += 1
    return blocks[0]


def to_everyone(vectors):
    return lax.all_to_all(vectors, ("docs", "seq"), split_axis=0, concat_axis=0, tiled=True)


def dot(a, b):
    return lax.dot_general(a, b, (((1,), (0,)), ((), ())), preferred_element_type=F32)


def dot_nt(a, b):
    return lax.dot_general(a, b, (((1,), (1,)), ((), ())), preferred_element_type=F32)


def dot_tn(a, b):
    return lax.dot_general(a, b, (((0,), (0,)), ((), ())), preferred_element_type=F32)


def params():
    return pltpu.CompilerParams(vmem_limit_bytes=VMEM_LIMIT)


def rows_of(rows, cols):
    return pl.BlockSpec((rows, cols), lambda i: (i, 0))


def all_of(rows, cols):
    return pl.BlockSpec((rows, cols), lambda i: (0, 0))


def cheap():
    return pl.CostEstimate(flops=1, bytes_accessed=1, transcendentals=0)


def waits_for(count):
    return [pl.BlockSpec(memory_space=pl.ANY)] * count


def gate_kernel(*refs):
    pass


def gate(x, *waits):
    return pl.pallas_call(
        gate_kernel,
        in_specs=waits_for(1 + len(waits)),
        out_specs=pl.BlockSpec(memory_space=pl.ANY),
        out_shape=jax.ShapeDtypeStruct(x.shape, x.dtype),
        input_output_aliases={0: 0},
        cost_estimate=cheap(),
        name="gate",
    )(x, *waits)


def pack_memory_kernel(heads, partner, key, value, mate_key, mate_value, *outs):
    for device in range(outs[0].shape[1]):
        for h in range(heads):
            at = slice((device * heads + h) * HEAD_DIM, (device * heads + h + 1) * HEAD_DIM)
            outs[h][0, device, 0, :, :HEAD_DIM] = key[0, :, at]
            outs[h][0, device, 0, :, HEAD_DIM:] = value[0, :, at]
            outs[h][0, device, 1, :, :HEAD_DIM] = mate_key[0, :, at]
            outs[h][0, device, 1, :, HEAD_DIM:] = mate_value[0, :, at]


def pack_memory(partner, cache_keys, cache_values, heads, seq_count):
    docs, rows, width = cache_keys.shape
    own = pl.BlockSpec((1, rows, width), lambda i, p: (i, 0, 0))
    mate = pl.BlockSpec((1, rows, width), lambda i, p: (p[i], 0, 0))
    shape = (docs, seq_count, 2, rows, 2 * HEAD_DIM)
    return pl.pallas_call(
        functools.partial(pack_memory_kernel, heads),
        grid_spec=pltpu.PrefetchScalarGridSpec(
            num_scalar_prefetch=1,
            grid=(docs,),
            in_specs=[own, own, mate, mate],
            out_specs=[pl.BlockSpec((1,) + shape[1:], lambda i, p: (i, 0, 0, 0, 0))] * heads,
        ),
        out_shape=[jax.ShapeDtypeStruct(shape, BF)] * heads,
        compiler_params=params(),
        cost_estimate=cheap(),
        name="pack_memory",
    )(partner, cache_keys, cache_values, cache_keys, cache_values)


def pack_inner_kernel(raw, down, out):
    part = out.shape[1]
    at = 0
    for c in range(raw.shape[1] // part):
        out[at : at + raw.shape[0], :] = raw[:, c * part : (c + 1) * part]
        at += raw.shape[0]
    group = (out.shape[0] - at) // (down.shape[1] // part)
    rest = jnp.zeros((group - down.shape[0], part), F32)
    for c in range(down.shape[1] // part):
        rows = jnp.concatenate([down[:, c * part : (c + 1) * part], rest], axis=0)
        out[at : at + group, :] = rows.astype(BF)
        at += group


def pack_inner(raw, down, group, part):
    rows = raw.shape[0] * (raw.shape[1] // part) + group * (down.shape[1] // part)
    return pl.pallas_call(
        pack_inner_kernel,
        in_specs=[whole(raw), whole(down)],
        out_specs=whole(None),
        out_shape=jax.ShapeDtypeStruct((rows, part), BF),
        cost_estimate=cheap(),
        name="pack_inner",
    )(raw, down)


def rows_at(ref, place, rows):
    return ref.at[pl.ds(pl.multiple_of(place * rows, rows), rows)]


def whole_spec(member):
    return pl.BlockSpec(member.shape, lambda i, here, n=member.ndim: (0,) * n)


def tile_spec(rows, cols):
    return pl.BlockSpec((rows, cols), lambda i, here: (i, 0))


def fixed_spec(rows, cols):
    return pl.BlockSpec((rows, cols), lambda i, here: (0, 0))


def lay_kernel(here, *refs):
    pieces, out = refs[:-1], refs[-1]
    for k, piece in enumerate(pieces):

        @pl.when(here[0] ^ k == pl.program_id(0))
        def _(piece=piece):
            out[...] = piece[...]


def lay_out(here, pieces):
    rows, cols = pieces[0].shape
    return pl.pallas_call(
        lay_kernel,
        grid_spec=pltpu.PrefetchScalarGridSpec(
            num_scalar_prefetch=1,
            grid=(len(pieces),),
            in_specs=[whole_spec(piece) for piece in pieces],
            out_specs=tile_spec(rows, cols),
        ),
        out_shape=jax.ShapeDtypeStruct((len(pieces) * rows, cols), pieces[0].dtype),
        compiler_params=params(),
        cost_estimate=cheap(),
        name="lay_out",
    )(here, *pieces)


def find_words(near, memory, per_device):
    wide = near.astype(F32).T.astype(jnp.int32)
    count = wide.shape[0] // 2
    index = wide[:count] * 64 + wide[count:]
    slot = index & (memory - 1)
    source = slot >> (per_device.bit_length() - 1)
    place = source * (2 * per_device) + (slot & (per_device - 1))
    place = place + (index >> (memory.bit_length() - 1)) * per_device
    bit = jnp.left_shift(jnp.int32(1), place >> 7)
    lane = place & (LANES - 1)
    shape = (LANES, near.shape[0])
    rows = lax.broadcasted_iota(jnp.int32, shape, 0)
    found = jnp.zeros(shape, jnp.int32)
    for n in range(count):
        found = found | jnp.where(rows == lane[n : n + 1], bit[n : n + 1], 0)
    return found.T


def project_kernel(heads, seq, docs, memory, per_device, here, *refs):
    tokens, weights = refs[:seq], refs[seq : seq + docs]
    cosine, sine = refs[seq + docs : seq + docs + 2]
    x, normed, ql, qm, kl, vl, words, weight, gains, held = refs[-10:]
    width = x.shape[1]
    cols = 3 * heads * HEAD_DIM
    step = pl.program_id(0)

    @pl.when(step == 0)
    def _():
        for k in range(docs):
            rows = weights[k].shape[0]
            rows_at(weight, here[1] ^ k, rows)[...] = weights[k][:, :cols]
            rows_at(held, here[1] ^ k, rows)[...] = weights[k][:, cols : cols + LANES].astype(F32)
        for part in range(width // LANES):
            lanes = slice(part * LANES, (part + 1) * LANES)
            gains[:, lanes] = held[lanes, :].T[: gains.shape[0]]

    for k in range(seq):

        @pl.when(here[0] ^ k == step)
        def _(k=k):
            x[...] = tokens[k][:, :width]
            words[...] = find_words(tokens[k][:, width:], memory, per_device)

    values = x[...].astype(F32)
    scale = lax.rsqrt(jnp.mean(values * values, axis=-1, keepdims=True) + NORM_EPS)
    low = (values * scale * gains[0:1, :]).astype(BF)
    normed[...] = low
    out = dot(low, weight[...])
    cos, sin = cosine[...], sine[...]
    for h in range(heads):
        part = slice(h * HEAD_DIM, (h + 1) * HEAD_DIM)
        q, k, v = (
            out[:, (3 * h + j) * HEAD_DIM : (3 * h + j + 1) * HEAD_DIM] for j in range(3)
        )
        qm[:, part] = q.astype(BF)
        ql[:, part] = (q * cos + pltpu.roll(q, HEAD_DIM // 2, 1) * sin).astype(BF)
        kl[:, part] = (k * cos + pltpu.roll(k, HEAD_DIM // 2, 1) * sin).astype(BF)
        vl[:, part] = v.astype(BF)


def project(here, tokens, weights, cosine, sine, heads, memory, per_device, waits):
    rows = tokens[0].shape[0]
    width = tokens[0].shape[1] - LANES
    length = rows * len(tokens)
    cols = heads * HEAD_DIM
    low = jax.ShapeDtypeStruct((length, cols), BF)
    full = jax.ShapeDtypeStruct((length, width), BF)
    return pl.pallas_call(
        functools.partial(project_kernel, heads, len(tokens), len(weights), memory, per_device),
        grid_spec=pltpu.PrefetchScalarGridSpec(
            num_scalar_prefetch=1,
            grid=(len(tokens),),
            in_specs=[whole_spec(member) for member in (*tokens, *weights)]
            + [tile_spec(rows, HEAD_DIM)] * 2
            + waits_for(len(waits)),
            out_specs=[tile_spec(rows, width)] * 2
            + [tile_spec(rows, cols)] * 4
            + [tile_spec(rows, LANES), fixed_spec(width, 3 * cols), fixed_spec(8, width)],
            scratch_shapes=[pltpu.VMEM((width, LANES), F32)],
        ),
        out_shape=[
            full, full, low, low, low, low,
            jax.ShapeDtypeStruct((length, LANES), jnp.int32),
            jax.ShapeDtypeStruct((width, 3 * cols), BF),
            jax.ShapeDtypeStruct((8, width), F32),
        ],
        compiler_params=params(),
        cost_estimate=cheap(),
        name="project",
    )(here, *tokens, *weights, cosine, sine, *waits)


def feed_forward_kernel(heads, seq, docs, here, *refs):
    blended, packed, refs = refs[: seq * heads], refs[seq * heads :][:docs], refs[seq * heads + docs :]
    x, merge, gains, cotangent = refs[:4]
    blend, normed, active, grad_raw, back, middle_mine, raw, down = refs[4:]
    step = pl.program_id(0)
    hidden = down.shape[0]
    part = packed[0].shape[1]
    rows, group = raw.shape[0] // docs, hidden // docs

    @pl.when(step == 0)
    def _():
        for k in range(docs):
            at = 0
            for c in range(raw.shape[1] // part):
                cols = slice(c * part, (c + 1) * part)
                rows_at(raw, here[1] ^ k, rows)[:, cols] = packed[k][at : at + rows, :]
                at += rows
            for c in range(down.shape[1] // part):
                cols = slice(c * part, (c + 1) * part)
                rows_at(down, here[1] ^ k, group)[:, cols] = packed[k][at : at + group, :]
                at += group

    for k in range(seq):
        for h in range(heads):
            at = pl.multiple_of(((here[0] ^ k) * heads + h) * HEAD_DIM, HEAD_DIM)
            blend[:, pl.ds(at, HEAD_DIM)] = blended[k * heads + h][...]
    middle = x[...].astype(F32) + dot(blend[...], merge[...])

    @pl.when(step == here[0])
    def _():
        middle_mine[...] = middle

    scale = lax.rsqrt(jnp.mean(middle * middle, axis=-1, keepdims=True) + NORM_EPS)
    low = (middle * scale * gains[1:2, :]).astype(BF)
    normed[...] = low
    grad_active = dot_nt(cotangent[...], down[...])
    gate_up = dot(low, raw[...])
    gate, up = gate_up[:, :hidden], gate_up[:, hidden:]
    sigmoid = jax.nn.sigmoid(gate)
    silu = gate * sigmoid
    active[...] = (silu * up).astype(BF)
    grad_gate = grad_active * up * sigmoid * (1.0 + gate * (1.0 - sigmoid))
    grad_raw[:, :hidden] = grad_gate.astype(BF)
    grad_raw[:, hidden:] = (grad_active * silu).astype(BF)
    back[...] = dot_nt(grad_raw[...], raw[...]).astype(BF)


def feed_forward(here, blended, packed, x, merge, gains, cotangent, heads, hidden):
    length, width = x.shape
    seq, docs = len(blended) // heads, len(packed)
    rows = length // seq
    double = 2 * hidden
    return pl.pallas_call(
        functools.partial(feed_forward_kernel, heads, seq, docs),
        grid_spec=pltpu.PrefetchScalarGridSpec(
            num_scalar_prefetch=1,
            grid=(seq,),
            in_specs=[tile_spec(rows, HEAD_DIM)] * len(blended)
            + [whole_spec(member) for member in packed]
            + [tile_spec(rows, width), whole_spec(merge), whole_spec(gains)]
            + [tile_spec(rows, width)],
            out_specs=[
                tile_spec(rows, width),
                tile_spec(rows, width),
                tile_spec(rows, hidden),
                tile_spec(rows, double),
                tile_spec(rows, width),
                fixed_spec(rows, width),
                fixed_spec(width, double),
                fixed_spec(hidden, width),
            ],
        ),
        out_shape=[
            jax.ShapeDtypeStruct((length, width), BF),
            jax.ShapeDtypeStruct((length, width), BF),
            jax.ShapeDtypeStruct((length, hidden), BF),
            jax.ShapeDtypeStruct((length, double), BF),
            jax.ShapeDtypeStruct((length, width), BF),
            jax.ShapeDtypeStruct((rows, width), F32),
            jax.ShapeDtypeStruct((width, double), BF),
            jax.ShapeDtypeStruct((hidden, width), BF),
        ],
        compiler_params=params(),
        cost_estimate=cheap(),
        name="feed_forward",
    )(here, *blended, *packed, x, merge, gains, cotangent)


def lower_triangle(span):
    row = lax.broadcasted_iota(jnp.int32, (span, span), 0)
    return lax.broadcasted_iota(jnp.int32, (span, span), 1) <= row


def allowed(words, chunk, chunk_keys):
    tiles = chunk_keys // LANES
    parts = []
    for tile in range(tiles):
        bit = chunk * tiles + tile
        mask = (1 << bit) if bit < 31 else -(1 << 31)
        parts.append((words & jnp.int32(mask)) != 0)
    return parts


def select_tiles(parts, values, other):
    cut = [
        jnp.where(part, values[:, t * LANES : (t + 1) * LANES], other)
        for t, part in enumerate(parts)
    ]
    return jnp.concatenate(cut, axis=1)


def attend_local_kernel(heads, tiles, ql, kl, vl, out, high, total):
    span = ql.shape[0]
    factor = SCALE * LOG2E

    for tile in range(tiles):

        @pl.when(pl.program_id(0) == tile)
        def _(tile=tile):
            seen = lower_triangle(span)
            for h in range(heads):
                part = slice(h * HEAD_DIM, (h + 1) * HEAD_DIM)
                keys = (tile + 1) * span
                scores = dot_nt(ql[:, part], kl[:keys, part]) * factor
                last = jnp.where(seen, scores[:, tile * span :], -jnp.inf)
                scores = jnp.concatenate([scores[:, : tile * span], last], 1) if tile else last
                top = jnp.max(scores, axis=1, keepdims=True)
                expo = jnp.exp2(scores - top)
                high[:, part] = jnp.broadcast_to(top, (span, HEAD_DIM))
                weight = jnp.sum(expo, axis=1, keepdims=True)
                total[:, part] = jnp.broadcast_to(weight, (span, HEAD_DIM))
                out[:, part] = dot(expo.astype(BF), vl[:keys, part])


def attend_local(ql, kl, vl, heads):
    length, width = ql.shape
    span = min(256, length)
    wide = jax.ShapeDtypeStruct((length, width), F32)
    return pl.pallas_call(
        functools.partial(attend_local_kernel, heads, length // span),
        grid=(length // span,),
        in_specs=[rows_of(span, width), all_of(length, width), all_of(length, width)],
        out_specs=[rows_of(span, width)] * 3,
        out_shape=[wide] * 3,
        compiler_params=params(),
        cost_estimate=cheap(),
        name="attend_local",
    )(ql, kl, vl)


def attend_memory_kernel(chunk_keys, flag, qm, words, kv, local, high, total, *refs):
    out, low, lse = refs[-3:]
    factor = SCALE * LOG2E

    def finish(top, weight, sums):
        values = sums / weight
        out[...] = values
        low[...] = values.astype(BF)
        lse[...] = jnp.broadcast_to(top + jnp.log2(weight), lse.shape)

    @pl.when(flag[0] == 0)
    def _():
        finish(high[:, :1], total[:, :1], local[...])

    @pl.when(flag[0] > 0)
    def _():
        bits = words[...]
        query = qm[...]
        top, weight, sums = high[:, :1], total[:, :1], local[...]
        for chunk in range(kv.shape[0] // chunk_keys):
            here = slice(chunk * chunk_keys, (chunk + 1) * chunk_keys)
            scores = dot_nt(query, kv[here, :HEAD_DIM]) * factor
            scores = select_tiles(allowed(bits, chunk, chunk_keys), scores, -jnp.inf)
            new_top = jnp.maximum(top, jnp.max(scores, axis=1, keepdims=True))
            shrink = jnp.exp2(top - new_top)
            expo = jnp.exp2(scores - new_top)
            weight = weight * shrink + jnp.sum(expo, axis=1, keepdims=True)
            sums = sums * shrink + dot(expo.astype(BF), kv[here, HEAD_DIM:])
            top = new_top
        finish(top, weight, sums)


def head_rows(span, head):
    return pl.BlockSpec((span, HEAD_DIM), lambda i: (i, head))


def head_all(length, head):
    return pl.BlockSpec((length, HEAD_DIM), lambda i: (0, head))


def attend_memory(flag, qm, words, kv, local, high, total, head, waits):
    length = qm.shape[0]
    span = min(256, length)
    keys = kv.shape[0]
    return pl.pallas_call(
        functools.partial(attend_memory_kernel, min(1024, keys)),
        grid=(length // span,),
        in_specs=[
            pl.BlockSpec(memory_space=pltpu.SMEM),
            head_rows(span, head),
            rows_of(span, LANES),
            all_of(keys, 2 * HEAD_DIM),
            head_rows(span, head),
            head_rows(span, head),
            head_rows(span, head),
            *waits_for(len(waits)),
        ],
        out_specs=[rows_of(span, HEAD_DIM)] * 3,
        out_shape=[
            jax.ShapeDtypeStruct((length, HEAD_DIM), F32),
            jax.ShapeDtypeStruct((length, HEAD_DIM), BF),
            jax.ShapeDtypeStruct((length, HEAD_DIM), F32),
        ],
        compiler_params=params(),
        cost_estimate=cheap(),
        name="attend_memory",
    )(flag, qm, words, kv, local, high, total, *waits)


def attend_back_kernel(
    chunk_keys, tiles, flag, ql, qm, kl, vl, words, kv, att, go, lse, cosq, sinq, cosk, sink, *refs
):
    out, sum_k, sum_v, sum_q = refs[-4:]
    span = ql.shape[0]
    factor = SCALE * LOG2E
    step = pl.program_id(0)
    grad = go[...]
    delta = jnp.sum(grad.astype(F32) * att[...], axis=1, keepdims=True)
    level = lse[:, :1]

    @pl.when(step == 0)
    def _():
        sum_k[...] = jnp.zeros_like(sum_k)
        sum_v[...] = jnp.zeros_like(sum_v)

    for tile in range(tiles):

        @pl.when(step == tile)
        def _(tile=tile):
            keys = (tile + 1) * span
            query = ql[...]
            scores = dot_nt(query, kl[:keys]) * factor
            prob = jnp.exp2(scores - level)
            last = jnp.where(lower_triangle(span), prob[:, tile * span :], 0.0)
            prob = jnp.concatenate([prob[:, : tile * span], last], 1) if tile else last
            grad_prob = dot_nt(grad, vl[:keys])
            grad_scores = (prob * (grad_prob - delta)).astype(BF)
            sum_v[:keys] += dot_tn(prob.astype(BF), grad)
            sum_k[:keys] += dot_tn(grad_scores, query)
            back = dot(grad_scores, kl[:keys])
            sum_q[...] = back * cosq[...] - pltpu.roll(back, HEAD_DIM // 2, 1) * sinq[...]

    @pl.when(flag[0] > 0)
    def _():
        bits = words[...]
        query = qm[...]
        sums = sum_q[...]
        for chunk in range(kv.shape[0] // chunk_keys):
            here = slice(chunk * chunk_keys, (chunk + 1) * chunk_keys)
            key = kv[here, :HEAD_DIM]
            scores = dot_nt(query, key) * factor
            prob = jnp.exp2(scores - level)
            prob = select_tiles(allowed(bits, chunk, chunk_keys), prob, 0.0)
            grad_prob = dot_nt(grad, kv[here, HEAD_DIM:])
            grad_scores = (prob * (grad_prob - delta)).astype(BF)
            sums = sums + dot(grad_scores, key)
        sum_q[...] = sums

    here = pl.ds(pl.multiple_of(step * span, span), span)
    out[here, :HEAD_DIM] = (sum_q[...] * SCALE).astype(BF)

    @pl.when(step == tiles - 1)
    def _():
        back = sum_k[...] * SCALE
        back = back * cosk[...] - pltpu.roll(back, HEAD_DIM // 2, 1) * sink[...]
        out[:, HEAD_DIM : 2 * HEAD_DIM] = back.astype(BF)
        out[:, 2 * HEAD_DIM :] = sum_v[...].astype(BF)


def attend_back(flag, ql, qm, kl, vl, words, kv, att, go, lse, cosine, sine, head, waits):
    length = ql.shape[0]
    span = min(256, length)
    keys = kv.shape[0]
    return pl.pallas_call(
        functools.partial(attend_back_kernel, min(1024, keys), length // span),
        grid=(length // span,),
        in_specs=[
            pl.BlockSpec(memory_space=pltpu.SMEM),
            head_rows(span, head),
            head_rows(span, head),
            head_all(length, head),
            head_all(length, head),
            rows_of(span, LANES),
            all_of(keys, 2 * HEAD_DIM),
            rows_of(span, HEAD_DIM),
            head_rows(span, head),
            rows_of(span, HEAD_DIM),
            rows_of(span, HEAD_DIM),
            rows_of(span, HEAD_DIM),
            all_of(length, HEAD_DIM),
            all_of(length, HEAD_DIM),
            *waits_for(len(waits)),
        ],
        out_specs=all_of(length, 3 * HEAD_DIM),
        out_shape=jax.ShapeDtypeStruct((length, 3 * HEAD_DIM), BF),
        scratch_shapes=[
            pltpu.VMEM((length, HEAD_DIM), F32),
            pltpu.VMEM((length, HEAD_DIM), F32),
            pltpu.VMEM((span, HEAD_DIM), F32),
        ],
        compiler_params=params(),
        cost_estimate=cheap(),
        name="attend_back",
    )(flag, ql, qm, kl, vl, words, kv, att, go, lse, cosine, sine, cosine, sine, *waits)


def total_of(member):
    return jnp.sum(jnp.sum(member * member, axis=1, keepdims=True), axis=0, keepdims=True)


def lanes_of(values):
    lane = lax.broadcasted_iota(jnp.int32, (1, LANES), 1)
    row = jnp.zeros((1, LANES), F32)
    for place, value in enumerate(values):
        row = jnp.where(lane == place, value, row)
    return row


def row_of(column):
    shape = (column.shape[0], column.shape[0])
    same = lax.broadcasted_iota(jnp.int32, shape, 0) == lax.broadcasted_iota(jnp.int32, shape, 1)
    return jnp.sum(jnp.where(same, column, 0.0), axis=0, keepdims=True)


def grads_kernel(heads, docs, *refs):
    masters, by_head = refs[:6], refs[6]
    merge, raw, down = refs[7:10]
    g_heads, gate, up, g_gains, sums = refs[-5:]
    rows = g_heads.shape[0]
    width = g_heads.shape[1] // 3
    count = by_head.shape[1] // (3 * HEAD_DIM * heads)
    for device in range(count):
        for h in range(heads):
            for j in range(3):
                at = (3 * (device * heads + h) + j) * HEAD_DIM
                to = j * width + (device * heads + h) * HEAD_DIM
                part = by_head[:, at : at + HEAD_DIM].astype(F32)
                g_heads[:, to : to + HEAD_DIM] = part
    seq = raw.shape[0] // rows
    group, part = raw.shape[1] // (2 * docs), gate.shape[1] // (docs * seq)
    for device in range(seq):
        lines = slice(device * rows, (device + 1) * rows)
        for d in range(docs):
            to = (d * seq + device) * part
            for j, target in enumerate((gate, up)):
                at = (j * docs + d) * group
                target[:, to : to + part] = raw[lines, at : at + part].astype(F32)
    low = masters[0][...].astype(BF).astype(F32)
    gain_one = jnp.sum(g_heads[...] * low, axis=1, keepdims=True)
    gain_two = jnp.sum(
        gate[...] * masters[2][...].astype(BF).astype(F32)
        + up[...] * masters[3][...].astype(BF).astype(F32),
        axis=1,
        keepdims=True,
    )
    gain_low = masters[5][...].astype(BF).astype(F32)
    g_gains[0:1, :] = row_of(gain_one) / gain_low[0:1]
    g_gains[1:2, :] = row_of(gain_two) / gain_low[1:2]
    grad = [total_of(ref[...]) for ref in (g_heads, merge, gate, up, down, g_gains)]
    row = lanes_of([sum(grad)] + [total_of(ref[...]) for ref in masters])
    sums[...] = jnp.broadcast_to(row[None], sums.shape)


def whole(ref_or_array):
    return pl.BlockSpec(memory_space=pltpu.VMEM)


def grads(masters, by_head, merge, raw, down, devices, heads, docs, waits):
    inputs = [*masters, by_head, merge, raw, down]
    return pl.pallas_call(
        functools.partial(grads_kernel, heads, docs),
        in_specs=[whole(member) for member in inputs] + waits_for(len(waits)),
        out_specs=[whole(None)] * 5,
        out_shape=[
            jax.ShapeDtypeStruct(masters[0].shape, F32),
            jax.ShapeDtypeStruct(masters[2].shape, F32),
            jax.ShapeDtypeStruct(masters[3].shape, F32),
            jax.ShapeDtypeStruct(masters[5].shape, F32),
            jax.ShapeDtypeStruct((devices, 1, LANES), F32),
        ],
        compiler_params=params(),
        cost_estimate=cheap(),
        name="grads",
    )(*inputs, *waits)


def moments_kernel(*refs):
    totals, refs = refs[0], refs[1:]
    masters, old_moments, old_squares, gradients = (refs[6 * j : 6 * j + 6] for j in range(4))
    moments, squares, directions = (refs[6 * j - 19 : 6 * j - 13] for j in range(3))
    sums = refs[-1]
    total = jnp.sum(totals[...], axis=0)
    factor = CLIP / jnp.maximum(jnp.sqrt(total[:, 0:1]), CLIP)
    fix_one = 1.0 - BETA_ONE**STEP
    fix_two = 1.0 - BETA_TWO**STEP
    norms = []
    for place in range(6):
        clipped = factor * gradients[place][...]
        moment = BETA_ONE * old_moments[place][...] + (1.0 - BETA_ONE) * clipped
        square = BETA_TWO * old_squares[place][...] + (1.0 - BETA_TWO) * clipped * clipped
        direction = moment / fix_one / (jnp.sqrt(square / fix_two) + ADAM_EPS)
        if place < 5:
            direction = direction + DECAY * masters[place][...]
        moments[place][...] = moment
        squares[place][...] = square
        directions[place][...] = direction
        norms.append(total_of(direction))
    sums[...] = jnp.broadcast_to(lanes_of(norms)[None], sums.shape)


def step_moments(totals, masters, moments, squares, gradients, waits):
    inputs = [totals, *masters, *moments, *squares, *gradients]
    shapes = [jax.ShapeDtypeStruct(member.shape, F32) for member in masters]
    out = pl.pallas_call(
        moments_kernel,
        in_specs=[whole(member) for member in inputs] + waits_for(len(waits)),
        out_specs=[whole(None)] * 19,
        out_shape=shapes * 3 + [jax.ShapeDtypeStruct(totals.shape, F32)],
        compiler_params=params(),
        cost_estimate=cheap(),
        name="moments",
    )(*inputs, *waits)
    return out[:6], out[6:12], out[12:18], out[18]


def weights_kernel(*refs):
    totals, updates, refs = refs[0], refs[1], refs[2:]
    masters, directions, fresh = refs[:6], refs[6:12], refs[-8:-2]
    norms, clip = refs[-2:]
    old = jnp.sqrt(jnp.sum(totals[...], axis=0))
    new = jnp.sqrt(jnp.sum(updates[...], axis=0))
    for place in range(6):
        trust = old[:, place + 1 : place + 2] / new[:, place : place + 1]
        fresh[place][...] = masters[place][...] - RATE * trust * directions[place][...]
    norms[0:1, :] = pltpu.roll(old, LANES - 1, 1)
    norms[1:2, :] = new
    clip[...] = old


def step_weights(totals, updates, masters, directions, waits):
    inputs = [totals, updates, *masters, *directions]
    shapes = [jax.ShapeDtypeStruct(member.shape, F32) for member in masters]
    out = pl.pallas_call(
        weights_kernel,
        in_specs=[whole(member) for member in inputs] + waits_for(len(waits)),
        out_specs=[whole(None)] * 8,
        out_shape=shapes
        + [jax.ShapeDtypeStruct((2, LANES), F32), jax.ShapeDtypeStruct((1, LANES), F32)],
        compiler_params=params(),
        cost_estimate=cheap(),
        name="weights",
    )(*inputs, *waits)
    return out[:6], out[6][:, :6], out[7][0, 0]


def norm_rows(values):
    row_scale = lax.rsqrt(jnp.mean(values * values, axis=-1, keepdims=True) + NORM_EPS)
    return (values * row_scale, row_scale)


def norm_back(grad_normed, unit_rows, row_scale, gain_row):
    weighted = grad_normed * gain_row
    inner = jnp.mean(weighted * unit_rows, axis=-1, keepdims=True)
    return row_scale * (weighted - unit_rows * inner)


def rotation(length):
    half = HEAD_DIM // 2
    frequency = jnp.exp(-jnp.log(10000.0) * jnp.arange(half, dtype=F32) / half)
    grid = jnp.arange(length, dtype=F32)[:, None] * frequency[None, :]
    cos, sin = jnp.cos(grid), jnp.sin(grid)
    return jnp.concatenate([cos, cos], 1), jnp.concatenate([-sin, sin], 1)


def shards(
    tokens, cotangent, cache_keys, cache_values, neighbours, partner, has_memory,
    w_heads, moment_heads, square_heads, w_merge, moment_merge, square_merge,
    w_gate, moment_gate, square_gate, w_up, moment_up, square_up,
    w_down, moment_down, square_down, gains, moment_gains, square_gains,
):
    _, rows, width = tokens.shape
    seq_count = lax.axis_size("seq")
    docs_count = lax.axis_size("docs")
    devices = seq_count * docs_count
    seq_index = lax.axis_index("seq")
    doc_index = lax.axis_index("docs")
    here = jnp.stack([seq_index, doc_index]).astype(jnp.int32)
    length = rows * seq_count
    heads = HEADS // seq_count
    cols = heads * HEAD_DIM
    weight_rows = w_heads.shape[0]
    down_rows = w_down.shape[0]
    group = -(-down_rows // 16) * 16
    hidden = group * docs_count
    per_device = cache_keys.shape[1]
    masters = (w_heads, w_merge, w_gate, w_up, w_down, gains)
    moments = (moment_heads, moment_merge, moment_gate, moment_up, moment_down, moment_gains)
    squares = (square_heads, square_merge, square_gate, square_up, square_down, square_gains)

    low_heads = w_heads.astype(BF).reshape(weight_rows, 3, seq_count, heads, HEAD_DIM)
    low_heads = low_heads.transpose(2, 0, 3, 1, 4).reshape(seq_count, weight_rows, 3 * cols)
    gain_cols = jnp.pad(gains.astype(BF).T, ((0, 0), (0, LANES - 2)))
    first_block = stack(
        swap(
            lambda j: jnp.concatenate(
                [lax.dynamic_index_in_dim(low_heads, j, 0, False), gain_cols], axis=1
            )
        ),
        "seq",
    )
    merge_cols = width // seq_count
    low_merge = w_merge.astype(BF).reshape(weight_rows, seq_count, merge_cols).transpose(1, 0, 2)
    low_merge = low_merge.reshape(seq_count * weight_rows, merge_cols)
    first = pieces_of(jnp.concatenate([first_block, low_merge], axis=1), "docs")


    def columns(member):
        split = member.astype(BF).reshape(weight_rows, docs_count, seq_count, down_rows)
        split = jnp.pad(split.transpose(2, 0, 1, 3), ((0, 0), (0, 0), (0, 0), (0, group - down_rows)))
        return split.reshape(seq_count, weight_rows, hidden)

    low_raw = after(jnp.concatenate([columns(w_gate), columns(w_up)], axis=2), first_block)
    low_raw = stack(swap(lambda j: lax.dynamic_index_in_dim(low_raw, j, 0, False)), "seq")
    packed = pack_inner(low_raw, w_down, group, min(512, width))
    packed = pieces_of(packed, "docs")

    near = jnp.concatenate([neighbours[0] // 64, neighbours[0] % 64], axis=1).astype(BF)
    x_near = pieces_of(after(jnp.concatenate([tokens[0], near], axis=1), low_raw), "seq")
    flag = jnp.take(has_memory, doc_index[None])
    grad_low = pieces_of(after(cotangent[0], x_near[2 if seq_count > 2 else -1]), "seq")
    low_merge = stack([piece[:, 3 * cols + LANES :] for piece in first], "docs")
    low_merge = low_merge.reshape(docs_count, seq_count, weight_rows, merge_cols)
    low_merge = low_merge.transpose(0, 2, 1, 3).reshape(docs_count, weight_rows, width)
    low_merge = pieces_of(low_merge, "seq")
    merge_full = jnp.stack([pick(low_merge, "seq", j) for j in range(seq_count)], axis=1)
    merge_full = merge_full.reshape(width, width)

    waits = (*first[1:], *packed[1:5], *packed[6:7], *x_near[1:], *grad_low[1:], *low_merge[1:])
    grad_low = lay_out(here, grad_low)
    gated, memory = [], []
    for member in pack_memory(partner, cache_keys, cache_values, heads, seq_count):
        gated.append(gate(member.reshape(devices, 2, per_device, 2 * HEAD_DIM), *waits))
        member = lax.all_to_all(
            gated[-1], ("docs", "seq"), split_axis=0, concat_axis=0, tiled=True
        )
        memory.append(member.reshape(devices * 2 * per_device, 2 * HEAD_DIM))
        waits = (memory[0], *packed[5:])
    cosine, sine = rotation(length)
    (
        x_low, normed_one, query_local, query_memory, key_local, value_local, words, heads_here, gain_rows,
    ) = project(here, x_near, first, cosine, sine, heads, per_device * devices, per_device,
      gated[:1])
    local, high, total = attend_local(query_local, key_local, value_local, heads)


    attended, blended, lse = [], [], []
    for h in range(heads):
        result = attend_memory(
            flag, query_memory, words, memory[h], local, high, total, h, (grad_low, merge_full)
        )
        attended.append(result[0])
        blended.append(pieces_of(result[1], "seq"))
        lse.append(result[2])

    blended, normed_two, active, grad_raw, back, middle, _, down_here = feed_forward(
        here, [piece for pieces in zip(*blended) for piece in pieces], packed,
        x_low, merge_full, gain_rows, grad_low, heads, hidden,
    )
    grad_normed_two = halve(back.reshape(seq_count, rows, width), "seq", 0)
    bits = docs_count.bit_length() - 1
    g_gate, g_up = (
        dot_tn(normed_two, grad_raw[:, j * hidden : (j + 1) * hidden]).astype(BF) for j in range(2)
    )
    g_down = dot_tn(active, grad_low).astype(BF).reshape(docs_count, group, width)
    grad_normed_two = reduce_over(grad_normed_two, "seq", 1)
    unit_two, scale_two = norm_rows(middle)
    grad_middle = cotangent[0].astype(F32) + norm_back(
        grad_normed_two, unit_two, scale_two, gain_rows[1:2]
    )
    grad_branch = grad_middle.astype(BF)
    grad_mine = dot_nt(grad_branch, merge_full).astype(BF)
    grad_attended = stack(swap(lambda j: lax.dynamic_slice_in_dim(grad_mine, j * cols, cols, 1)), "seq")

    down_out = dot(active, down_here).astype(BF).reshape(seq_count, rows, width)
    down_out = halve(down_out, "seq", 0)
    waits = (g_gate, g_up, g_down, down_out)
    g_gate = g_gate.reshape(docs_count, width // docs_count, hidden)
    g_gate = halve(g_gate, "docs", 0, token(grad_attended))
    g_up = g_up.reshape(docs_count, width // docs_count, hidden)
    branches = pieces_of(gate(grad_branch, grad_attended), "seq")

    projected, by_head = [], []
    for h in range(heads):
        projected.append(
            attend_back(
                flag, query_local, query_memory, key_local, value_local, words,
                memory[h], attended[h], grad_attended, lse[h], cosine, sine, h, waits,
            )
        )
        g_heads = dot_tn(normed_one, projected[h]).astype(BF)
        by_head.append(g_heads.reshape(docs_count, width // docs_count, 3 * HEAD_DIM))
        if h == 0:
            halfway = token(projected[0])
            down_out = gate(down_out, projected[0])
            g_gate = halve(g_gate, "docs", 1, halfway)
            g_up = halve(g_up, "docs", 0, halfway)
            g_down = halve(g_down, "docs", 0, halfway)
            waits = (g_heads, g_gate, g_up, g_down, *branches[1:])
    last = token(projected[-1])
    down_out = reduce_over(down_out, "seq", 1, last)
    activations = (middle + down_out).astype(BF)[None]
    by_head = [halve(member, "docs", 0, last) for member in by_head]
    begun = token(by_head[-1])
    g_gate = halve(g_gate, "docs", 2, begun) if bits > 2 else g_gate
    g_gate = reduce_over(g_gate, "docs", 3)
    g_up = reduce_over(halve(g_up, "docs", 1, last), "docs", 2, begun)
    g_down = reduce_over(halve(g_down, "docs", 1, last), "docs", 2, begun)[:down_rows]
    g_raw = jnp.concatenate([g_gate, g_up], axis=1)
    g_merge = (dot_tn(blended, stack(branches, "seq")) + begun).astype(BF)
    g_merge = g_merge.reshape(docs_count, seq_count, weight_rows, width)
    g_merge = lax.dynamic_index_in_dim(g_merge, seq_index, 1, False)
    by_head = jnp.concatenate(by_head, axis=2)
    g_merge = reduce_over(g_merge, "docs")
    def own_rows(member):
        member = member.astype(BF).reshape(seq_count, weight_rows, member.shape[1])
        return swap(lambda j: lax.dynamic_index_in_dim(member, j, 0, False))

    g_raw = stack(own_rows(g_raw), "seq")
    by_head = stack(own_rows(reduce_over(by_head, "docs", 1)), "seq", 1)
    grad_projected = jnp.concatenate(projected, axis=1)
    grad_normed_one = (dot_nt(grad_projected, heads_here) + begun).astype(BF)
    grad_normed_one = halve(grad_normed_one.reshape(seq_count, rows, width), "seq", 0)
    waits = (grad_normed_one, activations)
    grad_normed_one = reduce_over(grad_normed_one, "seq", 1)
    unit_one, scale_one = norm_rows(tokens[0].astype(F32))
    input_grad = grad_middle + norm_back(grad_normed_one, unit_one, scale_one, gain_rows[0:1])
    input_grad = input_grad[None]

    g_heads, g_gate, g_up, g_gains, totals = grads(
        masters, by_head, g_merge, g_raw, g_down, devices, heads, docs_count, waits
    )
    gradients = (g_heads, g_merge, g_gate, g_up, g_down, g_gains)
    totals = to_everyone(totals)
    new_moments, new_squares, directions, updates = step_moments(
        totals, masters, moments, squares, gradients, ()
    )
    new_weights, layer_norms, clip_norm = step_weights(
        totals, to_everyone(updates), masters, directions, (input_grad,)
    )
    results = [activations, input_grad]
    for place in range(6):
        results += [new_moments[place], new_squares[place], new_weights[place]]
    return (*results, clip_norm, layer_norms)


def solution(mesh):
    by_token = P("docs", "seq", None)
    by_slot = P(None, ("docs", "seq"), None)
    by_row = P(("docs", "seq"), None)
    by_gain = P(None, ("docs", "seq"))
    return jax.shard_map(
        shards,
        mesh=mesh,
        in_specs=(by_token, by_token, by_slot, by_slot, by_token, P(), P())
        + (by_row,) * 15
        + (by_gain,) * 3,
        out_specs=(by_token, by_token) + (by_row,) * 15 + (by_gain,) * 3 + (P(), P()),
        check_vma=False,
    )
```

time: 657 us -> 461 us (0.70)
  local copies, waits for them, and re-layouts: 110 us -> 32 us
  waiting for transfers between devices: 233 us -> 163 us
  Pallas kernels: 67.1 us -> 128 us
  other arithmetic: 90.1 us -> 30.2 us
  matrix products: 38.3 us -> 17.8 us
  between operations: 25.9 us -> 8.16 us
  starting transfers between devices: 82.3 us -> 75.6 us
    pallas_call x3 -> x17, Pallas kernels: 67.1 us -> 128 us  [the longest x2 32.6 us: attend_back(): pl.pallas_call(functools.partial(attend_back_kernel, min(1024, keys), len...]
    reduce_scatter x3 -> x0, waiting for transfers between devices: 54.1 us -> none  [the longest x1 54.1 us: shards(): g_raw = lax.psum_scatter(g_raw, 'docs', scatter_dimension=0, tiled=True)]
    dynamic_update_slice x43 -> x0, local copies, waits for them, and re-layouts: 30.5 us -> none  [the longest x25 16.9 us: put(): return lax.dynamic_update_slice(buffer, block, starts)]
    ppermute x68 -> x69, waiting for transfers between devices: 178 us -> 149 us  [send(): lax.ppermute(x, axis, [(i, i ^ bits) for i in range(lax.axis_size(axis))])]
    another operation x5 -> x7, other arithmetic: 24.7 us -> 2.01 us  [the longest x1 0.67 us: reduce_over(): return blocks[0]]
    reduce_sum x17 -> x0, other arithmetic: 21.6 us -> none  [the longest x6 9.44 us: shards(): jnp.sum(member * member)]
    ppermute x68 -> x69, starting transfers between devices: 78 us -> 60 us  [send(): lax.ppermute(x, axis, [(i, i ^ bits) for i in range(lax.axis_size(axis))])]
    transpose x3 -> x0, local copies, waits for them, and re-layouts: 13.6 us -> none  [the longest x1 7.48 us: shards(): pair.transpose(0, 3, 1, 2, 4).reshape(devices, 2 * per_device, 2 * cols)]
  transfers between devices with their start and end apart: 72 -> 73, of which waited for: 35 -> 32; matrix products, arithmetic and copies ran while one was open for 27% -> 14% of each run, Pallas kernels for 10% -> 23%
where the time goes in v2:
time: 461 us; the launch traced here: 455 us
  waiting for transfers between devices  163 us (35%)
  Pallas kernels  128 us (28%)
  starting transfers between devices  75.6 us (16%)
  local copies, waits for them, and re-layouts  32 us (7%)
  other arithmetic  30.2 us (7%)
  matrix products  17.8 us (4%)
  between operations  8.16 us (2%)
    ppermute x69, waiting for transfers between devices, send(): lax.ppermute(x, axis, [(i, i ^ bits) for i in range(lax.axis_size(axis))])  149 us
    ppermute x69, starting transfers between devices, send(): lax.ppermute(x, axis, [(i, i ^ bits) for i in range(lax.axis_size(axis))])  60 us
    pallas_call x2, Pallas kernels, attend_back(): pl.pallas_call(functools.partial(attend_back_kernel, min(1024, keys), len...  32.6 us
    pallas_call x2, Pallas kernels, attend_memory(): pl.pallas_call(functools.partial(attend_memory_kernel, min(1024, keys)),...  26.9 us
    pallas_call x1, Pallas kernels, feed_forward(): pl.pallas_call(functools.partial(feed_forward_kernel, heads, seq, docs),...  21.6 us
    pallas_call x1, Pallas kernels, project(): pl.pallas_call(functools.partial(project_kernel, heads, len(tokens), len(...  13.6 us
    dot_general x6, matrix products, dot_tn(): lax.dot_general(a, b, (((0,), (0,)), ((), ())), preferred_element_type=F32)  13.4 us
    all_to_all x2, waiting for transfers between devices, to_everyone(): lax.all_to_all(vectors, ('docs', 'seq'), split_axis=0, concat_axis=0, til...  11.6 us
  transfers between devices with their start and end apart: 73, of which 32 were waited for; matrix products, arithmetic and copies ran while one was open for 14% of the time, Pallas kernels for 23%

profile of v2, /device:TPU:0, one launch (start us, length us, event | category | flops | bytes accessed | tf_op | source)
XLA Modules:
  0.0 454.8 jit_solution(13836523282186275005)
XLA Ops:
  23.1 7.7 %collective-permute-done.12.refs_4_.refs_8_ = bf16[128,1152]{1,0:T(8,128)(2,1)S(1)} collective-permute-done((bf16[128,1152]{1,0:T(8,128)(2,1)}, bf16[128,1152]{1,0:T(8,128)(2,1)S(1)}, u32[]{:S(2)}, u32[]{:S(2)}) %collective-permute-start.12) | collective-permute-done | bytes 294944 | tf_op jit(solution)/shard_map/ppermute | solution.py:30
  38.4 4.8 %collective-permute-done.14.refs_6_.refs_10_ = bf16[128,1152]{1,0:T(8,128)(2,1)S(1)} collective-permute-done((bf16[128,1152]{1,0:T(8,128)(2,1)S(1)}, bf16[128,1152]{1,0:T(8,128)(2,1)S(1)}, u32[]{:S(2)}, u32[]{:S(2)}) %collective-permute-start.14) | collective-permute-done | bytes 294944 | tf_op jit(solution)/shard_map/ppermute | solution.py:30
  53.6 4.8 %collective-permute-done.13.refs_5_.refs_9_ = bf16[128,1152]{1,0:T(8,128)(2,1)S(1)} collective-permute-done((bf16[128,1152]{1,0:T(8,128)(2,1)S(1)}, bf16[128,1152]{1,0:T(8,128)(2,1)S(1)}, u32[]{:S(2)}, u32[]{:S(2)}) %collective-permute-start.13) | collective-permute-done | bytes 294944 | tf_op jit(solution)/shard_map/ppermute | solution.py:30
  67.0 7.8 %collective-permute-done.19.refs_11_.refs_12_ = bf16[576,512]{1,0:T(8,128)(2,1)S(1)} collective-permute-done((bf16[576,512]{1,0:T(8,128)(2,1)}, bf16[576,512]{1,0:T(8,128)(2,1)S(1)}, u32[]{:S(2)}, u32[]{:S(2)}) %collective-permute-start.19) | collective-permute-done | bytes 589856 | tf_op jit(solution)/shard_map/ppermute | solution.py:30
  80.3 7.5 %collective-permute-done.18.refs_10_.refs_11_ = bf16[576,512]{1,0:T(8,128)(2,1)S(1)} collective-permute-done((bf16[576,512]{1,0:T(8,128)(2,1)}, bf16[576,512]{1,0:T(8,128)(2,1)S(1)}, u32[]{:S(2)}, u32[]{:S(2)}) %collective-permute-start.18) | collective-permute-done | bytes 589856 | tf_op jit(solution)/shard_map/ppermute | solution.py:30
  89.3 7.7 %pack_memory.1 = (bf16[8,4,2,64,256]{4,3,2,1,0:T(8,128)(2,1)}, bf16[8,4,2,64,256]{4,3,2,1,0:T(8,128)(2,1)}) custom-call(s32[8]{0:T(128)} %partner.1, bf16[8,64,1024]{2,1,0:T(8,128)(2,1)} %mate_key.1, bf16[8,64,1024]{2,1,0:T(8,128)(2,1)} %mate_value.1, bf16[8,64,1024]{2,1,0:T(8,128)(2,1)} %mate_key.1, bf16[8,64,1024]{2,1,0:T(8,128)(2,1)} %mate_value.1), custom_call_target="tpu_custom_call" | custom-call | flops 1 | bytes 1 | tf_op jit(solution)/shard_map/pack_memory/pallas_call | solution.py:154
  98.6 5.9 %all-to-all-start = ((bf16[32,2,64,256]{3,2,1,0:T(8,128)(2,1)}), bf16[32,2,64,256]{3,2,1,0:T(8,128)(2,1)S(1)}, u32[]{:S(2)}, u32[]{:S(2)}) async-start(bf16[32,2,64,256]{3,2,1,0:T(8,128)(2,1)} %gate.4.refs_14_), calls=%async_computation | async-start | bytes 4194304 | tf_op jit(solution)/shard_map/all_to_all | solution.py:881
  106.7 33.8 %collective-permute-done.27.refs_2_.refs_13_ = bf16[576,512]{1,0:T(8,128)(2,1)S(1)} collective-permute-done((bf16[576,512]{1,0:T(8,128)(2,1)}, bf16[576,512]{1,0:T(8,128)(2,1)S(1)}, u32[]{:S(2)}, u32[]{:S(2)}) %collective-permute-start.27) | collective-permute-done | bytes 589856 | tf_op jit(solution)/shard_map/ppermute | solution.py:30
  141.3 14.3 %collective-permute-done.28.refs_4_.refs_15_ = bf16[576,512]{1,0:T(8,128)(2,1)} collective-permute-done((bf16[576,512]{1,0:T(8,128)(2,1)S(1)}, bf16[576,512]{1,0:T(8,128)(2,1)}, u32[]{:S(2)}, u32[]{:S(2)}) %collective-permute-start.28) | collective-permute-done | bytes 589856 | tf_op jit(solution)/shard_map/ppermute | solution.py:30
  156.8 4.6 %all-to-all-start.1 = ((bf16[32,2,64,256]{3,2,1,0:T(8,128)(2,1)}), bf16[32,2,64,256]{3,2,1,0:T(8,128)(2,1)S(1)}, u32[]{:S(2)}, u32[]{:S(2)}) async-start(bf16[32,2,64,256]{3,2,1,0:T(8,128)(2,1)} %gate.5), calls=%async_computation.1 | async-start | bytes 4194304 | tf_op jit(solution)/shard_map/all_to_all | solution.py:881
  170.7 13.6 %project.1 = (bf16[1024,1024]{1,0:T(8,128)(2,1)}, bf16[1024,1024]{1,0:T(8,128)(2,1)}, bf16[1024,256]{1,0:T(8,128)(2,1)}, bf16[1024,256]{1,0:T(8,128)(2,1)}, bf16...) custom-call(s32[2]{0:T(128)} %pad_add_fusion.here, ...), custom_call_target="tpu_custom_call" | custom-call | flops 1 | bytes 1 | tf_op jit(solution)/shard_map/project/pallas_call | solution.py:304
  184.3 6.5 %attend_local.1 = (f32[1024,256]{1,0:T(8,128)}, f32[1024,256]{1,0:T(8,128)}, f32[1024,256]{1,0:T(8,128)}) custom-call(bf16[1024,256]{1,0:T(8,128)(2,1)} %get-tuple-element.84.ql, bf16[1024,256]{1,0:T(8,128)(2,1)} %get-tuple-element.85.kl, bf16[1024,256]{1,0:T(8,128)(2,1)} %get-tuple-element.86.vl), custom_call_target="tpu_custom_call" | custom-call | flops 1 | bytes 1 | tf_op jit(solution)/shard_map/attend_local/pallas_call | solution.py:467
  193.0 13.5 %attend_memory.2 = (f32[1024,128]{1,0:T(8,128)}, bf16[1024,128]{1,0:T(8,128)(2,1)}, f32[1024,128]{1,0:T(8,128)}) custom-call(s32[1]{0:T(128)S(6)} %select_n.968.flag, bf16[1024,256]{1,0:T(8,128)(2,1)} %get-tuple-element.82.qm, s32[1024,128]{1,0:T(8,128)} %get-tuple-element.83.words, bf16[4096,256]{1,0:T(8,128)(2,1)} %bitcast.358, ...), custom_call_target="tpu_custom_call" | custom-call | flops 1 | bytes 1 | tf_op jit(solution)/shard_map/attend_memory/pallas_call | solution.py:523
  211.5 13.5 %attend_memory.3 = (f32[1024,128]{1,0:T(8,128)}, bf16[1024,128]{1,0:T(8,128)(2,1)}, f32[1024,128]{1,0:T(8,128)}) custom-call(s32[1]{0:T(128)S(6)} %select_n.968.flag, bf16[1024,256]{1,0:T(8,128)(2,1)} %get-tuple-element.82.qm, s32[1024,128]{1,0:T(8,128)} %get-tuple-element.83.words, bf16[4096,256]{1,0:T(8,128)(2,1)} %bitcast.365, ...), custom_call_target="tpu_custom_call" | custom-call | flops 1 | bytes 1 | tf_op jit(solution)/shard_map/attend_memory/pallas_call | solution.py:523
  227.0 6.0 %collective-permute-done.32.refs_5_ = bf16[1024,128]{1,0:T(8,128)(2,1)S(1)} collective-permute-done((bf16[1024,128]{1,0:T(8,128)(2,1)}, bf16[1024,128]{1,0:T(8,128)(2,1)S(1)}, u32[]{:S(2)}, u32[]{:S(2)}) %collective-permute-start.32) | collective-permute-done | bytes 262176 | tf_op jit(solution)/shard_map/ppermute | solution.py:30
  235.3 21.6 %feed_forward.1 = (bf16[1024,1024]{1,0:T(8,128)(2,1)}, bf16[1024,1024]{1,0:T(8,128)(2,1)}, bf16[1024,768]{1,0:T(8,128)(2,1)}, bf16[1024,1536]{1,0:T(8,128)(2,1)}...) custom-call(s32[2]{0:T(128)} %pad_add_fusion.here, ...), custom_call_target="tpu_custom_call" | custom-call | flops 1 | bytes 1 | tf_op jit(solution)/shard_map/feed_forward/pallas_call | solution.py:381
  274.9 8.4 %collective-permute-done.37 = bf16[1,1,256,1024]{3,2,1,0:T(8,128)(2,1)S(1)} collective-permute-done((bf16[1,1,256,1024]{3,2,1,0:T(8,128)(2,1)S(1)}, bf16[1,1,256,1024]{3,2,1,0:T(8,128)(2,1)S(1)}, u32[]{:S(2)}, u32[]{:S(2)}) %collective-permute-start.37) | collective-permute-done | bytes 524320 | tf_op jit(solution)/shard_map/ppermute | solution.py:30
  304.2 16.3 %attend_back.2.refs_1_ = bf16[1024,384]{1,0:T(8,128)(2,1)} custom-call(s32[1]{0:T(128)S(6)} %select_n.968.flag, bf16[1024,256]{1,0:T(8,128)(2,1)} %get-tuple-element.84.ql, bf16[1024,256]{1,0:T(8,128)(2,1)} %get-tuple-element.82.qm, bf16[1024,256]{1,0:T(8,128)(2,1)} %get-tuple-element.85.kl, bf16[1024,256]{1,0:T(8,128)(2,1)} %get-tuple-element.86.vl, ...), custom_call_target="tpu_custom_call" | custom-call | flops 1 | bytes 1 | tf_op jit(solution)/shard_map/attend_back/pallas_call | solution.py:612
  338.3 16.3 %attend_back.3 = bf16[1024,384]{1,0:T(8,128)(2,1)} custom-call(s32[1]{0:T(128)S(6)} %select_n.968.flag, bf16[1024,256]{1,0:T(8,128)(2,1)} %get-tuple-element.84.ql, bf16[1024,256]{1,0:T(8,128)(2,1)} %get-tuple-element.82.qm, bf16[1024,256]{1,0:T(8,128)(2,1)} %get-tuple-element.85.kl, bf16[1024,256]{1,0:T(8,128)(2,1)} %get-tuple-element.86.vl, ...), custom_call_target="tpu_custom_call" | custom-call | flops 1 | bytes 1 | tf_op jit(solution)/shard_map/attend_back/pallas_call | solution.py:612
  372.5 7.9 %collective-permute-done.63 = bf16[1,1,128,768]{3,2,0,1:T(8,128)(2,1)S(1)} collective-permute-done((bf16[1,1,128,768]{3,2,0,1:T(8,128)(2,1)S(1)}, bf16[1,1,128,768]{3,2,0,1:T(8,128)(2,1)S(1)}, u32[]{:S(2)}, u32[]{:S(2)}) %collective-permute-start.63) | collective-permute-done | bytes 196640 | tf_op jit(solution)/shard_map/ppermute | solution.py:30
  393.5 7.0 %collective-permute-done.53 = bf16[2,1,128,768]{3,2,1,0:T(8,128)(2,1)S(1)} collective-permute-done((bf16[2,1,128,768]{3,2,1,0:T(8,128)(2,1)S(1)}, bf16[2,1,128,768]{3,2,1,0:T(8,128)(2,1)S(1)}, u32[]{:S(2)}, u32[]{:S(2)}) %collective-permute-start.53) | collective-permute-done | bytes 393248 | tf_op jit(solution)/shard_map/ppermute | solution.py:30
  403.7 8.6 %collective-permute-done.54 = bf16[1,1,128,768]{3,2,1,0:T(8,128)(2,1)S(1)} collective-permute-done((bf16[1,1,128,768]{3,2,1,0:T(8,128)(2,1)S(1)}, bf16[1,1,128,768]{3,2,1,0:T(8,128)(2,1)S(1)}, u32[]{:S(2)}, u32[]{:S(2)}) %collective-permute-start.54) | collective-permute-done | bytes 196640 | tf_op jit(solution)/shard_map/ppermute | solution.py:30
  426.3 7.1 %all-to-all-done.2.refs_0_ = f32[32,1,128]{2,1,0:T(1,128)S(1)} async-done(((f32[32,1,128]{2,1,0:T(1,128)}), f32[32,1,128]{2,1,0:T(1,128)S(1)}, u32[]{:S(2)}, u32[]{:S(2)}) %all-to-all-start.2) | async-done | bytes 16416 | tf_op jit(solution)/shard_map/all_to_all | solution.py:88
  434.0 6.7 %moments.1 = (f32[32,3072]{1,0:T(8,128)}, f32[32,1024]{1,0:T(8,128)}, f32[32,2816]{1,0:T(8,128)}, f32[32,2816]{1,0:T(8,128)}, f32[88,1024]{1,0:T(8,128)}, /*inde...) custom-call(f32[32,1,128]{2,1,0:T(1,128)} %copy-done.70, ...), custom_call_target="tpu_custom_call" | custom-call | flops 1 | bytes 1 | tf_op jit(solution)/shard_map/moments/pallas_call | solution.py:752
  (433 shorter events, 194.7 us)
Async XLA Ops:
  20.0 24.7 %collective-permute-start.7 = (bf16[256,1152]{1,0:T(8,128)(2,1)S(1)}, bf16[256,1152]{1,0:T(8,128)(2,1)}, u32[]{:S(2)}, u32[]{:S(2)}) collective-permute-start(bf16[256,1152]{1,0:T(8,128)(2,1)S(1)} %broadcast_add_fusion.refs_0_), channel_id=1, source_target_pairs={{0,2},{1,3},{2,0},{3,1},{4,6},{5,7},{6,4},{7,5},{8,10},{9,11},{10,... | collective-permute-start | bytes 1769480 | tf_op jit(solution)/shard_map/ppermute | solution.py:30
  34.3 24.9 %collective-permute-start.17 = (bf16[576,512]{1,0:T(8,128)(2,1)}, bf16[576,512]{1,0:T(8,128)(2,1)}, u32[]{:S(2)}, u32[]{:S(2)}) collective-permute-start(bf16[576,512]{1,0:T(8,128)(2,1)} %pack_inner.1.refs_8_), channel_id=1, source_target_pairs={{0,8},{4,12},{8,0},{12,4},{16,24},{20,28},{24,16},{28,20},{1,9},{5... | collective-permute-start | bytes 1769480 | tf_op jit(solution)/shard_map/ppermute | solution.py:30
  48.2 26.6 %collective-permute-start.19 = (bf16[576,512]{1,0:T(8,128)(2,1)}, bf16[576,512]{1,0:T(8,128)(2,1)S(1)}, u32[]{:S(2)}, u32[]{:S(2)}) collective-permute-start(bf16[576,512]{1,0:T(8,128)(2,1)} %pack_inner.1.refs_8_), channel_id=1, source_target_pairs={{0,16},{4,20},{8,24},{12,28},{16,0},{20,4},{24,8},{28,12},{1,17},{... | collective-permute-start | bytes 1769480 | tf_op jit(solution)/shard_map/ppermute | solution.py:30
  52.1 25.3 %collective-permute-start.16 = (bf16[576,512]{1,0:T(8,128)(2,1)}, bf16[576,512]{1,0:T(8,128)(2,1)S(1)}, u32[]{:S(2)}, u32[]{:S(2)}) collective-permute-start(bf16[576,512]{1,0:T(8,128)(2,1)} %pack_inner.1.refs_8_), channel_id=1, source_target_pairs={{0,4},{4,0},{8,12},{12,8},{16,20},{20,16},{24,28},{28,24},{1,5},{5... | collective-permute-start | bytes 1769480 | tf_op jit(solution)/shard_map/ppermute | solution.py:30
  58.4 20.6 %collective-permute-start.6 = (bf16[256,1152]{1,0:T(8,128)(2,1)}, bf16[256,1152]{1,0:T(8,128)(2,1)S(1)}, u32[]{:S(2)}, u32[]{:S(2)}) collective-permute-start(bf16[256,1152]{1,0:T(8,128)(2,1)} %copy-done.46), channel_id=1, source_target_pairs={{0,1},{1,0},{2,3},{3,2},{4,5},{5,4},{6,7},{7,6},{8,9},{9,8},{10,11... | collective-permute-start | bytes 1769480 | tf_op jit(solution)/shard_map/ppermute | solution.py:30
  64.7 23.0 %collective-permute-start.18 = (bf16[576,512]{1,0:T(8,128)(2,1)}, bf16[576,512]{1,0:T(8,128)(2,1)S(1)}, u32[]{:S(2)}, u32[]{:S(2)}) collective-permute-start(bf16[576,512]{1,0:T(8,128)(2,1)} %collective-permute-done.17.refs_9_.refs_10_), channel_id=1, source_target_pairs={{0,4},{4,0},{8,12},{12,8},{16,20},{20,16},{24,28},{28,24},{1,5},{5... | collective-permute-start | bytes 1769480 | tf_op jit(solution)/shard_map/ppermute | solution.py:30
  98.6 56.9 %all-to-all-start = ((bf16[32,2,64,256]{3,2,1,0:T(8,128)(2,1)}), bf16[32,2,64,256]{3,2,1,0:T(8,128)(2,1)S(1)}, u32[]{:S(2)}, u32[]{:S(2)}) async-start(bf16[32,2,64,256]{3,2,1,0:T(8,128)(2,1)} %gate.4.refs_14_), calls=%async_computation | async-start | bytes 4194304 | tf_op jit(solution)/shard_map/all_to_all | solution.py:881
  104.6 35.9 %collective-permute-start.27 = (bf16[576,512]{1,0:T(8,128)(2,1)}, bf16[576,512]{1,0:T(8,128)(2,1)S(1)}, u32[]{:S(2)}, u32[]{:S(2)}) collective-permute-start(bf16[576,512]{1,0:T(8,128)(2,1)} %copy-done.40), channel_id=1, source_target_pairs={{0,4},{4,0},{8,12},{12,8},{16,20},{20,16},{24,28},{28,24},{1,5},{5... | collective-permute-start | bytes 1769480 | tf_op jit(solution)/shard_map/ppermute | solution.py:30
  106.4 49.1 %collective-permute-start.28 = (bf16[576,512]{1,0:T(8,128)(2,1)S(1)}, bf16[576,512]{1,0:T(8,128)(2,1)}, u32[]{:S(2)}, u32[]{:S(2)}) collective-permute-start(bf16[576,512]{1,0:T(8,128)(2,1)S(1)} %copy-done.24), channel_id=1, source_target_pairs={{0,4},{4,0},{8,12},{12,8},{16,20},{20,16},{24,28},{28,24},{1,5},{5... | collective-permute-start | bytes 1769480 | tf_op jit(solution)/shard_map/ppermute | solution.py:30
  156.8 53.3 %all-to-all-start.1 = ((bf16[32,2,64,256]{3,2,1,0:T(8,128)(2,1)}), bf16[32,2,64,256]{3,2,1,0:T(8,128)(2,1)S(1)}, u32[]{:S(2)}, u32[]{:S(2)}) async-start(bf16[32,2,64,256]{3,2,1,0:T(8,128)(2,1)} %gate.5), calls=%async_computation.1 | async-start | bytes 4194304 | tf_op jit(solution)/shard_map/all_to_all | solution.py:881
  264.1 33.4 %collective-permute-start.35 = (bf16[2,1,256,1024]{3,2,0,1:T(8,128)(2,1)S(1)}, bf16[2,1,256,1024]{3,2,0,1:T(8,128)(2,1)S(1)}, u32[]{:S(2)}, u32[]{:S(2)}) collective-permute-start(bf16[2,1,256,1024]{3,2,0,1:T(8,128)(2,1)S(1)} %dynamic-slice_bitcast_fusion.2), channel_id=1, source_target_pairs={{0,1},{1,0},{2,3},{3,2},{4,5},{5,4},{6,7},{7,6},{8,9},{9,8},{10,11... | collective-permute-start | bytes 3145736 | tf_op jit(solution)/shard_map/ppermute | solution.py:30
  271.5 30.0 %collective-permute-start.41 = (bf16[4,1,128,768]{3,2,0,1:T(8,128)(2,1)}, bf16[4,1,128,768]{3,2,0,1:T(8,128)(2,1)}, u32[]{:S(2)}, u32[]{:S(2)}) collective-permute-start(bf16[4,1,128,768]{3,2,0,1:T(8,128)(2,1)} %dynamic-slice_bitcast_fusion.5), channel_id=1, source_target_pairs={{0,4},{4,0},{8,12},{12,8},{16,20},{20,16},{24,28},{28,24},{1,5},{5... | collective-permute-start | bytes 2359304 | tf_op jit(solution)/shard_map/ppermute | solution.py:30
  292.2 30.4 %collective-permute-start.44 = (bf16[4,1,96,1024]{3,2,0,1:T(8,128)(2,1)}, bf16[4,1,96,1024]{3,2,0,1:T(8,128)(2,1)}, u32[]{:S(2)}, u32[]{:S(2)}) collective-permute-start(bf16[4,1,96,1024]{3,2,0,1:T(8,128)(2,1)} %dynamic-slice_bitcast_fusion.3), channel_id=1, source_target_pairs={{0,4},{4,0},{8,12},{12,8},{16,20},{20,16},{24,28},{28,24},{1,5},{5... | collective-permute-start | bytes 2359304 | tf_op jit(solution)/shard_map/ppermute | solution.py:30
  295.1 33.9 %collective-permute-start.43 = (bf16[4,1,128,768]{3,2,0,1:T(8,128)(2,1)}, bf16[4,1,128,768]{3,2,0,1:T(8,128)(2,1)}, u32[]{:S(2)}, u32[]{:S(2)}) collective-permute-start(bf16[4,1,128,768]{3,2,0,1:T(8,128)(2,1)} %dynamic-slice_bitcast_fusion.4), channel_id=1, source_target_pairs={{0,4},{4,0},{8,12},{12,8},{16,20},{20,16},{24,28},{28,24},{1,5},{5... | collective-permute-start | bytes 2359304 | tf_op jit(solution)/shard_map/ppermute | solution.py:30
  299.2 32.0 %collective-permute-start.46 = (bf16[256,1024]{1,0:T(8,128)(2,1)}, bf16[256,1024]{1,0:T(8,128)(2,1)}, u32[]{:S(2)}, u32[]{:S(2)}) collective-permute-start(bf16[256,1024]{1,0:T(8,128)(2,1)} %gate.7), channel_id=1, source_target_pairs={{0,2},{1,3},{2,0},{3,1},{4,6},{5,7},{6,4},{7,5},{8,10},{9,11},{10,... | collective-permute-start | bytes 1572872 | tf_op jit(solution)/shard_map/ppermute | solution.py:30
  300.4 36.4 %collective-permute-start.45 = (bf16[256,1024]{1,0:T(8,128)(2,1)}, bf16[256,1024]{1,0:T(8,128)(2,1)}, u32[]{:S(2)}, u32[]{:S(2)}) collective-permute-start(bf16[256,1024]{1,0:T(8,128)(2,1)} %gate.7), channel_id=1, source_target_pairs={{0,1},{1,0},{2,3},{3,2},{4,5},{5,4},{6,7},{7,6},{8,9},{9,8},{10,11... | collective-permute-start | bytes 1572872 | tf_op jit(solution)/shard_map/ppermute | solution.py:30
  326.3 32.7 %collective-permute-start.67 = (bf16[2,1,96,1024]{3,2,1,0:T(8,128)(2,1)}, bf16[2,1,96,1024]{3,2,1,0:T(8,128)(2,1)}, u32[]{:S(2)}, u32[]{:S(2)}) collective-permute-start(bf16[2,1,96,1024]{3,2,1,0:T(8,128)(2,1)} %fusion.43), channel_id=1, source_target_pairs={{0,8},{4,12},{8,0},{12,4},{16,24},{20,28},{24,16},{28,20},{1,9},{5... | collective-permute-start | bytes 1179656 | tf_op jit(solution)/shard_map/ppermute | solution.py:30
  331.2 29.3 %collective-permute-start.62 = (bf16[2,1,128,768]{3,2,0,1:T(8,128)(2,1)}, bf16[2,1,128,768]{3,2,0,1:T(8,128)(2,1)S(1)}, u32[]{:S(2)}, u32[]{:S(2)}) collective-permute-start(bf16[2,1,128,768]{3,2,0,1:T(8,128)(2,1)} %fusion.42), channel_id=1, source_target_pairs={{0,8},{4,12},{8,0},{12,4},{16,24},{20,28},{24,16},{28,20},{1,9},{5... | collective-permute-start | bytes 1179656 | tf_op jit(solution)/shard_map/ppermute | solution.py:30
  334.8 31.7 %collective-permute-start.52 = (bf16[4,1,128,384]{3,2,0,1:T(8,128)(2,1)}, bf16[4,1,128,384]{3,2,0,1:T(8,128)(2,1)S(1)}, u32[]{:S(2)}, u32[]{:S(2)}) collective-permute-start(bf16[4,1,128,384]{3,2,0,1:T(8,128)(2,1)} %dynamic-slice_bitcast_fusion.6), channel_id=1, source_target_pairs={{0,4},{4,0},{8,12},{12,8},{16,20},{20,16},{24,28},{28,24},{1,5},{5... | collective-permute-start | bytes 1179656 | tf_op jit(solution)/shard_map/ppermute | solution.py:30
  336.8 25.6 %collective-permute-start.48 = (bf16[1,1,256,1024]{3,2,1,0:T(8,128)(2,1)S(1)}, bf16[1,1,256,1024]{3,2,1,0:T(8,128)(2,1)S(1)}, u32[]{:S(2)}, u32[]{:S(2)}) collective-permute-start(bf16[1,1,256,1024]{3,2,1,0:T(8,128)(2,1)S(1)} %fusion.37), channel_id=1, source_target_pairs={{0,2},{1,3},{2,0},{3,1},{4,6},{5,7},{6,4},{7,5},{8,10},{9,11},{10,... | collective-permute-start | bytes 1572872 | tf_op jit(solution)/shard_map/ppermute | solution.py:30
  337.8 42.7 %collective-permute-start.61 = (bf16[1,1,128,768]{3,2,0,1:T(8,128)(2,1)S(1)}, bf16[1,1,128,768]{3,2,0,1:T(8,128)(2,1)S(1)}, u32[]{:S(2)}, u32[]{:S(2)}) collective-permute-start(bf16[1,1,128,768]{3,2,0,1:T(8,128)(2,1)S(1)} %dynamic-slice_convert_fusion.5), channel_id=1, source_target_pairs={{0,16},{4,20},{8,24},{12,28},{16,0},{20,4},{24,8},{28,12},{1,17},{... | collective-permute-start | bytes 589832 | tf_op jit(solution)/shard_map/ppermute | solution.py:30
  360.3 28.1 %collective-permute-start.68 = (bf16[1,1,96,1024]{3,2,1,0:T(8,128)(2,1)S(1)}, bf16[1,1,96,1024]{3,2,1,0:T(8,128)(2,1)S(1)}, u32[]{:S(2)}, u32[]{:S(2)}) collective-permute-start(bf16[1,1,96,1024]{3,2,1,0:T(8,128)(2,1)S(1)} %dynamic-slice_convert_fusion.3), channel_id=1, source_target_pairs={{0,16},{4,20},{8,24},{12,28},{16,0},{20,4},{24,8},{28,12},{1,17},{... | collective-permute-start | bytes 589832 | tf_op jit(solution)/shard_map/ppermute | solution.py:30
  389.4 28.2 %collective-permute-start.50 = (bf16[2,1,256,1024]{3,2,1,0:T(8,128)(2,1)S(1)}, bf16[2,1,256,1024]{3,2,1,0:T(8,128)(2,1)S(1)}, u32[]{:S(2)}, u32[]{:S(2)}) collective-permute-start(bf16[2,1,256,1024]{3,2,1,0:T(8,128)(2,1)S(1)} %dynamic-slice_bitcast_fusion), channel_id=1, source_target_pairs={{0,1},{1,0},{2,3},{3,2},{4,5},{5,4},{6,7},{7,6},{8,9},{9,8},{10,11... | collective-permute-start | bytes 3145736 | tf_op jit(solution)/shard_map/ppermute | solution.py:30
  419.1 24.3 %collective-permute-start.51 = (bf16[1,1,256,1024]{3,2,1,0:T(8,128)(2,1)}, bf16[1,1,256,1024]{3,2,1,0:T(8,128)(2,1)S(1)}, u32[]{:S(2)}, u32[]{:S(2)}) collective-permute-start(bf16[1,1,256,1024]{3,2,1,0:T(8,128)(2,1)} %dynamic-slice_convert_fusion), channel_id=1, source_target_pairs={{0,2},{1,3},{2,0},{3,1},{4,6},{5,7},{6,4},{7,5},{8,10},{9,11},{10,... | collective-permute-start | bytes 1572872 | tf_op jit(solution)/shard_map/ppermute | solution.py:30
  (131 other events, 1160.4 us)

commit v3 on v2

--- a/solution.py
+++ b/solution.py
@@ -23,7 +23,6 @@
 SCALE = HEAD_DIM ** (-0.5)
 BF = jnp.bfloat16
 F32 = jnp.float32
-VMEM_LIMIT = 56 * 1024 * 1024
 
 
 def send(x, axis, bits):
@@ -100,8 +99,8 @@
     return lax.dot_general(a, b, (((0,), (0,)), ((), ())), preferred_element_type=F32)
 
 
-def params():
-    return pltpu.CompilerParams(vmem_limit_bytes=VMEM_LIMIT)
+def params(mebibytes=56):
+    return pltpu.CompilerParams(vmem_limit_bytes=mebibytes * 1024 * 1024)
 
 
 def rows_of(rows, cols):
@@ -462,7 +461,7 @@
 
 def attend_local(ql, kl, vl, heads):
     length, width = ql.shape
-    span = min(256, length)
+    span = min(512, length)
     wide = jax.ShapeDtypeStruct((length, width), F32)
     return pl.pallas_call(
         functools.partial(attend_local_kernel, heads, length // span),
@@ -518,10 +517,10 @@
 
 def attend_memory(flag, qm, words, kv, local, high, total, head, waits):
     length = qm.shape[0]
-    span = min(256, length)
+    span = min(512, length)
     keys = kv.shape[0]
     return pl.pallas_call(
-        functools.partial(attend_memory_kernel, min(1024, keys)),
+        functools.partial(attend_memory_kernel, min(4096, keys)),
         grid=(length // span,),
         in_specs=[
             pl.BlockSpec(memory_space=pltpu.SMEM),
@@ -606,11 +605,11 @@
 
 
 def attend_back(flag, ql, qm, kl, vl, words, kv, att, go, lse, cosine, sine, head, waits):
-    length = ql.shape[0]
-    span = min(256, length)
+    length, width = ql.shape
+    span = min(512, length)
     keys = kv.shape[0]
     return pl.pallas_call(
-        functools.partial(attend_back_kernel, min(1024, keys), length // span),
+        functools.partial(attend_back_kernel, min(512, keys), length // span),
         grid=(length // span,),
         in_specs=[
             pl.BlockSpec(memory_space=pltpu.SMEM),
@@ -637,7 +636,9 @@
             pltpu.VMEM((span, HEAD_DIM), F32),
         ],
         compiler_params=params(),
-        cost_estimate=cheap(),
+        cost_estimate=pl.CostEstimate(
+            flops=16 * 10**9, bytes_accessed=8 * length * width, transcendentals=length * keys
+        ),
         name="attend_back",
     )(flag, ql, qm, kl, vl, words, kv, att, go, lse, cosine, sine, cosine, sine, *waits)
 
@@ -661,28 +662,25 @@
 
 
 def grads_kernel(heads, docs, *refs):
-    masters, by_head = refs[:6], refs[6]
-    merge, raw, down = refs[7:10]
-    g_heads, gate, up, g_gains, sums = refs[-5:]
+    masters = refs[:6]
+    swapped, merge, down, g_heads, gate, up, g_gains, sums = refs[6:]
     rows = g_heads.shape[0]
     width = g_heads.shape[1] // 3
-    count = by_head.shape[1] // (3 * HEAD_DIM * heads)
-    for device in range(count):
+    seq = swapped.shape[0] // rows
+    cols = 3 * HEAD_DIM * heads
+    group, part = (swapped.shape[1] - cols) // (2 * docs), gate.shape[1] // (docs * seq)
+    for device in range(seq):
+        lines = slice(device * rows, (device + 1) * rows)
         for h in range(heads):
             for j in range(3):
-                at = (3 * (device * heads + h) + j) * HEAD_DIM
+                at = swapped.shape[1] - cols + (3 * (heads - 1 - h) + j) * HEAD_DIM
                 to = j * width + (device * heads + h) * HEAD_DIM
-                part = by_head[:, at : at + HEAD_DIM].astype(F32)
-                g_heads[:, to : to + HEAD_DIM] = part
-    seq = raw.shape[0] // rows
-    group, part = raw.shape[1] // (2 * docs), gate.shape[1] // (docs * seq)
-    for device in range(seq):
-        lines = slice(device * rows, (device + 1) * rows)
+                g_heads[:, to : to + HEAD_DIM] = swapped[lines, at : at + HEAD_DIM].astype(F32)
         for d in range(docs):
             to = (d * seq + device) * part
             for j, target in enumerate((gate, up)):
                 at = (j * docs + d) * group
-                target[:, to : to + part] = raw[lines, at : at + part].astype(F32)
+                target[:, to : to + part] = swapped[lines, at : at + part].astype(F32)
     low = masters[0][...].astype(BF).astype(F32)
     gain_one = jnp.sum(g_heads[...] * low, axis=1, keepdims=True)
     gain_two = jnp.sum(
@@ -703,11 +701,11 @@
     return pl.BlockSpec(memory_space=pltpu.VMEM)
 
 
-def grads(masters, by_head, merge, raw, down, devices, heads, docs, waits):
-    inputs = [*masters, by_head, merge, raw, down]
+def grads(masters, swapped, merge, down, devices, heads, docs):
+    inputs = [*masters, swapped, merge, down]
     return pl.pallas_call(
         functools.partial(grads_kernel, heads, docs),
-        in_specs=[whole(member) for member in inputs] + waits_for(len(waits)),
+        in_specs=[whole(member) for member in inputs],
         out_specs=[whole(None)] * 5,
         out_shape=[
             jax.ShapeDtypeStruct(masters[0].shape, F32),
@@ -719,7 +717,7 @@
         compiler_params=params(),
         cost_estimate=cheap(),
         name="grads",
-    )(*inputs, *waits)
+    )(*inputs)
 
 
 def moments_kernel(*refs):
@@ -838,14 +836,12 @@
     low_heads = w_heads.astype(BF).reshape(weight_rows, 3, seq_count, heads, HEAD_DIM)
     low_heads = low_heads.transpose(2, 0, 3, 1, 4).reshape(seq_count, weight_rows, 3 * cols)
     gain_cols = jnp.pad(gains.astype(BF).T, ((0, 0), (0, LANES - 2)))
-    first_block = stack(
-        swap(
-            lambda j: jnp.concatenate(
-                [lax.dynamic_index_in_dim(low_heads, j, 0, False), gain_cols], axis=1
-            )
-        ),
-        "seq",
+    first_pieces = swap(
+        lambda j: jnp.concatenate(
+            [lax.dynamic_index_in_dim(low_heads, j, 0, False), gain_cols], axis=1
+        )
     )
+    first_block = stack(first_pieces, "seq")
     merge_cols = width // seq_count
     low_merge = w_merge.astype(BF).reshape(weight_rows, seq_count, merge_cols).transpose(1, 0, 2)
     low_merge = low_merge.reshape(seq_count * weight_rows, merge_cols)
@@ -858,7 +854,8 @@
         return split.reshape(seq_count, weight_rows, hidden)
 
     low_raw = after(jnp.concatenate([columns(w_gate), columns(w_up)], axis=2), first_block)
-    low_raw = stack(swap(lambda j: lax.dynamic_index_in_dim(low_raw, j, 0, False)), "seq")
+    raw_pieces = swap(lambda j: lax.dynamic_index_in_dim(low_raw, j, 0, False))
+    low_raw = stack(raw_pieces, "seq")
     packed = pack_inner(low_raw, w_down, group, min(512, width))
     packed = pieces_of(packed, "docs")
 
@@ -873,8 +870,8 @@
     merge_full = jnp.stack([pick(low_merge, "seq", j) for j in range(seq_count)], axis=1)
     merge_full = merge_full.reshape(width, width)
 
-    waits = (*first[1:], *packed[1:5], *packed[6:7], *x_near[1:], *grad_low[1:], *low_merge[1:])
-    grad_low = lay_out(here, grad_low)
+    small = [send(packed[k][:16], "docs", 1) for k in range(2, len(packed), 4)]
+    waits = (*first_pieces[1:], *raw_pieces[1:])
     gated, memory = [], []
     for member in pack_memory(partner, cache_keys, cache_values, heads, seq_count):
         gated.append(gate(member.reshape(devices, 2, per_device, 2 * HEAD_DIM), *waits))
@@ -882,19 +879,23 @@
             gated[-1], ("docs", "seq"), split_axis=0, concat_axis=0, tiled=True
         )
         memory.append(member.reshape(devices * 2 * per_device, 2 * HEAD_DIM))
-        waits = (memory[0], *packed[5:])
+        waits = (
+            memory[0], *first[1:], *packed[1:3], *small, *x_near[1:], *grad_low[1:], *low_merge[1:]
+        )
+    grad_low = lay_out(here, grad_low)
     cosine, sine = rotation(length)
     (
         x_low, normed_one, query_local, query_memory, key_local, value_local, words, heads_here, gain_rows,
     ) = project(here, x_near, first, cosine, sine, heads, per_device * devices, per_device,
-      gated[:1])
+      gated[-1:])
     local, high, total = attend_local(query_local, key_local, value_local, heads)
 
 
     attended, blended, lse = [], [], []
+    waits = (grad_low, merge_full)
     for h in range(heads):
         result = attend_memory(
-            flag, query_memory, words, memory[h], local, high, total, h, (grad_low, merge_full)
+            flag, query_memory, words, memory[h], local, high, total, h, waits
         )
         attended.append(result[0])
         blended.append(pieces_of(result[1], "seq"))
@@ -904,12 +905,13 @@
         here, [piece for pieces in zip(*blended) for piece in pieces], packed,
         x_low, merge_full, gain_rows, grad_low, heads, hidden,
     )
+    bits = docs_count.bit_length() - 1
+    g_raw = dot_tn(normed_two, grad_raw).astype(BF)
+    g_raw = g_raw.reshape(docs_count, width // docs_count, 2 * hidden)
     grad_normed_two = halve(back.reshape(seq_count, rows, width), "seq", 0)
-    bits = docs_count.bit_length() - 1
-    g_gate, g_up = (
-        dot_tn(normed_two, grad_raw[:, j * hidden : (j + 1) * hidden]).astype(BF) for j in range(2)
-    )
-    g_down = dot_tn(active, grad_low).astype(BF).reshape(docs_count, group, width)
+    started = token(grad_normed_two)
+    g_down = (dot_tn(active, grad_low) + started).astype(BF).reshape(docs_count, group, width)
+    down_out = (dot(active, down_here) + started).astype(BF).reshape(seq_count, rows, width)
     grad_normed_two = reduce_over(grad_normed_two, "seq", 1)
     unit_two, scale_two = norm_rows(middle)
     grad_middle = cotangent[0].astype(F32) + norm_back(
@@ -919,15 +921,16 @@
     grad_mine = dot_nt(grad_branch, merge_full).astype(BF)
     grad_attended = stack(swap(lambda j: lax.dynamic_slice_in_dim(grad_mine, j * cols, cols, 1)), "seq")
 
-    down_out = dot(active, down_here).astype(BF).reshape(seq_count, rows, width)
-    down_out = halve(down_out, "seq", 0)
-    waits = (g_gate, g_up, g_down, down_out)
-    g_gate = g_gate.reshape(docs_count, width // docs_count, hidden)
-    g_gate = halve(g_gate, "docs", 0, token(grad_attended))
-    g_up = g_up.reshape(docs_count, width // docs_count, hidden)
+    arrived = token(grad_attended)
+    x_bits = bits // 2
+    first_z = [(stage, 1 << x_bits) for stage in range(x_bits, bits)]
+    first_z += [(stage, 1) for stage in range(x_bits)]
+    g_down = halve(g_down, "docs", first_z[0][0], arrived, first_z[0][1])
+    g_raw = halve(g_raw, "docs", 0, arrived)
+    waits = (g_raw, g_down)
     branches = pieces_of(gate(grad_branch, grad_attended), "seq")
 
-    projected, by_head = [], []
+    projected, g_heads = [], []
     for h in range(heads):
         projected.append(
             attend_back(
@@ -935,55 +938,54 @@
                 memory[h], attended[h], grad_attended, lse[h], cosine, sine, h, waits,
             )
         )
-        g_heads = dot_tn(normed_one, projected[h]).astype(BF)
-        by_head.append(g_heads.reshape(docs_count, width // docs_count, 3 * HEAD_DIM))
+        g_head = dot_tn(normed_one, projected[h]).astype(BF)
+        g_head = g_head.reshape(docs_count, width // docs_count, 3 * HEAD_DIM)
         if h == 0:
             halfway = token(projected[0])
-            down_out = gate(down_out, projected[0])
-            g_gate = halve(g_gate, "docs", 1, halfway)
-            g_up = halve(g_up, "docs", 0, halfway)
-            g_down = halve(g_down, "docs", 0, halfway)
-            waits = (g_heads, g_gate, g_up, g_down, *branches[1:])
+            g_merge = (dot_tn(blended, stack(branches, "seq")) + halfway).astype(BF)
+            g_merge = g_merge.reshape(docs_count, seq_count, weight_rows, width)
+            g_merge = lax.dynamic_index_in_dim(g_merge, seq_index, 1, False)
+            down_out = halve(down_out, "seq", 0, halfway)
+            g_raw = halve(g_raw, "docs", 1, halfway)
+            waits = (g_head, g_merge)
+        g_heads.append(g_head)
     last = token(projected[-1])
-    down_out = reduce_over(down_out, "seq", 1, last)
-    activations = (middle + down_out).astype(BF)[None]
-    by_head = [halve(member, "docs", 0, last) for member in by_head]
-    begun = token(by_head[-1])
-    g_gate = halve(g_gate, "docs", 2, begun) if bits > 2 else g_gate
-    g_gate = reduce_over(g_gate, "docs", 3)
-    g_up = reduce_over(halve(g_up, "docs", 1, last), "docs", 2, begun)
-    g_down = reduce_over(halve(g_down, "docs", 1, last), "docs", 2, begun)[:down_rows]
-    g_raw = jnp.concatenate([g_gate, g_up], axis=1)
-    g_merge = (dot_tn(blended, stack(branches, "seq")) + begun).astype(BF)
-    g_merge = g_merge.reshape(docs_count, seq_count, weight_rows, width)
-    g_merge = lax.dynamic_index_in_dim(g_merge, seq_index, 1, False)
-    by_head = jnp.concatenate(by_head, axis=2)
-    g_merge = reduce_over(g_merge, "docs")
-    def own_rows(member):
-        member = member.astype(BF).reshape(seq_count, weight_rows, member.shape[1])
-        return swap(lambda j: lax.dynamic_index_in_dim(member, j, 0, False))
-
-    g_raw = stack(own_rows(g_raw), "seq")
-    by_head = stack(own_rows(reduce_over(by_head, "docs", 1)), "seq", 1)
+    g_heads = [halve(member, "docs", 0, last) for member in g_heads[::-1]]
+    arrived = token(g_heads[0])
+    g_heads = halve(jnp.concatenate(g_heads, axis=2), "docs", 1)
+    g_merge = halve(g_merge, "docs", 0, arrived)
+    g_merge = reduce_over(halve(g_merge, "docs", 1, token(g_heads)), "docs", 2)
+    for k in range(2, bits):
+        g_raw = halve(g_raw, "docs", k, last if k == 2 else 0.0)
+    for k in range(1, bits):
+        late = last if k == 1 else 0.0
+        g_down = halve(g_down, "docs", first_z[k][0], late, first_z[k][1])
+    g_heads = reduce_over(g_heads, "docs", 2)
+    g_down = g_down[0][:down_rows]
+    g_raw = jnp.concatenate([g_raw[0], g_heads], axis=1)
+    g_raw = g_raw.astype(BF).reshape(seq_count, weight_rows, 2 * hidden + 3 * cols)
+    g_raw = stack(swap(lambda j: lax.dynamic_index_in_dim(g_raw, j, 0, False)), "seq")
+    g_heads, g_gate, g_up, g_gains, totals = grads(
+        masters, g_raw, g_merge, g_down, devices, heads, docs_count
+    )
+    gradients = (g_heads, g_merge, g_gate, g_up, g_down, g_gains)
+    totals = to_everyone(totals)
     grad_projected = jnp.concatenate(projected, axis=1)
-    grad_normed_one = (dot_nt(grad_projected, heads_here) + begun).astype(BF)
+    grad_normed_one = (dot_nt(grad_projected, heads_here) + arrived).astype(BF)
     grad_normed_one = halve(grad_normed_one.reshape(seq_count, rows, width), "seq", 0)
-    waits = (grad_normed_one, activations)
-    grad_normed_one = reduce_over(grad_normed_one, "seq", 1)
+    new_moments, new_squares, directions, updates = step_moments(
+        totals, masters, moments, squares, gradients, ()
+    )
+    moved = token(updates)
+    grad_normed_one = reduce_over(grad_normed_one, "seq", 1, moved)
     unit_one, scale_one = norm_rows(tokens[0].astype(F32))
     input_grad = grad_middle + norm_back(grad_normed_one, unit_one, scale_one, gain_rows[0:1])
     input_grad = input_grad[None]
-
-    g_heads, g_gate, g_up, g_gains, totals = grads(
-        masters, by_head, g_merge, g_raw, g_down, devices, heads, docs_count, waits
-    )
-    gradients = (g_heads, g_merge, g_gate, g_up, g_down, g_gains)
-    totals = to_everyone(totals)
-    new_moments, new_squares, directions, updates = step_moments(
-        totals, masters, moments, squares, gradients, ()
-    )
+    down_out = reduce_over(down_out, "seq", 1, moved)
+    activations = (middle + down_out).astype(BF)[None]
+
     new_weights, layer_norms, clip_norm = step_weights(
-        totals, to_everyone(updates), masters, directions, (input_grad,)
+        totals, to_everyone(updates), masters, directions, (input_grad, activations)
     )
     results = [activations, input_grad]
     for place in range(6):

time: 461 us -> 444 us (0.963)
  Pallas kernels: 128 us -> 90.3 us
  starting transfers between devices: 75.6 us -> 109 us
  waiting for transfers between devices: 163 us -> 130 us
  other arithmetic: 30.2 us -> 44.9 us
    pallas_call x4, Pallas kernels: 59.5 us -> 22.7 us  [the longest x2 15.7 us: attend_back(): pl.pallas_call(functools.partial(attend_back_kernel, min(512, keys), leng...]
    ppermute x69 -> x65, waiting for transfers between devices: 149 us -> 115 us  [send(): lax.ppermute(x, axis, [(i, i ^ bits) for i in range(lax.axis_size(axis))])]
    ppermute x69 -> x65, starting transfers between devices: 60 us -> 90.9 us  [send(): lax.ppermute(x, axis, [(i, i ^ bits) for i in range(lax.axis_size(axis))])]
    all_to_all x2, waiting for transfers between devices: 1.88 us -> 8.39 us  [shards(): lax.all_to_all(gated[-1], ('docs', 'seq'), split_axis=0, concat_axis=0, t...]
    unnamed x7, other arithmetic: 0.53 us -> 6.88 us
    dot_general x6 -> x5, matrix products: 13.4 us -> 16.1 us  [dot_tn(): lax.dot_general(a, b, (((0,), (0,)), ((), ())), preferred_element_type=F32)]
    add x13 -> x12, other arithmetic: 7.93 us -> 10.4 us  [halve(): total = kept + late + send(away, axis, 1 << stage).astype(F32)]
    unnamed x167 -> x147, local copies, waits for them, and re-layouts: 10.1 us -> 8.29 us
  transfers between devices with their start and end apart: 73 -> 69, of which waited for: 32 -> 24; matrix products, arithmetic and copies ran while one was open for 14% -> 19% of each run, Pallas kernels for 23% -> 15%
where the time goes in v3:
time: 444 us; the launch traced here: 437 us
  waiting for transfers between devices  130 us (29%)
  starting transfers between devices  109 us (25%)
  Pallas kernels  90.3 us (20%)
  other arithmetic  44.9 us (10%)
  local copies, waits for them, and re-layouts  32.1 us (7%)
  matrix products  20.5 us (5%)
  between operations  9.62 us (2%)
    ppermute x65, waiting for transfers between devices, send(): lax.ppermute(x, axis, [(i, i ^ bits) for i in range(lax.axis_size(axis))])  115 us
    ppermute x65, starting transfers between devices, send(): lax.ppermute(x, axis, [(i, i ^ bits) for i in range(lax.axis_size(axis))])  90.9 us
    pallas_call x1, Pallas kernels, feed_forward(): pl.pallas_call(functools.partial(feed_forward_kernel, heads, seq, docs),...  21.6 us
    dot_general x5, matrix products, dot_tn(): lax.dot_general(a, b, (((0,), (0,)), ((), ())), preferred_element_type=F32)  16.1 us
    pallas_call x2, Pallas kernels, attend_back(): pl.pallas_call(functools.partial(attend_back_kernel, min(512, keys), leng...  15.7 us
    pallas_call x1, Pallas kernels, project(): pl.pallas_call(functools.partial(project_kernel, heads, len(tokens), len(...  13.5 us
    all_to_all x2, starting transfers between devices, shards(): lax.all_to_all(gated[-1], ('docs', 'seq'), split_axis=0, concat_axis=0, t...  12.6 us
    add x12, other arithmetic, halve(): total = kept + late + send(away, axis, 1 << stage).astype(F32)  10.4 us
  transfers between devices with their start and end apart: 69, of which 24 were waited for; matrix products, arithmetic and copies ran while one was open for 19% of the time, Pallas kernels for 15%

profile of v3, /device:TPU:0, one launch (start us, length us, event | category | flops | bytes accessed | tf_op | source)
XLA Modules:
  0.0 436.5 jit_solution(13273784565230299979)
XLA Ops:
  6.4 7.8 %pack_memory.1 = (bf16[8,4,2,64,256]{4,3,2,1,0:T(8,128)(2,1)}, bf16[8,4,2,64,256]{4,3,2,1,0:T(8,128)(2,1)}) custom-call(s32[8]{0:T(128)} %partner.1, bf16[8,64,1024]{2,1,0:T(8,128)(2,1)} %mate_key.1, bf16[8,64,1024]{2,1,0:T(8,128)(2,1)} %mate_value.1, bf16[8,64,1024]{2,1,0:T(8,128)(2,1)} %mate_key.1, bf16[8,64,1024]{2,1,0:T(8,128)(2,1)} %mate_value.1), custom_call_target="tpu_custom_call" | custom-call | flops 1 | bytes 1 | tf_op jit(solution)/shard_map/pack_memory/pallas_call | solution.py:153
  25.8 6.1 %all-to-all-start = ((bf16[32,2,64,256]{3,2,1,0:T(8,128)(2,1)}), bf16[32,2,64,256]{3,2,1,0:T(8,128)(2,1)S(1)}, u32[]{:S(2)}, u32[]{:S(2)}) async-start(bf16[32,2,64,256]{3,2,1,0:T(8,128)(2,1)} %gate.3), calls=%async_computation | async-start | bytes 4194304 | tf_op jit(solution)/shard_map/all_to_all | solution.py:878
  52.7 20.9 %collective-permute-done.10.refs_3_.refs_6_ = bf16[128,1152]{1,0:T(8,128)(2,1)S(1)} collective-permute-done((bf16[128,1152]{1,0:T(8,128)(2,1)}, bf16[128,1152]{1,0:T(8,128)(2,1)S(1)}, u32[]{:S(2)}, u32[]{:S(2)}) %collective-permute-start.10) | collective-permute-done | bytes 294944 | tf_op jit(solution)/shard_map/ppermute | solution.py:29
  75.0 9.6 %collective-permute-done.14.refs_7_.refs_10_ = bf16[128,1152]{1,0:T(8,128)(2,1)S(1)} collective-permute-done((bf16[128,1152]{1,0:T(8,128)(2,1)S(1)}, bf16[128,1152]{1,0:T(8,128)(2,1)S(1)}, u32[]{:S(2)}, u32[]{:S(2)}) %collective-permute-start.14) | collective-permute-done | bytes 294944 | tf_op jit(solution)/shard_map/ppermute | solution.py:29
  94.6 13.7 %collective-permute-done.19.refs_12_ = bf16[576,512]{1,0:T(8,128)(2,1)} collective-permute-done((bf16[576,512]{1,0:T(8,128)(2,1)}, bf16[576,512]{1,0:T(8,128)(2,1)}, u32[]{:S(2)}, u32[]{:S(2)}) %collective-permute-start.19) | collective-permute-done | bytes 589856 | tf_op jit(solution)/shard_map/ppermute | solution.py:29
  124.1 5.5 %collective-permute-done.20.refs_14_ = bf16[576,512]{1,0:T(8,128)(2,1)S(1)} collective-permute-done((bf16[576,512]{1,0:T(8,128)(2,1)}, bf16[576,512]{1,0:T(8,128)(2,1)S(1)}, u32[]{:S(2)}, u32[]{:S(2)}) %collective-permute-start.20) | collective-permute-done | bytes 589856 | tf_op jit(solution)/shard_map/ppermute | solution.py:29
  139.9 6.5 %all-to-all-start.1 = ((bf16[32,2,64,256]{3,2,1,0:T(8,128)(2,1)}), bf16[32,2,64,256]{3,2,1,0:T(8,128)(2,1)S(1)}, u32[]{:S(2)}, u32[]{:S(2)}) async-start(bf16[32,2,64,256]{3,2,1,0:T(8,128)(2,1)} %gate.4.refs_14_), calls=%async_computation.1 | async-start | bytes 4194304 | tf_op jit(solution)/shard_map/all_to_all | solution.py:878
  162.7 13.5 %project.1 = (bf16[1024,1024]{1,0:T(8,128)(2,1)}, bf16[1024,1024]{1,0:T(8,128)(2,1)}, bf16[1024,256]{1,0:T(8,128)(2,1)}, bf16[1024,256]{1,0:T(8,128)(2,1)}, bf16...) custom-call(s32[2]{0:T(128)} %pad_add_fusion.here, ...), custom_call_target="tpu_custom_call" | custom-call | flops 1 | bytes 1 | tf_op jit(solution)/shard_map/project/pallas_call | solution.py:303
  176.2 5.7 %attend_local.1 = (f32[1024,256]{1,0:T(8,128)}, f32[1024,256]{1,0:T(8,128)}, f32[1024,256]{1,0:T(8,128)}) custom-call(bf16[1024,256]{1,0:T(8,128)(2,1)} %get-tuple-element.85.ql, bf16[1024,256]{1,0:T(8,128)(2,1)} %get-tuple-element.86.kl, bf16[1024,256]{1,0:T(8,128)(2,1)} %get-tuple-element.87.vl), custom_call_target="tpu_custom_call" | custom-call | flops 1 | bytes 1 | tf_op jit(solution)/shard_map/attend_local/pallas_call | solution.py:466
  186.8 8.4 %all-to-all-done.1 = bf16[32,2,64,256]{3,2,1,0:T(8,128)(2,1)S(1)} async-done(((bf16[32,2,64,256]{3,2,1,0:T(8,128)(2,1)}), bf16[32,2,64,256]{3,2,1,0:T(8,128)(2,1)S(1)}, u32[]{:S(2)}, u32[]{:S(2)}) %all-to-all-start.1) | async-done | bytes 2097184 | tf_op jit(solution)/shard_map/all_to_all | solution.py:878
  202.0 6.0 %collective-permute-done.31.refs_5_ = bf16[1024,128]{1,0:T(8,128)(2,1)S(1)} collective-permute-done((bf16[1024,128]{1,0:T(8,128)(2,1)}, bf16[1024,128]{1,0:T(8,128)(2,1)S(1)}, u32[]{:S(2)}, u32[]{:S(2)}) %collective-permute-start.31) | collective-permute-done | bytes 262176 | tf_op jit(solution)/shard_map/ppermute | solution.py:29
  210.9 21.6 %feed_forward.1 = (bf16[1024,1024]{1,0:T(8,128)(2,1)}, bf16[1024,1024]{1,0:T(8,128)(2,1)}, bf16[1024,768]{1,0:T(8,128)(2,1)}, bf16[1024,1536]{1,0:T(8,128)(2,1)}...) custom-call(s32[2]{0:T(128)} %pad_add_fusion.here, ...), custom_call_target="tpu_custom_call" | custom-call | flops 1 | bytes 1 | tf_op jit(solution)/shard_map/feed_forward/pallas_call | solution.py:380
  234.5 5.6 %convolution_convert_fusion = bf16[1024,1536]{1,0:T(8,128)(2,1)S(1)} fusion(bf16[1024,1024]{1,0:T(8,128)(2,1)S(1)} %copy-done.65, bf16[1024,1536]{1,0:T(8,128)(2,1)} %get-tuple-element.102), kind=kOutput, calls=%fused_computation.3 | convolution fusion | flops 3222798336 | bytes 8388608 | tf_op jit(solution)/shard_map/dot_general | solution.py:99
  241.5 8.2 %collective-permute-start.42 = (bf16[4,1,128,1536]{3,2,0,1:T(8,128)(2,1)}, bf16[4,1,128,1536]{3,2,0,1:T(8,128)(2,1)}, u32[]{:S(2)}, u32[]{:S(2)}) collective-permute-start(bf16[4,1,128,1536]{3,2,0,1:T(8,128)(2,1)} %dynamic-slice_bitcast_fusion), channel_id=1, source_target_pairs={{0,4},{4,0},{8,12},{12,8},{16,20},{20,16},{24,28},{28,24},{1,5},{5... | collective-permute-start | bytes 4718600 | tf_op jit(solution)/shard_map/ppermute | solution.py:29
  279.1 5.5 %collective-permute-done.42 = bf16[4,1,128,1536]{3,2,0,1:T(8,128)(2,1)} collective-permute-done((bf16[4,1,128,1536]{3,2,0,1:T(8,128)(2,1)}, bf16[4,1,128,1536]{3,2,0,1:T(8,128)(2,1)}, u32[]{:S(2)}, u32[]{:S(2)}) %collective-permute-start.42) | collective-permute-done | bytes 1572896 | tf_op jit(solution)/shard_map/ppermute | solution.py:29
  290.8 7.9 %attend_back.2 = bf16[1024,384]{1,0:T(8,128)(2,1)} custom-call(s32[1]{0:T(128)S(6)} %select_n.913.flag, bf16[1024,256]{1,0:T(8,128)(2,1)} %get-tuple-element.85.ql, bf16[1024,256]{1,0:T(8,128)(2,1)} %get-tuple-element.83.qm, bf16[1024,256]{1,0:T(8,128)(2,1)} %get-tuple-element.86.kl, bf16[1024,256]{1,0:T(8,128)(2,1)} %get-tuple-element.87.vl, ...), custom_call_target="tpu_custom_call" | custom-call | flops 16000000000 | bytes 2097152 | tf_op jit(solution)/shard_map/attend_back/pallas_call | solution.py:611
  307.3 6.8 %collective-permute-start.51 = (bf16[4,1,128,384]{3,2,0,1:T(8,128)(2,1)}, bf16[4,1,128,384]{3,2,0,1:T(8,128)(2,1)}, u32[]{:S(2)}, u32[]{:S(2)}) collective-permute-start(bf16[4,1,128,384]{3,2,0,1:T(8,128)(2,1)} %dynamic-slice_bitcast_fusion.5), channel_id=1, source_target_pairs={{0,4},{4,0},{8,12},{12,8},{16,20},{20,16},{24,28},{28,24},{1,5},{5... | collective-permute-start | bytes 1179656 | tf_op jit(solution)/shard_map/ppermute | solution.py:29
  328.2 7.8 %attend_back.3 = bf16[1024,384]{1,0:T(8,128)(2,1)} custom-call(s32[1]{0:T(128)S(6)} %select_n.913.flag, bf16[1024,256]{1,0:T(8,128)(2,1)} %get-tuple-element.85.ql, bf16[1024,256]{1,0:T(8,128)(2,1)} %get-tuple-element.83.qm, bf16[1024,256]{1,0:T(8,128)(2,1)} %get-tuple-element.86.kl, bf16[1024,256]{1,0:T(8,128)(2,1)} %get-tuple-element.87.vl, ...), custom_call_target="tpu_custom_call" | custom-call | flops 16000000000 | bytes 2097152 | tf_op jit(solution)/shard_map/attend_back/pallas_call | solution.py:611
  340.3 7.3 %collective-permute-start.50 = (bf16[4,1,128,384]{3,2,0,1:T(8,128)(2,1)S(1)}, bf16[4,1,128,384]{3,2,0,1:T(8,128)(2,1)S(1)}, u32[]{:S(2)}, u32[]{:S(2)}) collective-permute-start(bf16[4,1,128,384]{3,2,0,1:T(8,128)(2,1)S(1)} %dynamic-slice_bitcast_fusion.6), channel_id=1, source_target_pairs={{0,4},{4,0},{8,12},{12,8},{16,20},{20,16},{24,28},{28,24},{1,5},{5... | collective-permute-start | bytes 1179656 | tf_op jit(solution)/shard_map/ppermute | solution.py:29
  352.9 8.8 %collective-permute-done.61 = bf16[1,1,96,1024]{3,2,1,0:T(8,128)(2,1)S(1)} collective-permute-done((bf16[1,1,96,1024]{3,2,1,0:T(8,128)(2,1)S(1)}, bf16[1,1,96,1024]{3,2,1,0:T(8,128)(2,1)S(1)}, u32[]{:S(2)}, u32[]{:S(2)}) %collective-permute-start.61) | collective-permute-done | bytes 196640 | tf_op jit(solution)/shard_map/ppermute | solution.py:29
  370.3 6.5 %collective-permute-done.52 = bf16[2,1,128,768]{3,2,0,1:T(8,128)(2,1)S(1)} collective-permute-done((bf16[2,1,128,768]{3,2,0,1:T(8,128)(2,1)S(1)}, bf16[2,1,128,768]{3,2,0,1:T(8,128)(2,1)S(1)}, u32[]{:S(2)}, u32[]{:S(2)}) %collective-permute-start.52) | collective-permute-done | bytes 393248 | tf_op jit(solution)/shard_map/ppermute | solution.py:29
  381.1 7.6 %collective-permute-done.53 = bf16[1,1,128,768]{3,2,0,1:T(8,128)(2,1)S(1)} collective-permute-done((bf16[1,1,128,768]{3,2,0,1:T(8,128)(2,1)S(1)}, bf16[1,1,128,768]{3,2,0,1:T(8,128)(2,1)S(1)}, u32[]{:S(2)}, u32[]{:S(2)}) %collective-permute-start.53) | collective-permute-done | bytes 196640 | tf_op jit(solution)/shard_map/ppermute | solution.py:29
  406.9 7.1 %all-to-all-done.2.refs_0_ = f32[32,1,128]{2,1,0:T(1,128)S(1)} async-done(((f32[32,1,128]{2,1,0:T(1,128)}), f32[32,1,128]{2,1,0:T(1,128)S(1)}, u32[]{:S(2)}, u32[]{:S(2)}) %all-to-all-start.2) | async-done | bytes 16416 | tf_op jit(solution)/shard_map/all_to_all | solution.py:87
  414.5 6.6 %moments.1 = (f32[32,3072]{1,0:T(8,128)}, f32[32,1024]{1,0:T(8,128)}, f32[32,2816]{1,0:T(8,128)}, f32[32,2816]{1,0:T(8,128)}, f32[88,1024]{1,0:T(8,128)}, /*inde...) custom-call(f32[32,1,128]{2,1,0:T(1,128)} %copy-done.59, ...), custom_call_target="tpu_custom_call" | custom-call | flops 1 | bytes 1 | tf_op jit(solution)/shard_map/moments/pallas_call | solution.py:750
  (400 shorter events, 216.1 us)
Async XLA Ops:
  25.8 112.7 %all-to-all-start = ((bf16[32,2,64,256]{3,2,1,0:T(8,128)(2,1)}), bf16[32,2,64,256]{3,2,1,0:T(8,128)(2,1)S(1)}, u32[]{:S(2)}, u32[]{:S(2)}) async-start(bf16[32,2,64,256]{3,2,1,0:T(8,128)(2,1)} %gate.3), calls=%async_computation | async-start | bytes 4194304 | tf_op jit(solution)/shard_map/all_to_all | solution.py:878
  34.9 51.5 %collective-permute-start.7 = (bf16[256,1152]{1,0:T(8,128)(2,1)}, bf16[256,1152]{1,0:T(8,128)(2,1)}, u32[]{:S(2)}, u32[]{:S(2)}) collective-permute-start(bf16[256,1152]{1,0:T(8,128)(2,1)} %broadcast_add_fusion.refs_0_), channel_id=1, source_target_pairs={{0,2},{1,3},{2,0},{3,1},{4,6},{5,7},{6,4},{7,5},{8,10},{9,11},{10,... | collective-permute-start | bytes 1769480 | tf_op jit(solution)/shard_map/ppermute | solution.py:29
  36.7 36.8 %collective-permute-start.10 = (bf16[128,1152]{1,0:T(8,128)(2,1)}, bf16[128,1152]{1,0:T(8,128)(2,1)S(1)}, u32[]{:S(2)}, u32[]{:S(2)}) collective-permute-start(bf16[128,1152]{1,0:T(8,128)(2,1)} %pad_maximum_fusion.6.refs_4_), channel_id=1, source_target_pairs={{0,8},{4,12},{8,0},{12,4},{16,24},{20,28},{24,16},{28,20},{1,9},{5... | collective-permute-start | bytes 884744 | tf_op jit(solution)/shard_map/ppermute | solution.py:29
  39.1 45.5 %collective-permute-start.14 = (bf16[128,1152]{1,0:T(8,128)(2,1)S(1)}, bf16[128,1152]{1,0:T(8,128)(2,1)S(1)}, u32[]{:S(2)}, u32[]{:S(2)}) collective-permute-start(bf16[128,1152]{1,0:T(8,128)(2,1)S(1)} %collective-permute-done.12.refs_5_.refs_8_), channel_id=1, source_target_pairs={{0,8},{4,12},{8,0},{12,4},{16,24},{20,28},{24,16},{28,20},{1,9},{5... | collective-permute-start | bytes 884744 | tf_op jit(solution)/shard_map/ppermute | solution.py:29
  47.1 61.2 %collective-permute-start.19 = (bf16[576,512]{1,0:T(8,128)(2,1)}, bf16[576,512]{1,0:T(8,128)(2,1)}, u32[]{:S(2)}, u32[]{:S(2)}) collective-permute-start(bf16[576,512]{1,0:T(8,128)(2,1)} %pack_inner.1.refs_8_), channel_id=1, source_target_pairs={{0,16},{4,20},{8,24},{12,28},{16,0},{20,4},{24,8},{28,12},{1,17},{... | collective-permute-start | bytes 1769480 | tf_op jit(solution)/shard_map/ppermute | solution.py:29
  50.5 39.0 %collective-permute-start.9 = (bf16[128,1152]{1,0:T(8,128)(2,1)}, bf16[128,1152]{1,0:T(8,128)(2,1)S(1)}, u32[]{:S(2)}, u32[]{:S(2)}) collective-permute-start(bf16[128,1152]{1,0:T(8,128)(2,1)} %pad_maximum_fusion.6.refs_4_), channel_id=1, source_target_pairs={{0,4},{4,0},{8,12},{12,8},{16,20},{20,16},{24,28},{28,24},{1,5},{5... | collective-permute-start | bytes 884744 | tf_op jit(solution)/shard_map/ppermute | solution.py:29
  89.6 28.7 %collective-permute-start.17 = (bf16[576,512]{1,0:T(8,128)(2,1)}, bf16[576,512]{1,0:T(8,128)(2,1)S(1)}, u32[]{:S(2)}, u32[]{:S(2)}) collective-permute-start(bf16[576,512]{1,0:T(8,128)(2,1)} %pack_inner.1.refs_8_), channel_id=1, source_target_pairs={{0,8},{4,12},{8,0},{12,4},{16,24},{20,28},{24,16},{28,20},{1,9},{5... | collective-permute-start | bytes 1769480 | tf_op jit(solution)/shard_map/ppermute | solution.py:29
  89.7 30.0 %collective-permute-start.16 = (bf16[576,512]{1,0:T(8,128)(2,1)}, bf16[576,512]{1,0:T(8,128)(2,1)S(1)}, u32[]{:S(2)}, u32[]{:S(2)}) collective-permute-start(bf16[576,512]{1,0:T(8,128)(2,1)} %pack_inner.1.refs_8_), channel_id=1, source_target_pairs={{0,4},{4,0},{8,12},{12,8},{16,20},{20,16},{24,28},{28,24},{1,5},{5... | collective-permute-start | bytes 1769480 | tf_op jit(solution)/shard_map/ppermute | solution.py:29
  139.9 55.3 %all-to-all-start.1 = ((bf16[32,2,64,256]{3,2,1,0:T(8,128)(2,1)}), bf16[32,2,64,256]{3,2,1,0:T(8,128)(2,1)S(1)}, u32[]{:S(2)}, u32[]{:S(2)}) async-start(bf16[32,2,64,256]{3,2,1,0:T(8,128)(2,1)} %gate.4.refs_14_), calls=%async_computation.1 | async-start | bytes 4194304 | tf_op jit(solution)/shard_map/all_to_all | solution.py:878
  151.5 49.9 %collective-permute-start.34 = (bf16[576,512]{1,0:T(8,128)(2,1)S(1)}, bf16[576,512]{1,0:T(8,128)(2,1)}, u32[]{:S(2)}, u32[]{:S(2)}) collective-permute-start(bf16[576,512]{1,0:T(8,128)(2,1)S(1)} %copy-done.23), channel_id=1, source_target_pairs={{0,4},{4,0},{8,12},{12,8},{16,20},{20,16},{24,28},{28,24},{1,5},{5... | collective-permute-start | bytes 1769480 | tf_op jit(solution)/shard_map/ppermute | solution.py:29
  153.5 48.4 %collective-permute-start.35 = (bf16[576,512]{1,0:T(8,128)(2,1)}, bf16[576,512]{1,0:T(8,128)(2,1)}, u32[]{:S(2)}, u32[]{:S(2)}) collective-permute-start(bf16[576,512]{1,0:T(8,128)(2,1)} %collective-permute-done.19.refs_12_), channel_id=1, source_target_pairs={{0,4},{4,0},{8,12},{12,8},{16,20},{20,16},{24,28},{28,24},{1,5},{5... | collective-permute-start | bytes 1769480 | tf_op jit(solution)/shard_map/ppermute | solution.py:29
  153.6 56.3 %collective-permute-start.36 = (bf16[576,512]{1,0:T(8,128)(2,1)S(1)}, bf16[576,512]{1,0:T(8,128)(2,1)}, u32[]{:S(2)}, u32[]{:S(2)}) collective-permute-start(bf16[576,512]{1,0:T(8,128)(2,1)S(1)} %copy-done.45), channel_id=1, source_target_pairs={{0,4},{4,0},{8,12},{12,8},{16,20},{20,16},{24,28},{28,24},{1,5},{5... | collective-permute-start | bytes 1769480 | tf_op jit(solution)/shard_map/ppermute | solution.py:29
  241.5 43.2 %collective-permute-start.42 = (bf16[4,1,128,1536]{3,2,0,1:T(8,128)(2,1)}, bf16[4,1,128,1536]{3,2,0,1:T(8,128)(2,1)}, u32[]{:S(2)}, u32[]{:S(2)}) collective-permute-start(bf16[4,1,128,1536]{3,2,0,1:T(8,128)(2,1)} %dynamic-slice_bitcast_fusion), channel_id=1, source_target_pairs={{0,4},{4,0},{8,12},{12,8},{16,20},{20,16},{24,28},{28,24},{1,5},{5... | collective-permute-start | bytes 4718600 | tf_op jit(solution)/shard_map/ppermute | solution.py:29
  255.9 32.3 %collective-permute-start.43 = (bf16[2,2,96,1024]{3,2,1,0:T(8,128)(2,1)}, bf16[2,2,96,1024]{3,2,1,0:T(8,128)(2,1)}, u32[]{:S(2)}, u32[]{:S(2)}) collective-permute-start(bf16[2,2,96,1024]{3,2,1,0:T(8,128)(2,1)} %dynamic-slice_bitcast_fusion.4), channel_id=1, source_target_pairs={{0,8},{4,12},{8,0},{12,4},{16,24},{20,28},{24,16},{28,20},{1,9},{5... | collective-permute-start | bytes 2359304 | tf_op jit(solution)/shard_map/ppermute | solution.py:29
  276.9 30.3 %collective-permute-start.44 = (bf16[2,1,256,1024]{3,2,1,0:T(8,128)(2,1)}, bf16[2,1,256,1024]{3,2,1,0:T(8,128)(2,1)}, u32[]{:S(2)}, u32[]{:S(2)}) collective-permute-start(bf16[2,1,256,1024]{3,2,1,0:T(8,128)(2,1)} %dynamic-slice_bitcast_fusion.2), channel_id=1, source_target_pairs={{0,1},{1,0},{2,3},{3,2},{4,5},{5,4},{6,7},{7,6},{8,9},{9,8},{10,11... | collective-permute-start | bytes 3145736 | tf_op jit(solution)/shard_map/ppermute | solution.py:29
  277.1 39.7 %collective-permute-start.46 = (bf16[256,1024]{1,0:T(8,128)(2,1)}, bf16[256,1024]{1,0:T(8,128)(2,1)}, u32[]{:S(2)}, u32[]{:S(2)}) collective-permute-start(bf16[256,1024]{1,0:T(8,128)(2,1)} %gate.5), channel_id=1, source_target_pairs={{0,2},{1,3},{2,0},{3,1},{4,6},{5,7},{6,4},{7,5},{8,10},{9,11},{10,... | collective-permute-start | bytes 1572872 | tf_op jit(solution)/shard_map/ppermute | solution.py:29
  277.9 42.6 %collective-permute-start.48 = (bf16[256,1024]{1,0:T(8,128)(2,1)}, bf16[256,1024]{1,0:T(8,128)(2,1)}, u32[]{:S(2)}, u32[]{:S(2)}) collective-permute-start(bf16[256,1024]{1,0:T(8,128)(2,1)} %gate.5), channel_id=1, source_target_pairs={{0,1},{1,0},{2,3},{3,2},{4,5},{5,4},{6,7},{7,6},{8,9},{9,8},{10,11... | collective-permute-start | bytes 1572872 | tf_op jit(solution)/shard_map/ppermute | solution.py:29
  287.1 31.2 %collective-permute-start.45 = (bf16[2,1,128,1536]{3,2,0,1:T(8,128)(2,1)S(1)}, bf16[2,1,128,1536]{3,2,0,1:T(8,128)(2,1)}, u32[]{:S(2)}, u32[]{:S(2)}) collective-permute-start(bf16[2,1,128,1536]{3,2,0,1:T(8,128)(2,1)S(1)} %fusion.24), channel_id=1, source_target_pairs={{0,8},{4,12},{8,0},{12,4},{16,24},{20,28},{24,16},{28,20},{1,9},{5... | collective-permute-start | bytes 2359304 | tf_op jit(solution)/shard_map/ppermute | solution.py:29
  301.4 46.9 %collective-permute-start.60 = (bf16[1,2,96,1024]{3,2,1,0:T(8,128)(2,1)}, bf16[1,2,96,1024]{3,2,1,0:T(8,128)(2,1)S(1)}, u32[]{:S(2)}, u32[]{:S(2)}) collective-permute-start(bf16[1,2,96,1024]{3,2,1,0:T(8,128)(2,1)} %dynamic-slice_convert_fusion.4), channel_id=1, source_target_pairs={{0,16},{4,20},{8,24},{12,28},{16,0},{20,4},{24,8},{28,12},{1,17},{... | collective-permute-start | bytes 1179656 | tf_op jit(solution)/shard_map/ppermute | solution.py:29
  307.3 41.4 %collective-permute-start.51 = (bf16[4,1,128,384]{3,2,0,1:T(8,128)(2,1)}, bf16[4,1,128,384]{3,2,0,1:T(8,128)(2,1)}, u32[]{:S(2)}, u32[]{:S(2)}) collective-permute-start(bf16[4,1,128,384]{3,2,0,1:T(8,128)(2,1)} %dynamic-slice_bitcast_fusion.5), channel_id=1, source_target_pairs={{0,4},{4,0},{8,12},{12,8},{16,20},{20,16},{24,28},{28,24},{1,5},{5... | collective-permute-start | bytes 1179656 | tf_op jit(solution)/shard_map/ppermute | solution.py:29
  316.8 109.1 %collective-permute-start.62 = (bf16[1,1,256,1024]{3,2,1,0:T(8,128)(2,1)}, bf16[1,1,256,1024]{3,2,1,0:T(8,128)(2,1)}, u32[]{:S(2)}, u32[]{:S(2)}) collective-permute-start(bf16[1,1,256,1024]{3,2,1,0:T(8,128)(2,1)} %dynamic-slice_convert_fusion.2), channel_id=1, source_target_pairs={{0,2},{1,3},{2,0},{3,1},{4,6},{5,7},{6,4},{7,5},{8,10},{9,11},{10,... | collective-permute-start | bytes 1572872 | tf_op jit(solution)/shard_map/ppermute | solution.py:29
  320.5 31.3 %collective-permute-start.49 = (bf16[1,1,128,1536]{3,2,0,1:T(8,128)(2,1)}, bf16[1,1,128,1536]{3,2,0,1:T(8,128)(2,1)}, u32[]{:S(2)}, u32[]{:S(2)}) collective-permute-start(bf16[1,1,128,1536]{3,2,0,1:T(8,128)(2,1)} %dynamic-slice_convert_fusion.5), channel_id=1, source_target_pairs={{0,16},{4,20},{8,24},{12,28},{16,0},{20,4},{24,8},{28,12},{1,17},{... | collective-permute-start | bytes 1179656 | tf_op jit(solution)/shard_map/ppermute | solution.py:29
  369.3 28.1 %collective-permute-start.63 = (bf16[2,1,256,1024]{3,2,1,0:T(8,128)(2,1)S(1)}, bf16[2,1,256,1024]{3,2,1,0:T(8,128)(2,1)S(1)}, u32[]{:S(2)}, u32[]{:S(2)}) collective-permute-start(bf16[2,1,256,1024]{3,2,1,0:T(8,128)(2,1)S(1)} %dynamic-slice_bitcast_fusion.1), channel_id=1, source_target_pairs={{0,1},{1,0},{2,3},{3,2},{4,5},{5,4},{6,7},{7,6},{8,9},{9,8},{10,11... | collective-permute-start | bytes 3145736 | tf_op jit(solution)/shard_map/ppermute | solution.py:29
  398.7 29.7 %collective-permute-start.64 = (bf16[1,1,256,1024]{3,2,1,0:T(8,128)(2,1)}, bf16[1,1,256,1024]{3,2,1,0:T(8,128)(2,1)}, u32[]{:S(2)}, u32[]{:S(2)}) collective-permute-start(bf16[1,1,256,1024]{3,2,1,0:T(8,128)(2,1)} %dynamic-slice_convert_fusion.1), channel_id=1, source_target_pairs={{0,2},{1,3},{2,0},{3,1},{4,6},{5,7},{6,4},{7,5},{8,10},{9,11},{10,... | collective-permute-start | bytes 1572872 | tf_op jit(solution)/shard_map/ppermute | solution.py:29
  (117 other events, 1129.9 us)

commit v4 on v3

--- a/solution.py
+++ b/solution.py
@@ -853,16 +853,16 @@
         split = jnp.pad(split.transpose(2, 0, 1, 3), ((0, 0), (0, 0), (0, 0), (0, group - down_rows)))
         return split.reshape(seq_count, weight_rows, hidden)
 
-    low_raw = after(jnp.concatenate([columns(w_gate), columns(w_up)], axis=2), first_block)
+    low_raw = jnp.concatenate([columns(w_gate), columns(w_up)], axis=2)
     raw_pieces = swap(lambda j: lax.dynamic_index_in_dim(low_raw, j, 0, False))
     low_raw = stack(raw_pieces, "seq")
     packed = pack_inner(low_raw, w_down, group, min(512, width))
     packed = pieces_of(packed, "docs")
 
     near = jnp.concatenate([neighbours[0] // 64, neighbours[0] % 64], axis=1).astype(BF)
-    x_near = pieces_of(after(jnp.concatenate([tokens[0], near], axis=1), low_raw), "seq")
+    x_near = pieces_of(gate(jnp.concatenate([tokens[0], near], axis=1), *raw_pieces[1:]), "seq")
     flag = jnp.take(has_memory, doc_index[None])
-    grad_low = pieces_of(after(cotangent[0], x_near[2 if seq_count > 2 else -1]), "seq")
+    grad_low = pieces_of(gate(cotangent[0], x_near[2 if seq_count > 2 else -1]), "seq")
     low_merge = stack([piece[:, 3 * cols + LANES :] for piece in first], "docs")
     low_merge = low_merge.reshape(docs_count, seq_count, weight_rows, merge_cols)
     low_merge = low_merge.transpose(0, 2, 1, 3).reshape(docs_count, weight_rows, width)
@@ -958,7 +958,7 @@
     for k in range(2, bits):
         g_raw = halve(g_raw, "docs", k, last if k == 2 else 0.0)
     for k in range(1, bits):
-        late = last if k == 1 else 0.0
+        late = last if k == 1 else token(g_heads)
         g_down = halve(g_down, "docs", first_z[k][0], late, first_z[k][1])
     g_heads = reduce_over(g_heads, "docs", 2)
     g_down = g_down[0][:down_rows]

time: 444 us -> 441 us (level)
  starting transfers between devices: 109 us -> 75.4 us
  Pallas kernels: 90.3 us -> 120 us
  waiting for transfers between devices: 130 us -> 135 us
    ppermute x65, starting transfers between devices: 90.9 us -> 59 us  [send(): lax.ppermute(x, axis, [(i, i ^ bits) for i in range(lax.axis_size(axis))])]
    pallas_call x2, Pallas kernels: 6.99 us -> 21.9 us  [attend_memory(): pl.pallas_call(functools.partial(attend_memory_kernel, min(4096, keys)),...]
    pallas_call x2, Pallas kernels: 15.7 us -> 30.2 us  [attend_back(): pl.pallas_call(functools.partial(attend_back_kernel, min(512, keys), leng...]
    ppermute x65, waiting for transfers between devices: 115 us -> 126 us  [send(): lax.ppermute(x, axis, [(i, i ^ bits) for i in range(lax.axis_size(axis))])]
    all_to_all x2, waiting for transfers between devices: 8.39 us -> 0.89 us  [shards(): lax.all_to_all(gated[-1], ('docs', 'seq'), split_axis=0, concat_axis=0, t...]
    unnamed x147 -> x151, local copies, waits for them, and re-layouts: 8.29 us -> 9.91 us
  transfers between devices with their start and end apart: 69 -> 69, of which waited for: 24 -> 22; matrix products, arithmetic and copies ran while one was open for 19% -> 20% of each run, Pallas kernels for 15% -> 22%
where the time goes in v4:
time: 441 us; the launch traced here: 434 us
  waiting for transfers between devices  135 us (31%)
  Pallas kernels  120 us (27%)
  starting transfers between devices  75.4 us (17%)
  other arithmetic  43.6 us (10%)
  local copies, waits for them, and re-layouts  32.3 us (7%)
  matrix products  20.5 us (5%)
  between operations  7.63 us (2%)
    ppermute x65, waiting for transfers between devices, send(): lax.ppermute(x, axis, [(i, i ^ bits) for i in range(lax.axis_size(axis))])  126 us
    ppermute x65, starting transfers between devices, send(): lax.ppermute(x, axis, [(i, i ^ bits) for i in range(lax.axis_size(axis))])  59 us
    pallas_call x2, Pallas kernels, attend_back(): pl.pallas_call(functools.partial(attend_back_kernel, min(512, keys), leng...  30.2 us
    pallas_call x2, Pallas kernels, attend_memory(): pl.pallas_call(functools.partial(attend_memory_kernel, min(4096, keys)),...  21.9 us
    pallas_call x1, Pallas kernels, feed_forward(): pl.pallas_call(functools.partial(feed_forward_kernel, heads, seq, docs),...  21.6 us
    dot_general x5, matrix products, dot_tn(): lax.dot_general(a, b, (((0,), (0,)), ((), ())), preferred_element_type=F32)  16.1 us
    pallas_call x1, Pallas kernels, project(): pl.pallas_call(functools.partial(project_kernel, heads, len(tokens), len(...  13.5 us
    all_to_all x2, starting transfers between devices, shards(): lax.all_to_all(gated[-1], ('docs', 'seq'), split_axis=0, concat_axis=0, t...  11.3 us
  transfers between devices with their start and end apart: 69, of which 22 were waited for; matrix products, arithmetic and copies ran while one was open for 20% of the time, Pallas kernels for 22%

profile of v4, /device:TPU:0, one launch (start us, length us, event | category | flops | bytes accessed | tf_op | source)
XLA Modules:
  0.0 433.8 jit_solution(1988186025287313100)
XLA Ops:
  10.4 7.7 %pack_memory.1 = (bf16[8,4,2,64,256]{4,3,2,1,0:T(8,128)(2,1)}, bf16[8,4,2,64,256]{4,3,2,1,0:T(8,128)(2,1)}) custom-call(s32[8]{0:T(128)} %partner.1, bf16[8,64,1024]{2,1,0:T(8,128)(2,1)} %mate_key.1, bf16[8,64,1024]{2,1,0:T(8,128)(2,1)} %mate_value.1, bf16[8,64,1024]{2,1,0:T(8,128)(2,1)} %mate_key.1, bf16[8,64,1024]{2,1,0:T(8,128)(2,1)} %mate_value.1), custom_call_target="tpu_custom_call" | custom-call | flops 1 | bytes 1 | tf_op jit(solution)/shard_map/pack_memory/pallas_call | solution.py:153
  25.1 4.6 %all-to-all-start = ((bf16[32,2,64,256]{3,2,1,0:T(8,128)(2,1)}), bf16[32,2,64,256]{3,2,1,0:T(8,128)(2,1)S(1)}, u32[]{:S(2)}, u32[]{:S(2)}) async-start(bf16[32,2,64,256]{3,2,1,0:T(8,128)(2,1)} %gate.6), calls=%async_computation | async-start | bytes 4194304 | tf_op jit(solution)/shard_map/all_to_all | solution.py:878
  31.6 5.9 %collective-permute-done.12.refs_5_.refs_8_ = bf16[128,1152]{1,0:T(8,128)(2,1)} collective-permute-done((bf16[128,1152]{1,0:T(8,128)(2,1)}, bf16[128,1152]{1,0:T(8,128)(2,1)}, u32[]{:S(2)}, u32[]{:S(2)}) %collective-permute-start.12) | collective-permute-done | bytes 294944 | tf_op jit(solution)/shard_map/ppermute | solution.py:29
  46.5 30.4 %collective-permute-done.14.refs_7_.refs_10_ = bf16[128,1152]{1,0:T(8,128)(2,1)} collective-permute-done((bf16[128,1152]{1,0:T(8,128)(2,1)}, bf16[128,1152]{1,0:T(8,128)(2,1)}, u32[]{:S(2)}, u32[]{:S(2)}) %collective-permute-start.14) | collective-permute-done | bytes 294944 | tf_op jit(solution)/shard_map/ppermute | solution.py:29
  87.2 20.3 %collective-permute-done.19.refs_12_ = bf16[576,512]{1,0:T(8,128)(2,1)} collective-permute-done((bf16[576,512]{1,0:T(8,128)(2,1)}, bf16[576,512]{1,0:T(8,128)(2,1)}, u32[]{:S(2)}, u32[]{:S(2)}) %collective-permute-start.19) | collective-permute-done | bytes 589856 | tf_op jit(solution)/shard_map/ppermute | solution.py:29
  124.1 8.6 %collective-permute-done.26.refs_20_ = bf16[8,32,1024]{2,1,0:T(8,128)(2,1)S(1)} collective-permute-done((bf16[8,32,1024]{2,1,0:T(8,128)(2,1)S(1)}, bf16[8,32,1024]{2,1,0:T(8,128)(2,1)S(1)}, u32[]{:S(2)}, u32[]{:S(2)}) %collective-permute-start.26) | collective-permute-done | bytes 524320 | tf_op jit(solution)/shard_map/ppermute | solution.py:29
  138.8 6.7 %all-to-all-start.1 = ((bf16[32,2,64,256]{3,2,1,0:T(8,128)(2,1)}), bf16[32,2,64,256]{3,2,1,0:T(8,128)(2,1)S(1)}, u32[]{:S(2)}, u32[]{:S(2)}) async-start(bf16[32,2,64,256]{3,2,1,0:T(8,128)(2,1)} %gate.8.refs_14_), calls=%async_computation.1 | async-start | bytes 4194304 | tf_op jit(solution)/shard_map/all_to_all | solution.py:878
  154.7 4.1 lay_out.1.refs_0_.refs_19_
  161.9 13.5 %project.1 = (bf16[1024,1024]{1,0:T(8,128)(2,1)}, bf16[1024,1024]{1,0:T(8,128)(2,1)}, bf16[1024,256]{1,0:T(8,128)(2,1)}, bf16[1024,256]{1,0:T(8,128)(2,1)}, bf16...) custom-call(s32[2]{0:T(128)} %pad_add_fusion.here, ...), custom_call_target="tpu_custom_call" | custom-call | flops 1 | bytes 1 | tf_op jit(solution)/shard_map/project/pallas_call | solution.py:303
  175.4 5.7 %attend_local.1 = (f32[1024,256]{1,0:T(8,128)}, f32[1024,256]{1,0:T(8,128)}, f32[1024,256]{1,0:T(8,128)}) custom-call(bf16[1024,256]{1,0:T(8,128)(2,1)} %get-tuple-element.85.ql, bf16[1024,256]{1,0:T(8,128)(2,1)} %get-tuple-element.86.kl, bf16[1024,256]{1,0:T(8,128)(2,1)} %get-tuple-element.87.vl), custom_call_target="tpu_custom_call" | custom-call | flops 1 | bytes 1 | tf_op jit(solution)/shard_map/attend_local/pallas_call | solution.py:466
  181.1 10.9 %attend_memory.2 = (f32[1024,128]{1,0:T(8,128)}, bf16[1024,128]{1,0:T(8,128)(2,1)}, f32[1024,128]{1,0:T(8,128)}) custom-call(s32[1]{0:T(128)S(6)} %select_n.913.flag, bf16[1024,256]{1,0:T(8,128)(2,1)} %get-tuple-element.83.qm, s32[1024,128]{1,0:T(8,128)} %get-tuple-element.84.words, bf16[4096,256]{1,0:T(8,128)(2,1)} %bitcast.289, ...), custom_call_target="tpu_custom_call" | custom-call | flops 1 | bytes 1 | tf_op jit(solution)/shard_map/attend_memory/pallas_call | solution.py:522
  195.6 10.9 %attend_memory.3 = (f32[1024,128]{1,0:T(8,128)}, bf16[1024,128]{1,0:T(8,128)(2,1)}, f32[1024,128]{1,0:T(8,128)}) custom-call(s32[1]{0:T(128)S(6)} %select_n.913.flag, bf16[1024,256]{1,0:T(8,128)(2,1)} %get-tuple-element.83.qm, s32[1024,128]{1,0:T(8,128)} %get-tuple-element.84.words, bf16[4096,256]{1,0:T(8,128)(2,1)} %bitcast.298, ...), custom_call_target="tpu_custom_call" | custom-call | flops 1 | bytes 1 | tf_op jit(solution)/shard_map/attend_memory/pallas_call | solution.py:522
  208.6 6.0 %collective-permute-done.31.refs_5_ = bf16[1024,128]{1,0:T(8,128)(2,1)S(1)} collective-permute-done((bf16[1024,128]{1,0:T(8,128)(2,1)}, bf16[1024,128]{1,0:T(8,128)(2,1)S(1)}, u32[]{:S(2)}, u32[]{:S(2)}) %collective-permute-start.31) | collective-permute-done | bytes 262176 | tf_op jit(solution)/shard_map/ppermute | solution.py:29
  216.9 21.6 %feed_forward.1 = (bf16[1024,1024]{1,0:T(8,128)(2,1)}, bf16[1024,1024]{1,0:T(8,128)(2,1)}, bf16[1024,768]{1,0:T(8,128)(2,1)}, bf16[1024,1536]{1,0:T(8,128)(2,1)}...) custom-call(s32[2]{0:T(128)} %pad_add_fusion.here, ...), custom_call_target="tpu_custom_call" | custom-call | flops 1 | bytes 1 | tf_op jit(solution)/shard_map/feed_forward/pallas_call | solution.py:380
  240.4 5.6 %convolution_convert_fusion = bf16[1024,1536]{1,0:T(8,128)(2,1)S(1)} fusion(bf16[1024,1024]{1,0:T(8,128)(2,1)S(1)} %copy-done.66, bf16[1024,1536]{1,0:T(8,128)(2,1)} %get-tuple-element.102), kind=kOutput, calls=%fused_computation.3 | convolution fusion | flops 3222798336 | bytes 8388608 | tf_op jit(solution)/shard_map/dot_general | solution.py:99
  257.5 6.7 %collective-permute-done.38 = bf16[1,1,256,1024]{3,2,1,0:T(8,128)(2,1)S(1)} collective-permute-done((bf16[1,1,256,1024]{3,2,1,0:T(8,128)(2,1)S(1)}, bf16[1,1,256,1024]{3,2,1,0:T(8,128)(2,1)S(1)}, u32[]{:S(2)}, u32[]{:S(2)}) %collective-permute-start.38) | collective-permute-done | bytes 524320 | tf_op jit(solution)/shard_map/ppermute | solution.py:29
  279.4 4.7 %collective-permute-done.42 = bf16[4,1,128,1536]{3,2,0,1:T(8,128)(2,1)} collective-permute-done((bf16[4,1,128,1536]{3,2,0,1:T(8,128)(2,1)}, bf16[4,1,128,1536]{3,2,0,1:T(8,128)(2,1)}, u32[]{:S(2)}, u32[]{:S(2)}) %collective-permute-start.42) | collective-permute-done | bytes 1572896 | tf_op jit(solution)/shard_map/ppermute | solution.py:29
  289.9 15.2 %attend_back.2 = bf16[1024,384]{1,0:T(8,128)(2,1)} custom-call(s32[1]{0:T(128)S(6)} %select_n.913.flag, bf16[1024,256]{1,0:T(8,128)(2,1)} %get-tuple-element.85.ql, bf16[1024,256]{1,0:T(8,128)(2,1)} %get-tuple-element.83.qm, bf16[1024,256]{1,0:T(8,128)(2,1)} %get-tuple-element.86.kl, bf16[1024,256]{1,0:T(8,128)(2,1)} %get-tuple-element.87.vl, ...), custom_call_target="tpu_custom_call" | custom-call | flops 16000000000 | bytes 2097152 | tf_op jit(solution)/shard_map/attend_back/pallas_call | solution.py:611
  327.3 15.1 %attend_back.3 = bf16[1024,384]{1,0:T(8,128)(2,1)} custom-call(s32[1]{0:T(128)S(6)} %select_n.913.flag, bf16[1024,256]{1,0:T(8,128)(2,1)} %get-tuple-element.85.ql, bf16[1024,256]{1,0:T(8,128)(2,1)} %get-tuple-element.83.qm, bf16[1024,256]{1,0:T(8,128)(2,1)} %get-tuple-element.86.kl, bf16[1024,256]{1,0:T(8,128)(2,1)} %get-tuple-element.87.vl, ...), custom_call_target="tpu_custom_call" | custom-call | flops 16000000000 | bytes 2097152 | tf_op jit(solution)/shard_map/attend_back/pallas_call | solution.py:611
  352.8 6.0 %collective-permute-done.50 = bf16[4,1,128,384]{3,2,0,1:T(8,128)(2,1)S(1)} collective-permute-done((bf16[4,1,128,384]{3,2,0,1:T(8,128)(2,1)S(1)}, bf16[4,1,128,384]{3,2,0,1:T(8,128)(2,1)S(1)}, u32[]{:S(2)}, u32[]{:S(2)}) %collective-permute-start.50) | collective-permute-done | bytes 393248 | tf_op jit(solution)/shard_map/ppermute | solution.py:29
  362.2 5.7 %collective-permute-done.57 = bf16[4,1,32,1024]{3,2,0,1:T(8,128)(2,1)S(1)} collective-permute-done((bf16[4,1,32,1024]{3,2,0,1:T(8,128)(2,1)S(1)}, bf16[4,1,32,1024]{3,2,0,1:T(8,128)(2,1)S(1)}, u32[]{:S(2)}, u32[]{:S(2)}) %collective-permute-start.57) | collective-permute-done | bytes 262176 | tf_op jit(solution)/shard_map/ppermute | solution.py:29
  376.9 9.2 %collective-permute-done.53 = bf16[1,1,128,768]{3,2,0,1:T(8,128)(2,1)S(1)} collective-permute-done((bf16[1,1,128,768]{3,2,0,1:T(8,128)(2,1)S(1)}, bf16[1,1,128,768]{3,2,0,1:T(8,128)(2,1)S(1)}, u32[]{:S(2)}, u32[]{:S(2)}) %collective-permute-start.53) | collective-permute-done | bytes 196640 | tf_op jit(solution)/shard_map/ppermute | solution.py:29
  404.2 7.3 %all-to-all-done.2.refs_0_ = f32[32,1,128]{2,1,0:T(1,128)S(1)} async-done(((f32[32,1,128]{2,1,0:T(1,128)}), f32[32,1,128]{2,1,0:T(1,128)S(1)}, u32[]{:S(2)}, u32[]{:S(2)}) %all-to-all-start.2) | async-done | bytes 16416 | tf_op jit(solution)/shard_map/all_to_all | solution.py:87
  412.1 6.6 %moments.1 = (f32[32,3072]{1,0:T(8,128)}, f32[32,1024]{1,0:T(8,128)}, f32[32,2816]{1,0:T(8,128)}, f32[32,2816]{1,0:T(8,128)}, f32[88,1024]{1,0:T(8,128)}, /*inde...) custom-call(f32[32,1,128]{2,1,0:T(1,128)} %copy-done.60, ...), custom_call_target="tpu_custom_call" | custom-call | flops 1 | bytes 1 | tf_op jit(solution)/shard_map/moments/pallas_call | solution.py:750
  (401 shorter events, 187.2 us)
Async XLA Ops:
  25.1 112.4 %all-to-all-start = ((bf16[32,2,64,256]{3,2,1,0:T(8,128)(2,1)}), bf16[32,2,64,256]{3,2,1,0:T(8,128)(2,1)S(1)}, u32[]{:S(2)}, u32[]{:S(2)}) async-start(bf16[32,2,64,256]{3,2,1,0:T(8,128)(2,1)} %gate.6), calls=%async_computation | async-start | bytes 4194304 | tf_op jit(solution)/shard_map/all_to_all | solution.py:878
  29.7 48.7 %collective-permute-start.4 = (bf16[256,1152]{1,0:T(8,128)(2,1)}, bf16[256,1152]{1,0:T(8,128)(2,1)S(1)}, u32[]{:S(2)}, u32[]{:S(2)}) collective-permute-start(bf16[256,1152]{1,0:T(8,128)(2,1)} %gate.5.refs_0_), channel_id=1, source_target_pairs={{0,2},{1,3},{2,0},{3,1},{4,6},{5,7},{6,4},{7,5},{8,10},{9,11},{10,... | collective-permute-start | bytes 1769480 | tf_op jit(solution)/shard_map/ppermute | solution.py:29
  37.5 39.5 %collective-permute-start.14 = (bf16[128,1152]{1,0:T(8,128)(2,1)}, bf16[128,1152]{1,0:T(8,128)(2,1)}, u32[]{:S(2)}, u32[]{:S(2)}) collective-permute-start(bf16[128,1152]{1,0:T(8,128)(2,1)} %collective-permute-done.12.refs_5_.refs_8_), channel_id=1, source_target_pairs={{0,8},{4,12},{8,0},{12,4},{16,24},{20,28},{24,16},{28,20},{1,9},{5... | collective-permute-start | bytes 884744 | tf_op jit(solution)/shard_map/ppermute | solution.py:29
  40.9 66.6 %collective-permute-start.19 = (bf16[576,512]{1,0:T(8,128)(2,1)}, bf16[576,512]{1,0:T(8,128)(2,1)}, u32[]{:S(2)}, u32[]{:S(2)}) collective-permute-start(bf16[576,512]{1,0:T(8,128)(2,1)} %pack_inner.1.refs_8_), channel_id=1, source_target_pairs={{0,16},{4,20},{8,24},{12,28},{16,0},{20,4},{24,8},{28,12},{1,17},{... | collective-permute-start | bytes 1769480 | tf_op jit(solution)/shard_map/ppermute | solution.py:29
  44.5 36.4 %collective-permute-start.9 = (bf16[128,1152]{1,0:T(8,128)(2,1)}, bf16[128,1152]{1,0:T(8,128)(2,1)}, u32[]{:S(2)}, u32[]{:S(2)}) collective-permute-start(bf16[128,1152]{1,0:T(8,128)(2,1)} %pad_maximum_fusion.6.refs_4_), channel_id=1, source_target_pairs={{0,4},{4,0},{8,12},{12,8},{16,20},{20,16},{24,28},{28,24},{1,5},{5... | collective-permute-start | bytes 884744 | tf_op jit(solution)/shard_map/ppermute | solution.py:29
  46.0 37.3 %collective-permute-start.11 = (bf16[128,1152]{1,0:T(8,128)(2,1)}, bf16[128,1152]{1,0:T(8,128)(2,1)}, u32[]{:S(2)}, u32[]{:S(2)}) collective-permute-start(bf16[128,1152]{1,0:T(8,128)(2,1)} %collective-permute-done.10.refs_3_.refs_6_), channel_id=1, source_target_pairs={{0,4},{4,0},{8,12},{12,8},{16,20},{20,16},{24,28},{28,24},{1,5},{5... | collective-permute-start | bytes 884744 | tf_op jit(solution)/shard_map/ppermute | solution.py:29
  80.9 37.9 %collective-permute-start.17 = (bf16[576,512]{1,0:T(8,128)(2,1)}, bf16[576,512]{1,0:T(8,128)(2,1)S(1)}, u32[]{:S(2)}, u32[]{:S(2)}) collective-permute-start(bf16[576,512]{1,0:T(8,128)(2,1)} %pack_inner.1.refs_8_), channel_id=1, source_target_pairs={{0,8},{4,12},{8,0},{12,4},{16,24},{20,28},{24,16},{28,20},{1,9},{5... | collective-permute-start | bytes 1769480 | tf_op jit(solution)/shard_map/ppermute | solution.py:29
  83.4 36.2 %collective-permute-start.16 = (bf16[576,512]{1,0:T(8,128)(2,1)}, bf16[576,512]{1,0:T(8,128)(2,1)S(1)}, u32[]{:S(2)}, u32[]{:S(2)}) collective-permute-start(bf16[576,512]{1,0:T(8,128)(2,1)} %pack_inner.1.refs_8_), channel_id=1, source_target_pairs={{0,4},{4,0},{8,12},{12,8},{16,20},{20,16},{24,28},{28,24},{1,5},{5... | collective-permute-start | bytes 1769480 | tf_op jit(solution)/shard_map/ppermute | solution.py:29
  87.2 32.4 %collective-permute-start.3 = (bf16[256,1152]{1,0:T(8,128)(2,1)S(1)}, bf16[256,1152]{1,0:T(8,128)(2,1)S(1)}, u32[]{:S(2)}, u32[]{:S(2)}) collective-permute-start(bf16[256,1152]{1,0:T(8,128)(2,1)S(1)} %copy-done.15), channel_id=1, source_target_pairs={{0,1},{1,0},{2,3},{3,2},{4,5},{5,4},{6,7},{7,6},{8,9},{9,8},{10,11... | collective-permute-start | bytes 1769480 | tf_op jit(solution)/shard_map/ppermute | solution.py:29
  138.8 55.5 %all-to-all-start.1 = ((bf16[32,2,64,256]{3,2,1,0:T(8,128)(2,1)}), bf16[32,2,64,256]{3,2,1,0:T(8,128)(2,1)S(1)}, u32[]{:S(2)}, u32[]{:S(2)}) async-start(bf16[32,2,64,256]{3,2,1,0:T(8,128)(2,1)} %gate.8.refs_14_), calls=%async_computation.1 | async-start | bytes 4194304 | tf_op jit(solution)/shard_map/all_to_all | solution.py:878
  150.7 57.3 %collective-permute-start.34 = (bf16[576,512]{1,0:T(8,128)(2,1)S(1)}, bf16[576,512]{1,0:T(8,128)(2,1)}, u32[]{:S(2)}, u32[]{:S(2)}) collective-permute-start(bf16[576,512]{1,0:T(8,128)(2,1)S(1)} %copy-done.23), channel_id=1, source_target_pairs={{0,4},{4,0},{8,12},{12,8},{16,20},{20,16},{24,28},{28,24},{1,5},{5... | collective-permute-start | bytes 1769480 | tf_op jit(solution)/shard_map/ppermute | solution.py:29
  152.6 55.9 %collective-permute-start.35 = (bf16[576,512]{1,0:T(8,128)(2,1)}, bf16[576,512]{1,0:T(8,128)(2,1)}, u32[]{:S(2)}, u32[]{:S(2)}) collective-permute-start(bf16[576,512]{1,0:T(8,128)(2,1)} %collective-permute-done.19.refs_12_), channel_id=1, source_target_pairs={{0,4},{4,0},{8,12},{12,8},{16,20},{20,16},{24,28},{28,24},{1,5},{5... | collective-permute-start | bytes 1769480 | tf_op jit(solution)/shard_map/ppermute | solution.py:29
  152.8 62.7 %collective-permute-start.36 = (bf16[576,512]{1,0:T(8,128)(2,1)S(1)}, bf16[576,512]{1,0:T(8,128)(2,1)}, u32[]{:S(2)}, u32[]{:S(2)}) collective-permute-start(bf16[576,512]{1,0:T(8,128)(2,1)S(1)} %copy-done.50), channel_id=1, source_target_pairs={{0,4},{4,0},{8,12},{12,8},{16,20},{20,16},{24,28},{28,24},{1,5},{5... | collective-permute-start | bytes 1769480 | tf_op jit(solution)/shard_map/ppermute | solution.py:29
  247.4 36.8 %collective-permute-start.42 = (bf16[4,1,128,1536]{3,2,0,1:T(8,128)(2,1)}, bf16[4,1,128,1536]{3,2,0,1:T(8,128)(2,1)}, u32[]{:S(2)}, u32[]{:S(2)}) collective-permute-start(bf16[4,1,128,1536]{3,2,0,1:T(8,128)(2,1)} %dynamic-slice_bitcast_fusion), channel_id=1, source_target_pairs={{0,4},{4,0},{8,12},{12,8},{16,20},{20,16},{24,28},{28,24},{1,5},{5... | collective-permute-start | bytes 4718600 | tf_op jit(solution)/shard_map/ppermute | solution.py:29
  255.7 31.0 %collective-permute-start.43 = (bf16[2,2,96,1024]{3,2,1,0:T(8,128)(2,1)}, bf16[2,2,96,1024]{3,2,1,0:T(8,128)(2,1)}, u32[]{:S(2)}, u32[]{:S(2)}) collective-permute-start(bf16[2,2,96,1024]{3,2,1,0:T(8,128)(2,1)} %dynamic-slice_bitcast_fusion.4), channel_id=1, source_target_pairs={{0,8},{4,12},{8,0},{12,4},{16,24},{20,28},{24,16},{28,20},{1,9},{5... | collective-permute-start | bytes 2359304 | tf_op jit(solution)/shard_map/ppermute | solution.py:29
  277.0 34.9 %collective-permute-start.44 = (bf16[2,1,256,1024]{3,2,1,0:T(8,128)(2,1)}, bf16[2,1,256,1024]{3,2,1,0:T(8,128)(2,1)}, u32[]{:S(2)}, u32[]{:S(2)}) collective-permute-start(bf16[2,1,256,1024]{3,2,1,0:T(8,128)(2,1)} %dynamic-slice_bitcast_fusion.2), channel_id=1, source_target_pairs={{0,1},{1,0},{2,3},{3,2},{4,5},{5,4},{6,7},{7,6},{8,9},{9,8},{10,11... | collective-permute-start | bytes 3145736 | tf_op jit(solution)/shard_map/ppermute | solution.py:29
  277.2 38.8 %collective-permute-start.46 = (bf16[256,1024]{1,0:T(8,128)(2,1)}, bf16[256,1024]{1,0:T(8,128)(2,1)}, u32[]{:S(2)}, u32[]{:S(2)}) collective-permute-start(bf16[256,1024]{1,0:T(8,128)(2,1)} %gate.9), channel_id=1, source_target_pairs={{0,2},{1,3},{2,0},{3,1},{4,6},{5,7},{6,4},{7,5},{8,10},{9,11},{10,... | collective-permute-start | bytes 1572872 | tf_op jit(solution)/shard_map/ppermute | solution.py:29
  278.3 41.4 %collective-permute-start.48 = (bf16[256,1024]{1,0:T(8,128)(2,1)}, bf16[256,1024]{1,0:T(8,128)(2,1)}, u32[]{:S(2)}, u32[]{:S(2)}) collective-permute-start(bf16[256,1024]{1,0:T(8,128)(2,1)} %gate.9), channel_id=1, source_target_pairs={{0,1},{1,0},{2,3},{3,2},{4,5},{5,4},{6,7},{7,6},{8,9},{9,8},{10,11... | collective-permute-start | bytes 1572872 | tf_op jit(solution)/shard_map/ppermute | solution.py:29
  286.6 30.9 %collective-permute-start.45 = (bf16[2,1,128,1536]{3,2,0,1:T(8,128)(2,1)S(1)}, bf16[2,1,128,1536]{3,2,0,1:T(8,128)(2,1)}, u32[]{:S(2)}, u32[]{:S(2)}) collective-permute-start(bf16[2,1,128,1536]{3,2,0,1:T(8,128)(2,1)S(1)} %fusion.24), channel_id=1, source_target_pairs={{0,8},{4,12},{8,0},{12,4},{16,24},{20,28},{24,16},{28,20},{1,9},{5... | collective-permute-start | bytes 2359304 | tf_op jit(solution)/shard_map/ppermute | solution.py:29
  307.7 40.3 %collective-permute-start.60 = (bf16[1,2,96,1024]{3,2,1,0:T(8,128)(2,1)}, bf16[1,2,96,1024]{3,2,1,0:T(8,128)(2,1)S(1)}, u32[]{:S(2)}, u32[]{:S(2)}) collective-permute-start(bf16[1,2,96,1024]{3,2,1,0:T(8,128)(2,1)} %dynamic-slice_convert_fusion.4), channel_id=1, source_target_pairs={{0,16},{4,20},{8,24},{12,28},{16,0},{20,4},{24,8},{28,12},{1,17},{... | collective-permute-start | bytes 1179656 | tf_op jit(solution)/shard_map/ppermute | solution.py:29
  311.8 38.0 %collective-permute-start.51 = (bf16[4,1,128,384]{3,2,0,1:T(8,128)(2,1)}, bf16[4,1,128,384]{3,2,0,1:T(8,128)(2,1)}, u32[]{:S(2)}, u32[]{:S(2)}) collective-permute-start(bf16[4,1,128,384]{3,2,0,1:T(8,128)(2,1)} %dynamic-slice_bitcast_fusion.5), channel_id=1, source_target_pairs={{0,4},{4,0},{8,12},{12,8},{16,20},{20,16},{24,28},{28,24},{1,5},{5... | collective-permute-start | bytes 1179656 | tf_op jit(solution)/shard_map/ppermute | solution.py:29
  316.0 107.2 %collective-permute-start.62 = (bf16[1,1,256,1024]{3,2,1,0:T(8,128)(2,1)}, bf16[1,1,256,1024]{3,2,1,0:T(8,128)(2,1)}, u32[]{:S(2)}, u32[]{:S(2)}) collective-permute-start(bf16[1,1,256,1024]{3,2,1,0:T(8,128)(2,1)} %dynamic-slice_convert_fusion.2), channel_id=1, source_target_pairs={{0,2},{1,3},{2,0},{3,1},{4,6},{5,7},{6,4},{7,5},{8,10},{9,11},{10,... | collective-permute-start | bytes 1572872 | tf_op jit(solution)/shard_map/ppermute | solution.py:29
  319.7 31.9 %collective-permute-start.49 = (bf16[1,1,128,1536]{3,2,0,1:T(8,128)(2,1)}, bf16[1,1,128,1536]{3,2,0,1:T(8,128)(2,1)}, u32[]{:S(2)}, u32[]{:S(2)}) collective-permute-start(bf16[1,1,128,1536]{3,2,0,1:T(8,128)(2,1)} %dynamic-slice_convert_fusion.5), channel_id=1, source_target_pairs={{0,16},{4,20},{8,24},{12,28},{16,0},{20,4},{24,8},{28,12},{1,17},{... | collective-permute-start | bytes 1179656 | tf_op jit(solution)/shard_map/ppermute | solution.py:29
  362.1 33.5 %collective-permute-start.63 = (bf16[2,1,256,1024]{3,2,1,0:T(8,128)(2,1)S(1)}, bf16[2,1,256,1024]{3,2,1,0:T(8,128)(2,1)S(1)}, u32[]{:S(2)}, u32[]{:S(2)}) collective-permute-start(bf16[2,1,256,1024]{3,2,1,0:T(8,128)(2,1)S(1)} %dynamic-slice_bitcast_fusion.1), channel_id=1, source_target_pairs={{0,1},{1,0},{2,3},{3,2},{4,5},{5,4},{6,7},{7,6},{8,9},{9,8},{10,11... | collective-permute-start | bytes 3145736 | tf_op jit(solution)/shard_map/ppermute | solution.py:29
  (118 other events, 980.7 us)
